TPU v7x, 32 devices: a whole 2x2x4 slice. The times are simulated.
32 devices in a mesh: groups: 2 (over y), wide: 8 (over z, x), narrow: 2 (over core).
Axes of the slice: x: 2, y: 2, z: 4, core: 2. Of those that a mesh axis runs over, the one named last changes fastest.
Arguments:
- new_tokens: bfloat16 [4096, 8192], P(('groups', 'wide')), parts along dimension 0, may hold values from -6 to 6
- kv_weight: bfloat16 [8192, 1024], P('wide', 'narrow'), may hold values from -0.0625 to 0.0625
- prefix_cache: bfloat16 [2, 2048, 1024], P(None, ('groups', 'wide'), 'narrow'), parts along dimension 1, may hold values from -6 to 6
- queries: bfloat16 [16, 4096], P(('groups', 'wide'), 'narrow'), parts along dimension 0, may hold values from -64 to 64
- doc_of_question: int32 [16], P('groups'), parts along dimension 0, may hold values from 0 to 1
- span_lists: int32 [16, 8], P('groups'), parts along dimension 0, may hold values from 0 to 3
- span_slot: int32 [8], P('groups'), parts along dimension 0, may hold values from 0 to 3, each once
Outputs:
- new_cache: bfloat16 [4096, 1024], P(('groups', 'wide'), 'narrow'), parts along dimension 0
- attended: bfloat16 [16, 4096], P(('groups', 'wide'), 'narrow'), parts along dimension 0
There are 2 independent parts, one for each index of `groups`. A program takes and returns all parts, laid end to end along the dimension named above; an argument that names none is the same for every part. Nothing has to cross between parts.
Inputs may be any that keep to these rules, and one draw needn't show every extreme that they name: `span_lists`: A list may name a span more than once; each named span is attended once.
All inputs are finite; a program needn't handle non-finite values.
Results may differ from a plain program's by a relative error of at most 0.0085.
Values may be sent and summed in bfloat16 or wider, within the bound.
No kernel may reach another device: no remote copies, remote signals or barrier semaphores. Data moves between devices by JAX's collectives and lax.ppermute only.
A program may use at most 64 MiB of HBM per device.

v0:
```python
import jax
import jax.numpy as jnp
from jax import lax
from jax.sharding import PartitionSpec as P

HD = 128
GROUP = 8
CLEN = 512
DOCS = 2


def combined_all(part, axis, combine):
    gathered = jax.tree.map(lambda a: lax.all_gather(a, axis), part)

    def take(source):
        return jax.tree.map(lambda a: lax.dynamic_index_in_dim(a, source, 0, False), gathered)

    return lax.fori_loop(
        1, lax.axis_size(axis), lambda source, state: combine(state, take(source)), take(0)
    )


def combine_pair(first, second):
    top = jnp.maximum(first[0], second[0])
    return (top, first[1] * jnp.exp(first[0] - top) + second[1] * jnp.exp(second[0] - top))


def shards(new_tokens, kv_weight, prefix_cache, queries, doc_of_question, span_lists, span_slot):
    tok_rows = new_tokens.shape[0]
    columns = kv_weight.shape[1]
    projected = jnp.dot(
        new_tokens,
        lax.all_gather(kv_weight, "wide", axis=0, tiled=True),
        preferred_element_type=jnp.float32,
    )
    new_cache = projected.astype(jnp.bfloat16)
    gathered = lax.all_gather(queries, "wide", axis=0, tiled=True)
    head_size = HD
    heads_here = columns // (2 * head_size)
    n_quest = gathered.shape[0]
    asked = gathered.reshape(n_quest, heads_here, GROUP, head_size)
    pref_rows = prefix_cache.shape[1]
    stacked = jnp.concatenate(
        [
            prefix_cache.reshape(DOCS * pref_rows, heads_here, 2, head_size),
            new_cache.reshape(tok_rows, heads_here, 2, head_size),
        ],
        0,
    )
    keys_all = stacked[:, :, 0]
    values_all = stacked[:, :, 1]
    key_doc = jnp.concatenate(
        [
            jnp.arange(DOCS * pref_rows, dtype=jnp.int32) // pref_rows,
            jnp.full((tok_rows,), -1, jnp.int32),
        ]
    )
    row_ids = lax.axis_index("wide") * tok_rows + jnp.arange(tok_rows, dtype=jnp.int32)
    key_slot = jnp.concatenate([jnp.full((DOCS * pref_rows,), -1, jnp.int32), row_ids // CLEN])
    wanted = span_slot[span_lists]
    visible = (doc_of_question[:, None] == key_doc[None, :]) | jnp.any(
        wanted[:, :, None] == key_slot[None, None, :], axis=1
    )
    scores = jnp.einsum("qgjd,kgd->qgjk", asked, keys_all, preferred_element_type=jnp.float32) * (
        1.0 / head_size**0.5
    )
    scores = jnp.where(visible[:, None, None, :], scores, -jnp.inf)
    peak = jnp.max(scores, axis=-1)
    weights = jnp.exp(scores - peak[..., None])
    total = jnp.sum(weights, axis=-1)
    mixed = jnp.einsum(
        "qgjk,kgd->qgjd",
        weights.astype(jnp.bfloat16),
        values_all,
        preferred_element_type=jnp.float32,
    )
    own_rows = queries.shape[0]
    top_peak, top_total = combined_all((peak, total), "wide", combine_pair)
    mixed = mixed * jnp.exp(peak - top_peak)[..., None]
    mixed = lax.psum_scatter(mixed, "wide", scatter_dimension=0, tiled=True)
    start = lax.axis_index("wide") * own_rows
    total = lax.dynamic_slice_in_dim(top_total, start, own_rows, 0)
    attended = (
        (mixed / total[..., None])
        .reshape(own_rows, heads_here * GROUP * head_size)
        .astype(jnp.bfloat16)
    )
    return (new_cache, attended)


def solution(mesh):
    placed = (
        P(("groups", "wide"), None),
        P("wide", "narrow"),
        P(None, ("groups", "wide"), "narrow"),
        P(("groups", "wide"), "narrow"),
        P("groups"),
        P("groups", None),
        P("groups"),
    )
    return jax.shard_map(
        shards,
        mesh=mesh,
        in_specs=placed,
        out_specs=(P(("groups", "wide"), "narrow"), P(("groups", "wide"), "narrow")),
        check_vma=False,
    )
```

profile of v0, /device:TPU:0, one launch (start us, length us, event | category | flops | bytes accessed | tf_op | source)
XLA Modules:
  0.0 283.8 jit_solution(3416020012122537280)
XLA Ops:
  7.2 0.7 all-gather.5.cloned.1.call-update
  8.0 1.0 reshape.60
  9.0 0.7 compare_select_fusion
  9.7 0.1 reshape.65
  9.8 0.8 gather_fusion
  10.6 0.1 reshape.64
  10.7 33.0 %all-gather.2 = bf16[8,1,2048]{2,1,0:T(2,128)(2,1)S(1)} all-gather(bf16[1,1,2048]{2,1,0:T(2,128)(2,1)} %bitcast.62), channel_id=1, replica_groups=mesh['groups'=2,'wide'=8,'narrow'=2] {'wide'}, dimensions={0}, use_global_device_ids=true | all-gather | bytes 36864 | tf_op jit(solution)/shard_map/all_gather | solution.py:37
  43.7 0.2 reduce
  43.9 1.2 dynamic-slice
  45.1 0.1 compare_reduce_fusion
  45.3 0.7 compare_or_fusion
  46.0 92.4 %all-gather.5.cloned.1.call-done = bf16[8192,512]{1,0:T(8,128)(2,1)} async-done(((bf16[1024,512]{1,0:T(8,128)(2,1)}), bf16[8192,512]{1,0:T(8,128)(2,1)}) %all-gather.5.cloned.1.call-update) | async-done | bytes 8388624 | tf_op jit(solution)/shard_map/all_gather | solution.py:33
  138.4 7.0 %convolution_convert_fusion = bf16[256,512]{1,0:T(8,128)(2,1)S(1)} fusion(bf16[256,8192]{1,0:T(8,128)(2,1)} %param.9, bf16[8192,512]{1,0:T(8,128)(2,1)} %all-gather.5.cloned.1.call-done), kind=kOutput, calls=%fused_computation.6 | convolution fusion | flops 2147614720 | bytes 12845056 | tf_op jit(solution)/shard_map/dot_general | solution.py:31
  145.4 0.1 reshape.61
  145.5 0.1 copy_dynamic-update-slice_fusion
  145.6 0.3 fusion.11
  145.9 30.5 %all-gather = f32[64,2,8]{2,0,1:T(8,128)S(1)} all-gather(f32[8,2,8]{2,0,1:T(8,128)S(1)} %get-tuple-element.169), channel_id=2, replica_groups=mesh['groups'=2,'wide'=8,'narrow'=2] {'wide'}, dimensions={0}, use_global_device_ids=true | all-gather | bytes 4608 | tf_op jit(solution)/shard_map/all_gather | solution.py:13
  176.4 0.2 fusion.5
  176.6 30.5 %all-gather.1 = f32[64,2,8]{2,0,1:T(8,128)S(1)} all-gather(f32[8,2,8]{2,0,1:T(8,128)S(1)} %fusion.5), channel_id=3, replica_groups=mesh['groups'=2,'wide'=8,'narrow'=2] {'wide'}, dimensions={0}, use_global_device_ids=true | all-gather | bytes 4608 | tf_op jit(solution)/shard_map/all_gather | solution.py:13
  207.1 0.3 while.17
  207.4 0.9 fusion.4
  208.3 66.7 %all-reduce.5.cloned.1.call-done = f32[8,2,8,128]{3,2,0,1:T(8,128)} async-done(((f32[8,2,8,128]{3,2,0,1:T(8,128)}), f32[8,2,8,128]{3,2,0,1:T(8,128)}) %all-reduce.5.cloned.1.call-update) | async-done | bytes 65552
  275.0 1.3 fusion.10
  276.3 0.6 convert_element_type.23
  (24 shorter events, 0.3 us)
Async XLA Ops:
  7.2 2.6 copy-start
  7.2 131.2 %all-gather.5.cloned.1.call-start = ((), (), s32[]{:S(2)}) async-start(), calls=%async_computation | async-start | bytes 9437184 | tf_op jit(solution)/shard_map/all_gather | solution.py:33
  7.9 267.1 %all-reduce.5.cloned.1.call-start = ((), (), s32[]{:S(2)}) async-start(), calls=%async_computation.1 | async-start | bytes 131072
  145.4 131.5 %copy-start.1 = (bf16[256,512]{1,0:T(8,128)(2,1)}, bf16[256,512]{1,0:T(8,128)(2,1)S(1)}, u32[]{:S(2)}) copy-start(bf16[256,512]{1,0:T(8,128)(2,1)S(1)} %convolution_convert_fusion) | copy-start | bytes 786436
Sparse Core Ops, SparseCore 0:
  10.1 128.2 all-gather.4
  208.4 66.5 all-reduce.4
where the time goes:
time: 284 us
  waiting for transfers between devices  160 us (56%)
  blocking collectives  94.1 us (33%)
  between operations  14.2 us (5%)
  matrix products  8.12 us (3%)
  local copies, waits for them, and re-layouts  4 us (1%)
  other arithmetic  3.41 us (1%)
    all_gather x1, waiting for transfers between devices, shards(): lax.all_gather(kv_weight, 'wide', axis=0, tiled=True)  92.4 us
    unnamed x3, waiting for transfers between devices  67.4 us
    all_gather x2, blocking collectives, combined_all(): gathered = jax.tree.map(lambda a: lax.all_gather(a, axis), part)  61 us
    all_gather x1, blocking collectives, shards(): gathered = lax.all_gather(queries, 'wide', axis=0, tiled=True)  33 us
    dot_general x1, matrix products, shards(): jnp.dot(new_tokens, lax.all_gather(kv_weight, 'wide', axis=0, tiled=True)...  6.98 us
  transfers between devices with their start and end apart: 2, of which 2 were waited for; matrix products, arithmetic and copies ran while one was open for 2% of the time, Pallas kernels for 0%

commit v1 on v0

v1 whole, which is shorter than its diff:
```python
import functools

import jax
import jax.numpy as jnp
from jax import lax
from jax.experimental import pallas as pl
from jax.experimental.pallas import tpu as pltpu
from jax.sharding import Mesh
from jax.sharding import PartitionSpec as P

HD = 128
GROUP = 8
CLEN = 512
DOCS = 2
FLIPS = ((0, 0), (1, 0), (0, 1), (1, 1))
SWAP = [(0, 1), (1, 0)]


def flip_pairs(dx, dy):
    return [((y * 2 + x), ((y ^ dy) * 2 + (x ^ dx))) for y in range(2) for x in range(2)]


def plane_permute(a, flip):
    dx, dy = flip
    if dy == 0:
        return lax.ppermute(a, "x", SWAP)
    if dx == 0:
        return lax.ppermute(a, "y", SWAP)
    return lax.ppermute(a, ("y", "x"), flip_pairs(dx, dy))


def dot32(a, b):
    return jnp.dot(a, b, preferred_element_type=jnp.float32)


def line_gather(w, z):
    pair = [(0, 1), (1, 0), (2, 3), (3, 2)]
    middle = [(1, 2), (2, 1)]
    outward = [(1, 0), (2, 3)]
    near = lax.ppermute(w, "z", pair)
    across = lax.ppermute(w, "z", middle)
    across_next = lax.ppermute(near, "z", middle)
    out = lax.ppermute(across, "z", outward)
    out_next = lax.ppermute(across_next, "z", outward)
    edge = (z == 0) | (z == 3)
    low = z < 2
    third = jnp.where(edge, out, across)
    fourth = jnp.where(edge, out_next, across_next)
    return [
        (z, w),
        (z ^ 1, near),
        (jnp.where(low, 2, 1), third),
        (jnp.where(low, 3, 0), fourth),
    ]


def project(tokens, weight):
    x, y, z, c = (lax.axis_index(a) for a in ("x", "y", "z", "c"))
    rows = tokens.shape[0]
    half = weight.shape[0] // 2
    nz, hz = 4, 2

    mine = lax.dynamic_slice_in_dim(weight, y * half, half, 0)
    blocks = line_gather(mine, z)

    view = tokens.reshape(rows, 2, hz, 2, 2, half)

    def piece(core, px, py):
        t = lax.dynamic_slice(view, (0, core, 0, px, py, 0), (rows, 1, hz, 1, 1, half))
        return jnp.transpose(t.reshape(rows, hz, half), (1, 0, 2))

    first = [piece(c, x, y)]
    second = [piece(1 - c, x, y)]
    for flip in FLIPS[1:]:
        got = plane_permute(piece(c, x ^ flip[0], y ^ flip[1]), flip)
        first.append(got)
        second.append(lax.ppermute(got, "c", SWAP))
    tall = jnp.concatenate([jnp.concatenate(first, 1), jnp.concatenate(second, 1)], 0)

    acc = None
    for source, block in blocks:
        at = lax.rem(source + c * hz, nz)
        t = lax.dynamic_index_in_dim(tall, at, 0, False)
        term = dot32(t, block)
        acc = term if acc is None else acc + term
    total = acc[:rows]
    for i, flip in enumerate(FLIPS):
        if i:
            total = total + plane_permute(acc[i * rows : (i + 1) * rows], flip)
    return total.astype(jnp.bfloat16)


def attend_kernel(q_ref, bias_ref, pre_ref, new_ref, out_ref):
    heads = q_ref.shape[0]
    rows = q_ref.shape[1]
    docs, pref_rows = pre_ref.shape[0], pre_ref.shape[1]
    lane = lax.broadcasted_iota(jnp.int32, (rows, HD), 1)
    contract = (((1,), (1,)), ((), ()))
    for g in range(heads):
        key = slice(2 * g * HD, (2 * g + 1) * HD)
        val = slice((2 * g + 1) * HD, (2 * g + 2) * HD)
        q = q_ref[g]
        parts = [(pre_ref[d, :, key], pre_ref[d, :, val]) for d in range(docs)]
        parts.append((new_ref[:, key], new_ref[:, val]))
        scores = []
        at = 0
        for k, _ in parts:
            s = lax.dot_general(q, k, contract, preferred_element_type=jnp.float32)
            s = s * (1.0 / HD**0.5) + bias_ref[:, at : at + k.shape[0]]
            scores.append(s)
            at += k.shape[0]
        peak = functools.reduce(jnp.maximum, [jnp.max(s, axis=1, keepdims=True) for s in scores])
        total = jnp.zeros((rows, 1), jnp.float32)
        mixed = jnp.zeros((rows, HD), jnp.float32)
        for s, (_, v) in zip(scores, parts):
            e = jnp.exp(s - peak)
            total = total + jnp.sum(e, axis=1, keepdims=True)
            mixed = mixed + jnp.dot(e.astype(jnp.bfloat16), v, preferred_element_type=jnp.float32)
        stat = jnp.where(lane < HD // 2, peak, total)
        n_quest = rows // GROUP
        out_ref[:, 0, g] = mixed.reshape(n_quest, GROUP, HD)
        out_ref[:, 1, g] = stat.reshape(n_quest, GROUP, HD)


def finish_kernel(n_dev, part_ref, out_ref):
    own = part_ref.shape[0] // n_dev
    heads = part_ref.shape[2]
    for r in range(own):
        for g in range(heads):
            peaks = [part_ref[d * own + r, 1, g, :, 0:1] for d in range(n_dev)]
            top = functools.reduce(jnp.maximum, peaks)
            total = jnp.zeros((GROUP, 1), jnp.float32)
            mixed = jnp.zeros((GROUP, HD), jnp.float32)
            for d in range(n_dev):
                scale = jnp.exp(peaks[d] - top)
                total = total + scale * part_ref[d * own + r, 1, g, :, HD // 2 : HD // 2 + 1]
                mixed = mixed + scale * part_ref[d * own + r, 0, g]
            done = (mixed / total).astype(jnp.bfloat16)
            for j in range(GROUP):
                at = (g * GROUP + j) * HD
                out_ref[r : r + 1, at : at + HD] = done[j : j + 1]


def shards(tokens, weight, prefix, queries, doc, lists, slots):
    nz = lax.axis_size("z")
    x, z = lax.axis_index("x"), lax.axis_index("z")
    rows = tokens.shape[0]
    heads = weight.shape[1] // (2 * HD)
    own_q = queries.shape[0]

    if nz == 4:
        new_cache = project(tokens, weight)
    else:
        new_cache = dot32(tokens, lax.all_gather(weight, ("z", "x"), axis=0, tiled=True)).astype(jnp.bfloat16)

    pair_q = jnp.concatenate([queries, lax.ppermute(queries, "x", SWAP)], 0)
    swapped = jnp.concatenate([pair_q[own_q:], pair_q[:own_q]], 0)
    pair_q = jnp.where(x == 0, pair_q, swapped)
    if nz == 4:
        near_q = lax.ppermute(pair_q, "z", [(0, 1), (1, 0), (2, 3), (3, 2)])
        low_q = jnp.where(z % 2 == 0, pair_q, near_q)
        high_q = jnp.where(z % 2 == 0, near_q, pair_q)
        half_q = jnp.concatenate([low_q, high_q], 0)
        far_q = lax.ppermute(half_q, "z", [(0, 2), (2, 0), (1, 3), (3, 1)])
        asked = jnp.concatenate([jnp.where(z < 2, half_q, far_q), jnp.where(z < 2, far_q, half_q)], 0)
    else:
        asked = lax.all_gather(pair_q, "z", axis=0, tiled=True)
    n_quest = asked.shape[0]
    asked = jnp.transpose(asked.reshape(n_quest, heads, GROUP, HD), (1, 0, 2, 3))
    asked = asked.reshape(heads, n_quest * GROUP, HD)

    pref_rows = prefix.shape[1]
    row_slot = ((z * 2 + x) * rows + jnp.arange(rows, dtype=jnp.int32)) // CLEN
    key_doc = jnp.concatenate(
        [jnp.arange(DOCS * pref_rows, dtype=jnp.int32) // pref_rows, jnp.full((rows,), -1, jnp.int32)]
    )
    key_slot = jnp.concatenate([jnp.full((DOCS * pref_rows,), -1, jnp.int32), row_slot])
    wanted = slots[lists]
    visible = (doc[:, None] == key_doc[None, :]) | jnp.any(
        wanted[:, :, None] == key_slot[None, None, :], axis=1
    )
    bias = jnp.where(visible, 0.0, -jnp.inf).astype(jnp.float32)
    bias = jnp.repeat(bias, GROUP, axis=0)

    part = pl.pallas_call(
        attend_kernel,
        out_shape=jax.ShapeDtypeStruct((n_quest, 2, heads, GROUP, HD), jnp.float32),
        compiler_params=pltpu.CompilerParams(vmem_limit_bytes=48 * 2**20),
    )(asked, bias, prefix, new_cache)
    part = lax.all_to_all(part, ("z", "x"), 0, 0, tiled=True)
    attended = pl.pallas_call(
        functools.partial(finish_kernel, 2 * nz),
        out_shape=jax.ShapeDtypeStruct((own_q, heads * GROUP * HD), jnp.bfloat16),
        compiler_params=pltpu.CompilerParams(vmem_limit_bytes=48 * 2**20),
    )(part)
    return new_cache, attended


def solution(mesh):
    groups, wide, narrow = (mesh.shape[a] for a in ("groups", "wide", "narrow"))
    split = Mesh(mesh.devices.reshape(groups, wide // 2, 2, narrow), ("y", "z", "x", "c"))
    row = ("y", "z", "x")
    placed = (
        P(row, None),
        P(("z", "x"), "c"),
        P(None, row, "c"),
        P(row, "c"),
        P("y"),
        P("y", None),
        P("y"),
    )
    return jax.shard_map(
        shards,
        mesh=split,
        in_specs=placed,
        out_specs=(P(row, "c"), P(row, "c")),
        check_vma=False,
    )
```

time: 284 us -> 121 us (0.43)
  waiting for transfers between devices: 160 us -> 49.1 us
  blocking collectives: 94.1 us -> 11.1 us
  starting transfers between devices: 0.08 us -> 35.7 us
  between operations: 14.2 us -> 1.01 us
  local copies, waits for them, and re-layouts: 4 us -> 14.8 us
  matrix products: 8.12 us -> 3.88 us
    all_gather x3 -> x0, blocking collectives: 94.1 us -> none  [the longest x2 61 us: combined_all(): gathered = jax.tree.map(lambda a: lax.all_gather(a, axis), part)]
    all_gather x1 -> x0, waiting for transfers between devices: 92.4 us -> none  [shards(): lax.all_gather(kv_weight, 'wide', axis=0, tiled=True)]
    unnamed x3 -> x0, waiting for transfers between devices: 67.4 us -> none
    ppermute x0 -> x17, waiting for transfers between devices: none -> 49.1 us  [the longest x1 15.2 us: shards(): pair_q = jnp.concatenate([queries, lax.ppermute(queries, 'x', SWAP)], 0)]
    ppermute x0 -> x17, starting transfers between devices: none -> 35.7 us  [the longest x1 17.6 us: shards(): far_q = lax.ppermute(half_q, 'z', [(0, 2), (2, 0), (1, 3), (3, 1)])]
    all_to_all x0 -> x1, blocking collectives: none -> 11.1 us  [shards(): part = lax.all_to_all(part, ('z', 'x'), 0, 0, tiled=True)]
    dynamic_slice x3 -> x7, local copies, waits for them, and re-layouts: 0.01 us -> 7.24 us  [the longest x6 7.21 us: piece(): lax.dynamic_slice(view, (0, core, 0, px, py, 0), (rows, 1, hz, 1, 1, half))]
    unnamed x6 -> x15, local copies, waits for them, and re-layouts: 1.27 us -> 6.47 us
  transfers between devices with their start and end apart: 2 -> 17, of which waited for: 2 -> 7; matrix products, arithmetic and copies ran while one was open for 2% -> 9% of each run, Pallas kernels for 0% -> 0%
where the time goes in v1:
time: 121 us
  waiting for transfers between devices  49.1 us (41%)
  starting transfers between devices  35.7 us (30%)
  local copies, waits for them, and re-layouts  14.8 us (12%)
  blocking collectives  11.1 us (9%)
  matrix products  3.88 us (3%)
  other arithmetic  3.45 us (3%)
  Pallas kernels  1.48 us (1%)
    ppermute x1, starting transfers between devices, shards(): far_q = lax.ppermute(half_q, 'z', [(0, 2), (2, 0), (1, 3), (3, 1)])  17.6 us
    ppermute x1, waiting for transfers between devices, shards(): pair_q = jnp.concatenate([queries, lax.ppermute(queries, 'x', SWAP)], 0)  15.2 us
    ppermute x2, waiting for transfers between devices, plane_permute(): return lax.ppermute(a, 'x', SWAP)  11.3 us
    all_to_all x1, blocking collectives, shards(): part = lax.all_to_all(part, ('z', 'x'), 0, 0, tiled=True)  11.1 us
    dynamic_slice x6, local copies, waits for them, and re-layouts, piece(): lax.dynamic_slice(view, (0, core, 0, px, py, 0), (rows, 1, hz, 1, 1, half))  7.21 us
    ppermute x1, waiting for transfers between devices, line_gather(): out = lax.ppermute(across, 'z', outward)  7.13 us
    ppermute x1, waiting for transfers between devices, line_gather(): out_next = lax.ppermute(across_next, 'z', outward)  6.72 us
    unnamed x15, local copies, waits for them, and re-layouts  6.47 us
  transfers between devices with their start and end apart: 17, of which 7 were waited for; matrix products, arithmetic and copies ran while one was open for 9% of the time, Pallas kernels for 0%

profile of v1, /device:TPU:0, one launch (start us, length us, event | category | flops | bytes accessed | tf_op | source)
XLA Modules:
  0.0 120.5 jit_solution(6763233719752181761)
XLA Ops:
  0.7 6.4 %copy.18 = bf16[256,8192]{0,1:T(8,128)(2,1)} copy(bf16[256,8192]{1,0:T(8,128)(2,1)} %param.7) | data formatting | bytes 8388608 | tf_op args[0]
  7.1 2.7 %constant_dynamic-slice_fusion.5 = (bf16[256,1,2,1,1,512]{0,5,4,3,2,1:T(8,128)(2,1)S(1)}, bf16[256,1,2,1,1,512]{0,5,4,3,2,1:T(8,128)(2,1)S(1)}, bf16[256,1,2,1,1...) fusion(bf16[256,2,2,2,2,512]{0,5,4,3,2,1:T(8,128)(2,1)} %bitcast.39, ...), kind=kLoop, calls=%fused_computation.44 | loop fusion | bytes 5242904 | tf_op jit(solution)/shard_map/dynamic_slice | solution.py:69
  9.8 2.1 %copy.20 = bf16[256,1,2,1,1,512]{5,0,4,3,2,1:T(8,128)(2,1)} copy(bf16[256,1,2,1,1,512]{0,5,4,3,2,1:T(8,128)(2,1)} %get-tuple-element.6) | data formatting | bytes 1048576 | tf_op jit(solution)/shard_map/dynamic_slice | solution.py:69
  11.9 2.9 %collective-permute-start = (bf16[2,256,512]{2,1,0:T(8,128)(2,1)}, bf16[2,256,512]{2,1,0:T(8,128)(2,1)}, u32[]{:S(2)}, u32[]{:S(2)}) collective-permute-start(bf16[2,256,512]{2,1,0:T(8,128)(2,1)} %bitcast.43), channel_id=1, source_target_pairs={{0,2},{2,0},{1,3},{3,1},{4,6},{6,4},{5,7},{7,5},{8,10},{10,8},{9,1... | collective-permute-start | bytes 1572872 | tf_op jit(solution)/shard_map/ppermute | solution.py:26
  15.8 1.5 %collective-permute-start.1 = (bf16[2,256,512]{2,1,0:T(8,128)(2,1)}, bf16[2,256,512]{2,1,0:T(8,128)(2,1)}, u32[]{:S(2)}, u32[]{:S(2)}) collective-permute-start(bf16[2,256,512]{2,1,0:T(8,128)(2,1)} %bitcast.42), channel_id=1, source_target_pairs={{0,16},{16,0},{1,17},{17,1},{2,18},{18,2},{3,19},{19,3},{4,20},{20... | collective-permute-start | bytes 1572872 | tf_op jit(solution)/shard_map/ppermute | solution.py:28
  17.3 1.0 copy.22
  18.4 2.1 %collective-permute-start.6 = (bf16[512,512]{1,0:T(8,128)(2,1)S(1)}, bf16[512,512]{1,0:T(8,128)(2,1)}, u32[]{:S(2)}, u32[]{:S(2)}) collective-permute-start(bf16[512,512]{1,0:T(8,128)(2,1)S(1)} %constant_dynamic-slice_fusion), channel_id=1, source_target_pairs={{0,4},{4,0},{8,12},{12,8},{1,5},{5,1},{9,13},{13,9},{2,6},{6,2},{1... | collective-permute-start | bytes 1572872 | tf_op jit(solution)/shard_map/ppermute | solution.py:40
  20.5 1.5 %collective-permute-start.14 = (bf16[1,2048]{1,0:T(2,128)(2,1)S(1)}, bf16[1,2048]{1,0:T(2,128)(2,1)S(1)}, u32[]{:S(2)}, u32[]{:S(2)}) collective-permute-start(bf16[1,2048]{1,0:T(2,128)(2,1)S(1)} %copy-done.4), channel_id=1, source_target_pairs={{0,2},{2,0},{1,3},{3,1},{4,6},{6,4},{5,7},{7,5},{8,10},{10,8},{9,1... | collective-permute-start | bytes 12296 | tf_op jit(solution)/shard_map/ppermute | solution.py:156
  23.2 15.2 %collective-permute-done.14 = bf16[1,2048]{1,0:T(2,128)(2,1)S(1)} collective-permute-done((bf16[1,2048]{1,0:T(2,128)(2,1)S(1)}, bf16[1,2048]{1,0:T(2,128)(2,1)S(1)}, u32[]{:S(2)}, u32[]{:S(2)}) %collective-permute-start.14) | collective-permute-done | bytes 4128 | tf_op jit(solution)/shard_map/ppermute | solution.py:156
  38.4 1.9 %collective-permute-start.15 = (bf16[2,2048]{1,0:T(2,128)(2,1)S(1)}, bf16[2,2048]{1,0:T(2,128)(2,1)S(1)}, u32[]{:S(2)}, u32[]{:S(2)}) collective-permute-start(bf16[2,2048]{1,0:T(2,128)(2,1)S(1)} %broadcast_select_fusion), channel_id=1, source_target_pairs={{0,4},{4,0},{8,12},{12,8},{1,5},{5,1},{9,13},{13,9},{2,6},{6,2},{1... | collective-permute-start | bytes 24584 | tf_op jit(solution)/shard_map/ppermute | solution.py:160
  40.9 1.3 %collective-permute-done.15 = bf16[2,2048]{1,0:T(2,128)(2,1)S(1)} collective-permute-done((bf16[2,2048]{1,0:T(2,128)(2,1)S(1)}, bf16[2,2048]{1,0:T(2,128)(2,1)S(1)}, u32[]{:S(2)}, u32[]{:S(2)}) %collective-permute-start.15) | collective-permute-done | bytes 8224 | tf_op jit(solution)/shard_map/ppermute | solution.py:160
  44.3 17.6 %collective-permute-start.16 = (bf16[4,2048]{1,0:T(4,128)(2,1)S(1)}, bf16[4,2048]{1,0:T(4,128)(2,1)S(1)}, u32[]{:S(2)}, u32[]{:S(2)}) collective-permute-start(bf16[4,2048]{1,0:T(4,128)(2,1)S(1)} %pad_maximum_fusion.1), channel_id=1, source_target_pairs={{0,8},{8,0},{4,12},{12,4},{1,9},{9,1},{5,13},{13,5},{2,10},{10,2},... | collective-permute-start | bytes 49160 | tf_op jit(solution)/shard_map/ppermute | solution.py:164
  61.9 1.3 %collective-permute-start.8 = (bf16[512,512]{1,0:T(8,128)(2,1)S(1)}, bf16[512,512]{1,0:T(8,128)(2,1)S(1)}, u32[]{:S(2)}, u32[]{:S(2)}) collective-permute-start(bf16[512,512]{1,0:T(8,128)(2,1)S(1)} %collective-permute-done.7), channel_id=1, source_target_pairs={{4,0},{8,12},{5,1},{9,13},{6,2},{10,14},{7,3},{11,15},{20,16},{24,... | collective-permute-start | bytes 1572872 | tf_op jit(solution)/shard_map/ppermute | solution.py:43
  63.2 1.3 %collective-permute-start.10 = (bf16[512,512]{1,0:T(8,128)(2,1)S(1)}, bf16[512,512]{1,0:T(8,128)(2,1)S(1)}, u32[]{:S(2)}, u32[]{:S(2)}) collective-permute-start(bf16[512,512]{1,0:T(8,128)(2,1)S(1)} %collective-permute-done.9), channel_id=1, source_target_pairs={{4,0},{8,12},{5,1},{9,13},{6,2},{10,14},{7,3},{11,15},{20,16},{24,... | collective-permute-start | bytes 1572872 | tf_op jit(solution)/shard_map/ppermute | solution.py:44
  64.6 2.8 %maximum_maximum_fusion = bf16[4,1024,512]{2,1,0:T(8,128)(2,1)S(1)} fusion(bf16[2,256,512]{2,1,0:T(8,128)(2,1)S(1)} %collective-permute-done.5, bf16[2,256,512]{2,1,0:T(8,128)(2,1)S(1)} %collective-permute-done.4, bf16[2,256,512]{2,1,0:T(8,128)(2,1)S(1)} %collective-permute-done.3, bf16[2,256,512]{2,1,0:T(8,128)(2,1)S(1)} %bitcast.40, ...), kind=kLoop, calls=%fused_computation.1 | loop fusion | flops 33554432 | bytes 8388608 | tf_op jit(solution)/shard_map/concatenate | solution.py:78
  68.1 1.8 %fusion.3 = f32[1024,512]{1,0:T(8,128)S(1)} fusion(bf16[512,512]{1,0:T(8,128)(2,1)} %collective-permute-done.6, bf16[4,1024,512]{2,1,0:T(8,128)(2,1)S(1)} %maximum_maximum_fusion, s32[]{:T(128)S(6)} %select_n.124), kind=kOutput, calls=%fused_computation.6 | convolution fusion | flops 536870912 | bytes 3670020 | tf_op jit(solution)/shard_map/dot_general | solution.py:33
  69.8 7.1 %collective-permute-done.8 = bf16[512,512]{1,0:T(8,128)(2,1)S(1)} collective-permute-done((bf16[512,512]{1,0:T(8,128)(2,1)S(1)}, bf16[512,512]{1,0:T(8,128)(2,1)S(1)}, u32[]{:S(2)}, u32[]{:S(2)}) %collective-permute-start.8) | collective-permute-done | bytes 524320 | tf_op jit(solution)/shard_map/ppermute | solution.py:43
  77.7 6.7 %collective-permute-done.10 = bf16[512,512]{1,0:T(8,128)(2,1)S(1)} collective-permute-done((bf16[512,512]{1,0:T(8,128)(2,1)S(1)}, bf16[512,512]{1,0:T(8,128)(2,1)S(1)}, u32[]{:S(2)}, u32[]{:S(2)}) %collective-permute-start.10) | collective-permute-done | bytes 524320 | tf_op jit(solution)/shard_map/ppermute | solution.py:44
  85.3 1.6 %collective-permute-start.11 = (f32[256,512]{1,0:T(8,128)S(1)}, f32[256,512]{1,0:T(8,128)S(1)}, u32[]{:S(2)}, u32[]{:S(2)}) collective-permute-start(f32[256,512]{1,0:T(8,128)S(1)} %get-tuple-element.7), channel_id=1, source_target_pairs={{0,2},{2,0},{1,3},{3,1},{4,6},{6,4},{5,7},{7,5},{8,10},{10,8},{9,1... | collective-permute-start | bytes 1572872 | tf_op jit(solution)/shard_map/ppermute | solution.py:26
  86.8 1.5 %collective-permute-start.12 = (f32[256,512]{1,0:T(8,128)S(1)}, f32[256,512]{1,0:T(8,128)S(1)}, u32[]{:S(2)}, u32[]{:S(2)}) collective-permute-start(f32[256,512]{1,0:T(8,128)S(1)} %get-tuple-element.9), channel_id=1, source_target_pairs={{0,16},{16,0},{1,17},{17,1},{2,18},{18,2},{3,19},{19,3},{4,20},{20... | collective-permute-start | bytes 1572872 | tf_op jit(solution)/shard_map/ppermute | solution.py:28
  88.9 11.3 %collective-permute-done.11 = f32[256,512]{1,0:T(8,128)S(1)} collective-permute-done((f32[256,512]{1,0:T(8,128)S(1)}, f32[256,512]{1,0:T(8,128)S(1)}, u32[]{:S(2)}, u32[]{:S(2)}) %collective-permute-start.11) | collective-permute-done | bytes 524320 | tf_op jit(solution)/shard_map/ppermute | solution.py:26
  100.2 6.1 %collective-permute-done.12 = f32[256,512]{1,0:T(8,128)S(1)} collective-permute-done((f32[256,512]{1,0:T(8,128)S(1)}, f32[256,512]{1,0:T(8,128)S(1)}, u32[]{:S(2)}, u32[]{:S(2)}) %collective-permute-start.12) | collective-permute-done | bytes 524320 | tf_op jit(solution)/shard_map/ppermute | solution.py:28
  106.3 1.3 %collective-permute-done.13 = f32[256,512]{1,0:T(8,128)S(1)} collective-permute-done((f32[256,512]{1,0:T(8,128)S(1)}, f32[256,512]{1,0:T(8,128)S(1)}, u32[]{:S(2)}, u32[]{:S(2)}) %collective-permute-start.13) | collective-permute-done | bytes 524320 | tf_op jit(solution)/shard_map/ppermute | solution.py:29
  108.6 11.1 %all_to_all.5.part_ref = f32[8,2,2,8,128]{4,3,2,1,0:T(8,128)S(1)} all-to-all(f32[8,2,2,8,128]{4,3,2,1,0:T(8,128)S(1)} %shard_map.86), channel_id=1, replica_groups=mesh['y'=2,'z'=4,'x'=2,'c'=2] {'z','x'}, dimensions={0} | all-to-all | bytes 262144 | tf_op jit(solution)/shard_map/all_to_all | solution.py:190
  (59 shorter events, 9.3 us)
Async XLA Ops:
  0.6 17.7 %copy-start = (bf16[1024,512]{1,0:T(8,128)(2,1)S(1)}, bf16[1024,512]{1,0:T(8,128)(2,1)}, u32[]{:S(2)}) copy-start(bf16[1024,512]{1,0:T(8,128)(2,1)} %param.8) | copy-start | bytes 3145732
  7.1 13.4 %copy-start.4 = (bf16[1,2048]{1,0:T(2,128)(2,1)S(1)}, bf16[1,2048]{1,0:T(2,128)(2,1)}, u32[]{:S(2)}) copy-start(bf16[1,2048]{1,0:T(2,128)(2,1)} %param.10) | copy-start | bytes 12292
  7.1 14.9 %copy-start.5 = (s32[8,8]{1,0:T(8,128)S(1)}, s32[8,8]{1,0:T(8,128)}, u32[]{:S(2)}) copy-start(s32[8,8]{1,0:T(8,128)} %param.12) | copy-start | bytes 772
  7.1 15.0 %copy-start.3 = (s32[4]{0:T(128)S(1)}, s32[4]{0:T(128)}, u32[]{:S(2)}) copy-start(s32[4]{0:T(128)} %param.13) | copy-start | bytes 52
  9.8 13.3 %copy-start.6 = (s32[8]{0:T(128)S(1)}, s32[8]{0:T(128)}, u32[]{:S(2)}) copy-start(s32[8]{0:T(128)} %param.11) | copy-start | bytes 100
  11.9 31.0 %collective-permute-start = (bf16[2,256,512]{2,1,0:T(8,128)(2,1)}, bf16[2,256,512]{2,1,0:T(8,128)(2,1)}, u32[]{:S(2)}, u32[]{:S(2)}) collective-permute-start(bf16[2,256,512]{2,1,0:T(8,128)(2,1)} %bitcast.43), channel_id=1, source_target_pairs={{0,2},{2,0},{1,3},{3,1},{4,6},{6,4},{5,7},{7,5},{8,10},{10,8},{9,1... | collective-permute-start | bytes 1572872 | tf_op jit(solution)/shard_map/ppermute | solution.py:26
  15.8 27.1 %collective-permute-start.1 = (bf16[2,256,512]{2,1,0:T(8,128)(2,1)}, bf16[2,256,512]{2,1,0:T(8,128)(2,1)}, u32[]{:S(2)}, u32[]{:S(2)}) collective-permute-start(bf16[2,256,512]{2,1,0:T(8,128)(2,1)} %bitcast.42), channel_id=1, source_target_pairs={{0,16},{16,0},{1,17},{17,1},{2,18},{18,2},{3,19},{19,3},{4,20},{20... | collective-permute-start | bytes 1572872 | tf_op jit(solution)/shard_map/ppermute | solution.py:28
  18.4 25.1 %collective-permute-start.2 = (bf16[2,256,512]{2,1,0:T(8,128)(2,1)}, bf16[2,256,512]{2,1,0:T(8,128)(2,1)}, u32[]{:S(2)}, u32[]{:S(2)}) collective-permute-start(bf16[2,256,512]{2,1,0:T(8,128)(2,1)} %bitcast.8), channel_id=1, source_target_pairs={{0,18},{2,16},{16,2},{18,0},{1,19},{3,17},{17,3},{19,1},{4,22},{6,... | collective-permute-start | bytes 1572872 | tf_op jit(solution)/shard_map/ppermute | solution.py:29
  18.4 25.1 %collective-permute-start.6 = (bf16[512,512]{1,0:T(8,128)(2,1)S(1)}, bf16[512,512]{1,0:T(8,128)(2,1)}, u32[]{:S(2)}, u32[]{:S(2)}) collective-permute-start(bf16[512,512]{1,0:T(8,128)(2,1)S(1)} %constant_dynamic-slice_fusion), channel_id=1, source_target_pairs={{0,4},{4,0},{8,12},{12,8},{1,5},{5,1},{9,13},{13,9},{2,6},{6,2},{1... | collective-permute-start | bytes 1572872 | tf_op jit(solution)/shard_map/ppermute | solution.py:40
  20.5 17.9 %collective-permute-start.14 = (bf16[1,2048]{1,0:T(2,128)(2,1)S(1)}, bf16[1,2048]{1,0:T(2,128)(2,1)S(1)}, u32[]{:S(2)}, u32[]{:S(2)}) collective-permute-start(bf16[1,2048]{1,0:T(2,128)(2,1)S(1)} %copy-done.4), channel_id=1, source_target_pairs={{0,2},{2,0},{1,3},{3,1},{4,6},{6,4},{5,7},{7,5},{8,10},{10,8},{9,1... | collective-permute-start | bytes 12296 | tf_op jit(solution)/shard_map/ppermute | solution.py:156
  38.4 3.7 %collective-permute-start.15 = (bf16[2,2048]{1,0:T(2,128)(2,1)S(1)}, bf16[2,2048]{1,0:T(2,128)(2,1)S(1)}, u32[]{:S(2)}, u32[]{:S(2)}) collective-permute-start(bf16[2,2048]{1,0:T(2,128)(2,1)S(1)} %broadcast_select_fusion), channel_id=1, source_target_pairs={{0,4},{4,0},{8,12},{12,8},{1,5},{5,1},{9,13},{13,9},{2,6},{6,2},{1... | collective-permute-start | bytes 24584 | tf_op jit(solution)/shard_map/ppermute | solution.py:160
  42.2 2.2 %collective-permute-start.7 = (bf16[512,512]{1,0:T(8,128)(2,1)S(1)}, bf16[512,512]{1,0:T(8,128)(2,1)S(1)}, u32[]{:S(2)}, u32[]{:S(2)}) collective-permute-start(bf16[512,512]{1,0:T(8,128)(2,1)S(1)} %constant_dynamic-slice_fusion), channel_id=1, source_target_pairs={{4,8},{8,4},{5,9},{9,5},{6,10},{10,6},{7,11},{11,7},{20,24},{24,20... | collective-permute-start | bytes 1572872 | tf_op jit(solution)/shard_map/ppermute | solution.py:41
  42.9 19.1 %collective-permute-start.3 = (bf16[2,256,512]{2,1,0:T(8,128)(2,1)}, bf16[2,256,512]{2,1,0:T(8,128)(2,1)S(1)}, u32[]{:S(2)}, u32[]{:S(2)}) collective-permute-start(bf16[2,256,512]{2,1,0:T(8,128)(2,1)} %collective-permute-done), channel_id=1, source_target_pairs={{0,1},{1,0},{2,3},{3,2},{4,5},{5,4},{6,7},{7,6},{8,9},{9,8},{10,11... | collective-permute-start | bytes 1572872 | tf_op jit(solution)/shard_map/ppermute | solution.py:77
  43.0 21.6 %collective-permute-start.4 = (bf16[2,256,512]{2,1,0:T(8,128)(2,1)}, bf16[2,256,512]{2,1,0:T(8,128)(2,1)S(1)}, u32[]{:S(2)}, u32[]{:S(2)}) collective-permute-start(bf16[2,256,512]{2,1,0:T(8,128)(2,1)} %collective-permute-done.1), channel_id=1, source_target_pairs={{0,1},{1,0},{2,3},{3,2},{4,5},{5,4},{6,7},{7,6},{8,9},{9,8},{10,11... | collective-permute-start | bytes 1572872 | tf_op jit(solution)/shard_map/ppermute | solution.py:77
  43.4 21.1 %collective-permute-start.5 = (bf16[2,256,512]{2,1,0:T(8,128)(2,1)}, bf16[2,256,512]{2,1,0:T(8,128)(2,1)S(1)}, u32[]{:S(2)}, u32[]{:S(2)}) collective-permute-start(bf16[2,256,512]{2,1,0:T(8,128)(2,1)} %collective-permute-done.2), channel_id=1, source_target_pairs={{0,1},{1,0},{2,3},{3,2},{4,5},{5,4},{6,7},{7,6},{8,9},{9,8},{10,11... | collective-permute-start | bytes 1572872 | tf_op jit(solution)/shard_map/ppermute | solution.py:77
  43.5 19.7 %collective-permute-start.9 = (bf16[512,512]{1,0:T(8,128)(2,1)}, bf16[512,512]{1,0:T(8,128)(2,1)S(1)}, u32[]{:S(2)}, u32[]{:S(2)}) collective-permute-start(bf16[512,512]{1,0:T(8,128)(2,1)} %collective-permute-done.6), channel_id=1, source_target_pairs={{4,8},{8,4},{5,9},{9,5},{6,10},{10,6},{7,11},{11,7},{20,24},{24,20... | collective-permute-start | bytes 1572872 | tf_op jit(solution)/shard_map/ppermute | solution.py:42
  44.3 44.5 %collective-permute-start.16 = (bf16[4,2048]{1,0:T(4,128)(2,1)S(1)}, bf16[4,2048]{1,0:T(4,128)(2,1)S(1)}, u32[]{:S(2)}, u32[]{:S(2)}) collective-permute-start(bf16[4,2048]{1,0:T(4,128)(2,1)S(1)} %pad_maximum_fusion.1), channel_id=1, source_target_pairs={{0,8},{8,0},{4,12},{12,4},{1,9},{9,1},{5,13},{13,5},{2,10},{10,2},... | collective-permute-start | bytes 49160 | tf_op jit(solution)/shard_map/ppermute | solution.py:164
  61.9 15.0 %collective-permute-start.8 = (bf16[512,512]{1,0:T(8,128)(2,1)S(1)}, bf16[512,512]{1,0:T(8,128)(2,1)S(1)}, u32[]{:S(2)}, u32[]{:S(2)}) collective-permute-start(bf16[512,512]{1,0:T(8,128)(2,1)S(1)} %collective-permute-done.7), channel_id=1, source_target_pairs={{4,0},{8,12},{5,1},{9,13},{6,2},{10,14},{7,3},{11,15},{20,16},{24,... | collective-permute-start | bytes 1572872 | tf_op jit(solution)/shard_map/ppermute | solution.py:43
  63.2 21.2 %collective-permute-start.10 = (bf16[512,512]{1,0:T(8,128)(2,1)S(1)}, bf16[512,512]{1,0:T(8,128)(2,1)S(1)}, u32[]{:S(2)}, u32[]{:S(2)}) collective-permute-start(bf16[512,512]{1,0:T(8,128)(2,1)S(1)} %collective-permute-done.9), channel_id=1, source_target_pairs={{4,0},{8,12},{5,1},{9,13},{6,2},{10,14},{7,3},{11,15},{20,16},{24,... | collective-permute-start | bytes 1572872 | tf_op jit(solution)/shard_map/ppermute | solution.py:44
  85.1 22.8 %copy-start.2 = (bf16[2,128,512]{2,1,0:T(8,128)(2,1)S(1)}, bf16[2,128,512]{2,1,0:T(8,128)(2,1)}, u32[]{:S(2)}) copy-start(bf16[2,128,512]{2,1,0:T(8,128)(2,1)} %pre_ref.1) | copy-start | bytes 786436
  85.3 14.9 %collective-permute-start.11 = (f32[256,512]{1,0:T(8,128)S(1)}, f32[256,512]{1,0:T(8,128)S(1)}, u32[]{:S(2)}, u32[]{:S(2)}) collective-permute-start(f32[256,512]{1,0:T(8,128)S(1)} %get-tuple-element.7), channel_id=1, source_target_pairs={{0,2},{2,0},{1,3},{3,1},{4,6},{6,4},{5,7},{7,5},{8,10},{10,8},{9,1... | collective-permute-start | bytes 1572872 | tf_op jit(solution)/shard_map/ppermute | solution.py:26
  86.8 19.5 %collective-permute-start.12 = (f32[256,512]{1,0:T(8,128)S(1)}, f32[256,512]{1,0:T(8,128)S(1)}, u32[]{:S(2)}, u32[]{:S(2)}) collective-permute-start(f32[256,512]{1,0:T(8,128)S(1)} %get-tuple-element.9), channel_id=1, source_target_pairs={{0,16},{16,0},{1,17},{17,1},{2,18},{18,2},{3,19},{19,3},{4,20},{20... | collective-permute-start | bytes 1572872 | tf_op jit(solution)/shard_map/ppermute | solution.py:28
  88.4 19.3 %collective-permute-start.13 = (f32[256,512]{1,0:T(8,128)S(1)}, f32[256,512]{1,0:T(8,128)S(1)}, u32[]{:S(2)}, u32[]{:S(2)}) collective-permute-start(f32[256,512]{1,0:T(8,128)S(1)} %get-tuple-element.8), channel_id=1, source_target_pairs={{0,18},{2,16},{16,2},{18,0},{1,19},{3,17},{17,3},{19,1},{4,22},{6,... | collective-permute-start | bytes 1572872 | tf_op jit(solution)/shard_map/ppermute | solution.py:29
  107.9 12.6 %copy-start.1 = (bf16[256,512]{1,0:T(8,128)(2,1)}, bf16[256,512]{1,0:T(8,128)(2,1)S(1)}, u32[]{:S(2)}) copy-start(bf16[256,512]{1,0:T(8,128)(2,1)S(1)} %fusion.13.new_ref) | copy-start | bytes 786436

commit v2 on v1

v2 whole, which is shorter than its diff:
```python
import functools

import jax
import jax.numpy as jnp
from jax import lax
from jax.experimental import pallas as pl
from jax.experimental.pallas import tpu as pltpu
from jax.sharding import Mesh
from jax.sharding import PartitionSpec as P

HD = 128
GROUP = 8
CLEN = 512
DOCS = 2
FLIPS = ((0, 0), (1, 0), (0, 1), (1, 1))
SWAP = [(0, 1), (1, 0)]
ALL = pltpu.CompilerParams(vmem_limit_bytes=60 * 2**20)
ROOM = pltpu.CompilerParams(vmem_limit_bytes=16 * 2**20)


def flip_pairs(dx, dy):
    return [((y * 2 + x), ((y ^ dy) * 2 + (x ^ dx))) for y in range(2) for x in range(2)]


def plane_permute(a, flip):
    dx, dy = flip
    if dy == 0:
        return lax.ppermute(a, "x", SWAP)
    if dx == 0:
        return lax.ppermute(a, "y", SWAP)
    return lax.ppermute(a, ("y", "x"), flip_pairs(dx, dy))


def dot32(a, b):
    return jnp.dot(a, b, preferred_element_type=jnp.float32)


def order_of(z):
    low = z < 2
    return [z, z ^ 1, jnp.where(low, 2, 1), jnp.where(low, 3, 0)]


def add_block(core, firsts, seconds, block):
    width = block.shape[0] // 2
    top, bottom = block[:width], block[width:]
    near = jnp.where(core == 0, top, bottom)
    far = jnp.where(core == 0, bottom, top)
    return [dot32(f, near) + dot32(s, far) for f, s in zip(firsts, seconds)]


def carve_kernel(flips, place_ref, tokens, *refs):
    *piece_refs, sems = refs
    width = piece_refs[0].shape[1] // 4
    order = [place_ref[i] for i in range(4)]
    core, x, y = place_ref[4], place_ref[6], place_ref[7]
    copies = []
    for n, (ref, (dx, dy, dc)) in enumerate(zip(piece_refs, flips)):
        for i, s in enumerate(order):
            at = (((s * 2 + (x ^ dx)) * 2 + (y ^ dy)) * 2 + (core ^ dc)) * width
            copies.append(
                pltpu.make_async_copy(
                    tokens.at[:, pl.ds(pl.multiple_of(at, width), width)],
                    ref.at[:, pl.ds(i * width, width)],
                    sems.at[n * 4 + i],
                )
            )
    for copy in copies:
        copy.start()
    for copy in copies:
        copy.wait()


def add_up(place_ref, firsts, seconds, blocks, half, start, sums):
    width = half // 2
    for index, block in enumerate(blocks, start):
        cut = slice(index * width, (index + 1) * width)
        terms = add_block(place_ref[4], [f[:, cut] for f in firsts], [s[:, cut] for s in seconds], block[:half])
        sums = [term if s is None else s + term for s, term in zip(sums, terms)]
    return sums


def early_kernel(half, place_ref, *refs):
    firsts, seconds, (own, near), acc_ref = refs[:3], refs[3:6], refs[6:8], refs[8]
    for b, s in enumerate(add_up(place_ref, firsts, seconds, [own, near], half, 0, [None] * 3)):
        acc_ref[b] = s


def late_blocks(place_ref, across, out, across_next, out_next):
    edge = place_ref[5] == 1
    return [jnp.where(edge, out[...], across[...]), jnp.where(edge, out_next[...], across_next[...])]


def late_kernel(half, place_ref, *refs):
    firsts, seconds, acc_ref, keep_ref, send_refs = refs[:3], refs[3:6], refs[6], refs[11], refs[12:]
    blocks = late_blocks(place_ref, *refs[7:11])
    sums = add_up(place_ref, firsts, seconds, blocks, half, 2, [acc_ref[b] for b in range(3)])
    keep_ref[...] = sums[0]
    for send, part in zip(send_refs, sums[1:]):
        pack(part, send)


def last_kernel(half, place_ref, first, second, own, near, across, out, across_next, out_next, send_ref, line_ref):
    blocks = [own[...], near[...], *late_blocks(place_ref, across, out, across_next, out_next)]
    for i, block in enumerate(blocks):
        line_ref[place_ref[i]] = block[half:]
    pack(add_up(place_ref, [first], [second], blocks, half, 0, [None])[0], send_ref)


def pack(part, ref):
    for g in range(part.shape[1] // (2 * HD)):
        key = part[:, 2 * g * HD : (2 * g + 1) * HD]
        high = key.astype(jnp.bfloat16)
        at = 3 * g * HD
        ref[:, at : at + HD] = high
        ref[:, at + HD : at + 2 * HD] = (key - high.astype(jnp.float32)).astype(jnp.bfloat16)
        ref[:, at + 2 * HD : at + 3 * HD] = part[:, (2 * g + 1) * HD : (2 * g + 2) * HD].astype(jnp.bfloat16)


def unpack(ref, g):
    at = 3 * g * HD
    high, low, value = (ref[:, at + i * HD : at + (i + 1) * HD].astype(jnp.float32) for i in range(3))
    return high + low, value


def project(tokens, weight, queries):
    x, y, z, c = (lax.axis_index(a) for a in ("x", "y", "z", "c"))
    rows = tokens.shape[0]
    columns = weight.shape[1]
    half = weight.shape[0] // 2
    nz = 4
    edge = (z == 0) | (z == 3)
    place = jnp.stack([*order_of(z), c, edge, x, y]).astype(jnp.int32)
    fence = lax.optimization_barrier
    own_q, q_width = queries.shape
    q_rows = own_q * q_width // columns
    q_room = q_rows + -q_rows % 16
    smem = pl.BlockSpec(memory_space=pltpu.SMEM)
    vmem = pl.BlockSpec(memory_space=pltpu.VMEM)
    hbm = pl.BlockSpec(memory_space=pltpu.HBM)

    flips = [(dx, dy, 0) for dx, dy in FLIPS[1:]] + [(0, 0, 0), (0, 0, 1)]
    piece = jax.ShapeDtypeStruct((rows, 2 * half), tokens.dtype)
    own = jnp.concatenate(
        [
            lax.dynamic_slice_in_dim(weight, y * half, half, 0),
            jnp.pad(queries.reshape(q_rows, columns), ((0, q_room - q_rows), (0, 0))),
        ],
        0,
    )
    own, tokens = fence((own, tokens))
    piece_x, piece_y, piece_d, kept, kept_other = pl.pallas_call(
        functools.partial(carve_kernel, flips),
        in_specs=[smem, hbm],
        out_specs=[vmem] * 5,
        out_shape=[piece] * 5,
        scratch_shapes=[pltpu.SemaphoreType.DMA((20,))],
        compiler_params=ALL,
    )(place, tokens)
    middle, outward = [(1, 2), (2, 1)], [(1, 0), (2, 3)]
    near = lax.ppermute(own, "z", [(0, 1), (1, 0), (2, 3), (3, 2)])
    across = lax.ppermute(own, "z", middle)
    across_next = lax.ppermute(near, "z", middle)
    out = lax.ppermute(across, "z", outward)
    across_then, _ = fence((across_next, out))
    out_next = lax.ppermute(across_then, "z", outward)
    tok_x = plane_permute(piece_x, FLIPS[1])
    tok_y = plane_permute(piece_y, FLIPS[2])
    tok_x, tok_y, piece_d = fence((tok_x, tok_y, piece_d))
    tok_d = plane_permute(piece_d, FLIPS[3])
    other_x, other_y, other_d = (lax.ppermute(t, "c", SWAP) for t in (tok_x, tok_y, tok_d))
    firsts, seconds = [kept, tok_x, tok_y], [kept_other, other_x, other_y]

    line = jax.ShapeDtypeStruct((nz, q_room, columns), queries.dtype)
    free = pl.BlockSpec()
    acc = pl.pallas_call(
        functools.partial(early_kernel, half),
        in_specs=[smem] + [free] * 8,
        out_specs=free,
        out_shape=jax.ShapeDtypeStruct((3, rows, columns), jnp.float32),
        compiler_params=ROOM,
    )(place, *firsts, *seconds, own, near)
    keep = jax.ShapeDtypeStruct((rows, columns), jnp.float32)
    send = jax.ShapeDtypeStruct((rows, columns // 2 * 3), jnp.bfloat16)
    arrived = (across, out, across_next, out_next)
    keep, send_x, send_y = pl.pallas_call(
        functools.partial(late_kernel, half),
        in_specs=[smem] + [free] * 11,
        out_specs=[free] * 3,
        out_shape=[keep, send, send],
        cost_estimate=pl.CostEstimate(flops=10**10, bytes_accessed=10**7, transcendentals=0),
        compiler_params=ROOM,
    )(place, *firsts, *seconds, acc, *arrived)
    send_d, line_q = pl.pallas_call(
        functools.partial(last_kernel, half),
        in_specs=[smem] + [free] * 8,
        out_specs=[free] * 2,
        out_shape=[send, line],
        compiler_params=ROOM,
    )(place, tok_d, other_d, own, near, *arrived)
    parts = [keep] + [plane_permute(p, flip) for p, flip in zip((send_x, send_y, send_d), FLIPS[1:])]

    line_q = line_q[:, :q_rows]
    other_q = lax.ppermute(line_q, "x", SWAP)
    low_q = jnp.where(x == 0, line_q, other_q).reshape(nz, own_q, q_width)
    high_q = jnp.where(x == 0, other_q, line_q).reshape(nz, own_q, q_width)
    asked = jnp.stack([low_q, high_q], 1).reshape(nz * 2 * own_q, q_width)
    return parts, asked


def attend_kernel(q_ref, bias_ref, pre_ref, *refs):
    keep_ref, *got_refs, new_ref, out_ref = refs
    for g in range(q_ref.shape[0]):
        cut = [slice((2 * g + i) * HD, (2 * g + i + 1) * HD) for i in range(2)]
        sums = [keep_ref[:, at] for at in cut]
        for got in got_refs:
            sums = [s + more for s, more in zip(sums, unpack(got, g))]
        for at, s in zip(cut, sums):
            new_ref[:, at] = s.astype(jnp.bfloat16)
    heads = q_ref.shape[0]
    rows = q_ref.shape[1]
    docs, pref_rows = pre_ref.shape[0], pre_ref.shape[1]
    lane = lax.broadcasted_iota(jnp.int32, (rows, HD), 1)
    contract = (((1,), (1,)), ((), ()))
    stat = jnp.zeros((rows, HD), jnp.float32)
    for g in range(heads):
        key = slice(2 * g * HD, (2 * g + 1) * HD)
        val = slice((2 * g + 1) * HD, (2 * g + 2) * HD)
        q = q_ref[g]
        parts = [(pre_ref[d, :, key], pre_ref[d, :, val]) for d in range(docs)]
        parts.append((new_ref[:, key], new_ref[:, val]))
        scores = []
        at = 0
        for k, _ in parts:
            s = lax.dot_general(q, k, contract, preferred_element_type=jnp.float32)
            s = s * (1.0 / HD**0.5) + bias_ref[:, at : at + k.shape[0]]
            scores.append(s)
            at += k.shape[0]
        peak = functools.reduce(jnp.maximum, [jnp.max(s, axis=1, keepdims=True) for s in scores])
        total = jnp.zeros((rows, 1), jnp.float32)
        mixed = jnp.zeros((rows, HD), jnp.float32)
        for s, (_, v) in zip(scores, parts):
            e = jnp.exp(s - peak)
            total = total + jnp.sum(e, axis=1, keepdims=True)
            mixed = mixed + jnp.dot(e.astype(jnp.bfloat16), v, preferred_element_type=jnp.float32)
        n_quest = rows // GROUP
        out_ref[:, g] = mixed.reshape(n_quest, GROUP, HD)
        stat = jnp.where(lane == 2 * g, peak, jnp.where(lane == 2 * g + 1, total, stat))
    out_ref[:, heads] = stat.reshape(n_quest, GROUP, HD)


def finish_kernel(n_dev, part_ref, out_ref):
    own = part_ref.shape[0] // n_dev
    heads = part_ref.shape[1] - 1
    for r in range(own):
        for g in range(heads):
            peaks = [part_ref[d * own + r, heads, :, 2 * g : 2 * g + 1] for d in range(n_dev)]
            top = functools.reduce(jnp.maximum, peaks)
            total = jnp.zeros((GROUP, 1), jnp.float32)
            mixed = jnp.zeros((GROUP, HD), jnp.float32)
            for d in range(n_dev):
                scale = jnp.exp(peaks[d] - top)
                total = total + scale * part_ref[d * own + r, heads, :, 2 * g + 1 : 2 * g + 2]
                mixed = mixed + scale * part_ref[d * own + r, g]
            done = (mixed / total).astype(jnp.bfloat16)
            for j in range(GROUP):
                at = (g * GROUP + j) * HD
                out_ref[r : r + 1, at : at + HD] = done[j : j + 1]


def shards(tokens, weight, prefix, queries, doc, lists, slots):
    nz = lax.axis_size("z")
    x, z = lax.axis_index("x"), lax.axis_index("z")
    rows = tokens.shape[0]
    heads = weight.shape[1] // (2 * HD)
    own_q = queries.shape[0]

    if nz == 4:
        parts, asked = project(tokens, weight, queries)
    else:
        parts = [dot32(tokens, lax.all_gather(weight, ("z", "x"), axis=0, tiled=True))]
        asked = lax.all_gather(queries, ("z", "x"), axis=0, tiled=True)
    n_quest = asked.shape[0]
    asked = jnp.transpose(asked.reshape(n_quest, heads, GROUP, HD), (1, 0, 2, 3))
    asked = asked.reshape(heads, n_quest * GROUP, HD)

    pref_rows = prefix.shape[1]
    row_slot = ((z * 2 + x) * rows + jnp.arange(rows, dtype=jnp.int32)) // CLEN
    key_doc = jnp.concatenate(
        [jnp.arange(DOCS * pref_rows, dtype=jnp.int32) // pref_rows, jnp.full((rows,), -1, jnp.int32)]
    )
    key_slot = jnp.concatenate([jnp.full((DOCS * pref_rows,), -1, jnp.int32), row_slot])
    wanted = slots[lists]
    visible = (doc[:, None] == key_doc[None, :]) | jnp.any(
        wanted[:, :, None] == key_slot[None, None, :], axis=1
    )
    bias = jnp.where(visible, 0.0, -jnp.inf).astype(jnp.float32)
    bias = jnp.repeat(bias, GROUP, axis=0)

    new_cache, part = pl.pallas_call(
        attend_kernel,
        out_shape=(
            jax.ShapeDtypeStruct(parts[0].shape, jnp.bfloat16),
            jax.ShapeDtypeStruct((n_quest, heads + 1, GROUP, HD), jnp.float32),
        ),
        compiler_params=ROOM,
    )(asked, bias, prefix, *parts)
    part = lax.all_to_all(part, ("z", "x"), 0, 0, tiled=True)
    attended = pl.pallas_call(
        functools.partial(finish_kernel, 2 * nz),
        out_shape=jax.ShapeDtypeStruct((own_q, heads * GROUP * HD), jnp.bfloat16),
        compiler_params=ROOM,
    )(part)
    return new_cache, attended


def solution(mesh):
    groups, wide, narrow = (mesh.shape[a] for a in ("groups", "wide", "narrow"))
    split = Mesh(mesh.devices.reshape(groups, wide // 2, 2, narrow), ("y", "z", "x", "c"))
    row = ("y", "z", "x")
    placed = (
        P(row, None),
        P(("z", "x"), "c"),
        P(None, row, "c"),
        P(row, "c"),
        P("y"),
        P("y", None),
        P("y"),
    )
    return jax.shard_map(
        shards,
        mesh=split,
        in_specs=placed,
        out_specs=(P(row, "c"), P(row, "c")),
        check_vma=False,
    )
```

time: 121 us -> 95.4 us (0.79)
  starting transfers between devices: 35.7 us -> 20.5 us
  Pallas kernels: 1.48 us -> 15 us
  waiting for transfers between devices: 49.1 us -> 39 us
  local copies, waits for them, and re-layouts: 14.8 us -> 8.03 us
  matrix products: 3.88 us -> 0 us
  other arithmetic: 3.45 us -> 1.17 us
    ppermute x11 -> x9, waiting for transfers between devices: 30.3 us -> 10 us  [the longest x1 7.76 us: project(): out_next = lax.ppermute(across_then, 'z', outward)]
    ppermute x11 -> x9, starting transfers between devices: 27.7 us -> 12.5 us  [the longest x1 5.88 us: project(): near = lax.ppermute(own, 'z', [(0, 1), (1, 0), (2, 3), (3, 2)])]
    pallas_call x1 -> x5, Pallas kernels: 0.72 us -> 14.3 us  [the longest x1 4.23 us: project(): pl.pallas_call(functools.partial(carve_kernel, flips), in_specs=[smem, hb...]
    ppermute x2, waiting for transfers between devices: 1.34 us -> 12.5 us  [plane_permute(): return lax.ppermute(a, ('y', 'x'), flip_pairs(dx, dy))]
    dynamic_slice x7 -> x1, local copies, waits for them, and re-layouts: 7.24 us -> 0.03 us  [project(): lax.dynamic_slice_in_dim(weight, y * half, half, 0)]
    ppermute x2, waiting for transfers between devices: 6.12 us -> 2.05 us  [plane_permute(): return lax.ppermute(a, 'y', SWAP)]
    dot_general x4 -> x0, matrix products: 3.88 us -> none  [dot32(): return jnp.dot(a, b, preferred_element_type=jnp.float32)]
    ppermute x2, waiting for transfers between devices: 11.3 us -> 14.4 us  [plane_permute(): return lax.ppermute(a, 'x', SWAP)]
  transfers between devices with their start and end apart: 17 -> 15, of which waited for: 7 -> 8; matrix products, arithmetic and copies ran while one was open for 9% -> 2% of each run, Pallas kernels for 0% -> 10%
where the time goes in v2:
time: 95.4 us; the launch traced here: 94.8 us
  waiting for transfers between devices  39 us (41%)
  starting transfers between devices  20.5 us (21%)
  Pallas kernels  15 us (16%)
  blocking collectives  10.2 us (11%)
  local copies, waits for them, and re-layouts  8.03 us (8%)
  other arithmetic  1.17 us (1%)
    ppermute x2, waiting for transfers between devices, plane_permute(): return lax.ppermute(a, 'x', SWAP)  14.4 us
    ppermute x2, waiting for transfers between devices, plane_permute(): return lax.ppermute(a, ('y', 'x'), flip_pairs(dx, dy))  12.5 us
    all_to_all x1, blocking collectives, shards(): part = lax.all_to_all(part, ('z', 'x'), 0, 0, tiled=True)  10.2 us
    ppermute x1, waiting for transfers between devices, project(): out_next = lax.ppermute(across_then, 'z', outward)  7.76 us
    unnamed x30, local copies, waits for them, and re-layouts  6.35 us
    ppermute x1, starting transfers between devices, project(): near = lax.ppermute(own, 'z', [(0, 1), (1, 0), (2, 3), (3, 2)])  5.88 us
    pallas_call x1, Pallas kernels, project(): pl.pallas_call(functools.partial(carve_kernel, flips), in_specs=[smem, hb...  4.23 us
    ppermute x2, starting transfers between devices, plane_permute(): return lax.ppermute(a, ('y', 'x'), flip_pairs(dx, dy))  3.23 us
  transfers between devices with their start and end apart: 15, of which 8 were waited for; matrix products, arithmetic and copies ran while one was open for 2% of the time, Pallas kernels for 10%

profile of v2, /device:TPU:0, one launch (start us, length us, event | category | flops | bytes accessed | tf_op | source)
XLA Modules:
  0.0 94.8 jit_solution(17934954751673889750)
XLA Ops:
  2.7 5.9 %collective-permute-start.4 = (bf16[528,512]{1,0:T(8,128)(2,1)S(1)}, bf16[528,512]{1,0:T(8,128)(2,1)S(1)}, u32[]{:S(2)}, u32[]{:S(2)}) collective-permute-start(bf16[528,512]{1,0:T(8,128)(2,1)S(1)} %fusion.1.own.refs_6_), channel_id=1, source_target_pairs={{0,4},{4,0},{8,12},{12,8},{1,5},{5,1},{9,13},{13,9},{2,6},{6,2},{1... | collective-permute-start | bytes 1622024 | tf_op jit(solution)/shard_map/ppermute | solution.py:160
  9.2 4.2 %shard_map.86 = (bf16[256,1024]{1,0:T(8,128)(2,1)}, bf16[256,1024]{1,0:T(8,128)(2,1)}, bf16[256,1024]{1,0:T(8,128)(2,1)}, bf16[256,1024]{1,0:T(8,128)(2,1)}, bf16[256,1024]{1,0:T(8,128)(2,1)}) custom-call(s32[8]{0:T(128)} %stack.42.place_ref, bf16[256,8192]{1,0:T(8,128)(2,1)} %tokens), custom_call_target="tpu_custom_call" | custom-call | tf_op jit(solution)/shard_map/pallas_call | solution.py:151
  13.4 1.6 %collective-permute-start = (bf16[256,1024]{1,0:T(8,128)(2,1)}, bf16[256,1024]{1,0:T(8,128)(2,1)S(1)}, u32[]{:S(2)}, u32[]{:S(2)}) collective-permute-start(bf16[256,1024]{1,0:T(8,128)(2,1)} %get-tuple-element.21), channel_id=1, source_target_pairs={{0,2},{2,0},{1,3},{3,1},{4,6},{6,4},{5,7},{7,5},{8,10},{10,8},{9,1... | collective-permute-start | bytes 1572872 | tf_op jit(solution)/shard_map/ppermute | solution.py:28
  14.9 1.5 %collective-permute-start.1 = (bf16[256,1024]{1,0:T(8,128)(2,1)}, bf16[256,1024]{1,0:T(8,128)(2,1)}, u32[]{:S(2)}, u32[]{:S(2)}) collective-permute-start(bf16[256,1024]{1,0:T(8,128)(2,1)} %get-tuple-element.22), channel_id=1, source_target_pairs={{0,16},{16,0},{1,17},{17,1},{2,18},{18,2},{3,19},{19,3},{4,20},{20... | collective-permute-start | bytes 1572872 | tf_op jit(solution)/shard_map/ppermute | solution.py:30
  16.5 10.3 %collective-permute-done.refs_1_ = bf16[256,1024]{1,0:T(8,128)(2,1)S(1)} collective-permute-done((bf16[256,1024]{1,0:T(8,128)(2,1)}, bf16[256,1024]{1,0:T(8,128)(2,1)S(1)}, u32[]{:S(2)}, u32[]{:S(2)}) %collective-permute-start) | collective-permute-done | bytes 524320 | tf_op jit(solution)/shard_map/ppermute | solution.py:28
  26.8 1.3 %collective-permute-done.1.refs_2_ = bf16[256,1024]{1,0:T(8,128)(2,1)} collective-permute-done((bf16[256,1024]{1,0:T(8,128)(2,1)}, bf16[256,1024]{1,0:T(8,128)(2,1)}, u32[]{:S(2)}, u32[]{:S(2)}) %collective-permute-start.1) | collective-permute-done | bytes 524320 | tf_op jit(solution)/shard_map/ppermute | solution.py:30
  28.1 1.5 %collective-permute-start.2 = (bf16[256,1024]{1,0:T(8,128)(2,1)}, bf16[256,1024]{1,0:T(8,128)(2,1)}, u32[]{:S(2)}, u32[]{:S(2)}) collective-permute-start(bf16[256,1024]{1,0:T(8,128)(2,1)} %get-tuple-element.24), channel_id=1, source_target_pairs={{0,18},{2,16},{16,2},{18,0},{1,19},{3,17},{17,3},{19,1},{4,22},{6,... | collective-permute-start | bytes 1572872 | tf_op jit(solution)/shard_map/ppermute | solution.py:31
  29.6 1.3 %collective-permute-start.6 = (bf16[528,512]{1,0:T(8,128)(2,1)S(1)}, bf16[528,512]{1,0:T(8,128)(2,1)S(1)}, u32[]{:S(2)}, u32[]{:S(2)}) collective-permute-start(bf16[528,512]{1,0:T(8,128)(2,1)S(1)} %collective-permute-done.5.across.refs_7_), channel_id=1, source_target_pairs={{4,0},{8,12},{5,1},{9,13},{6,2},{10,14},{7,3},{11,15},{20,16},{24,... | collective-permute-start | bytes 1622024 | tf_op jit(solution)/shard_map/ppermute | solution.py:163
  30.9 1.5 %collective-permute-start.7 = (bf16[528,512]{1,0:T(8,128)(2,1)S(1)}, bf16[528,512]{1,0:T(8,128)(2,1)}, u32[]{:S(2)}, u32[]{:S(2)}) collective-permute-start(bf16[528,512]{1,0:T(8,128)(2,1)S(1)} %collective-permute-done.4.near.refs_7_), channel_id=1, source_target_pairs={{4,8},{8,4},{5,9},{9,5},{6,10},{10,6},{7,11},{11,7},{20,24},{24,20... | collective-permute-start | bytes 1622024 | tf_op jit(solution)/shard_map/ppermute | solution.py:162
  33.9 7.3 %collective-permute-done.2.first = bf16[256,1024]{1,0:T(8,128)(2,1)} collective-permute-done((bf16[256,1024]{1,0:T(8,128)(2,1)}, bf16[256,1024]{1,0:T(8,128)(2,1)}, u32[]{:S(2)}, u32[]{:S(2)}) %collective-permute-start.2) | collective-permute-done | bytes 524320 | tf_op jit(solution)/shard_map/ppermute | solution.py:31
  41.2 2.3 %collective-permute-done.6.out.refs_8_ = bf16[528,512]{1,0:T(8,128)(2,1)S(1)} collective-permute-done((bf16[528,512]{1,0:T(8,128)(2,1)S(1)}, bf16[528,512]{1,0:T(8,128)(2,1)S(1)}, u32[]{:S(2)}, u32[]{:S(2)}) %collective-permute-start.6) | collective-permute-done | bytes 540704 | tf_op jit(solution)/shard_map/ppermute | solution.py:163
  43.5 1.3 %collective-permute-start.8 = (bf16[528,512]{1,0:T(8,128)(2,1)}, bf16[528,512]{1,0:T(8,128)(2,1)S(1)}, u32[]{:S(2)}, u32[]{:S(2)}) collective-permute-start(bf16[528,512]{1,0:T(8,128)(2,1)} %collective-permute-done.7.across_next.refs_9_), channel_id=1, source_target_pairs={{4,0},{8,12},{5,1},{9,13},{6,2},{10,14},{7,3},{11,15},{20,16},{24,... | collective-permute-start | bytes 1622024 | tf_op jit(solution)/shard_map/ppermute | solution.py:165
  48.1 2.0 %shard_map.88.refs_6_ = f32[3,256,512]{2,1,0:T(8,128)S(1)} custom-call(s32[8]{0:T(128)S(1)} %copy-done.11, bf16[256,1024]{1,0:T(8,128)(2,1)S(1)} %copy-done.1, bf16[256,1024]{1,0:T(8,128)(2,1)S(1)} %copy-done.6, bf16[256,1024]{1,0:T(8,128)(2,1)} %collective-permute-done.1.refs_2_, bf16[256,1024]{1,0:T(8,128)(2,1)S(1)} %copy-done.3, ...), custom_call_target="tpu_custom_call" | custom-call | tf_op jit(solution)/shard_map/pallas_call | solution.py:175
  50.2 7.8 %collective-permute-done.8.out_next.refs_10_ = bf16[528,512]{1,0:T(8,128)(2,1)S(1)} collective-permute-done((bf16[528,512]{1,0:T(8,128)(2,1)}, bf16[528,512]{1,0:T(8,128)(2,1)S(1)}, u32[]{:S(2)}, u32[]{:S(2)}) %collective-permute-start.8) | collective-permute-done | bytes 540704 | tf_op jit(solution)/shard_map/ppermute | solution.py:165
  58.0 2.7 %shard_map.87 = (bf16[256,768]{1,0:T(8,128)(2,1)}, bf16[4,16,512]{2,1,0:T(8,128)(2,1)S(1)}) custom-call(s32[8]{0:T(128)S(1)} %copy-done.11, bf16[256,1024]{1,0:T(8,128)(2,1)} %collective-permute-done.2.first, bf16[256,1024]{1,0:T(8,128)(2,1)S(1)} %collective-permute-done.3.second, bf16[528,512]{1,0:T(8,128)(2,1)S(1)} %fusion.1.own.refs_6_, ...), custom_call_target="tpu_custom_call" | custom-call | tf_op jit(solution)/shard_map/pallas_call | solution.py:193
  60.7 1.3 %collective-permute-start.9 = (bf16[4,4,512]{2,1,0:T(4,128)(2,1)S(1)}, bf16[4,4,512]{2,1,0:T(4,128)(2,1)S(1)}, u32[]{:S(2)}, u32[]{:S(2)}) collective-permute-start(bf16[4,4,512]{2,1,0:T(4,128)(2,1)S(1)} %slice.3), channel_id=1, source_target_pairs={{0,2},{2,0},{1,3},{3,1},{4,6},{6,4},{5,7},{7,5},{8,10},{10,8},{9,1... | collective-permute-start | bytes 49160 | tf_op jit(solution)/shard_map/ppermute | solution.py:203
  62.0 1.7 %collective-permute-start.14 = (bf16[256,768]{1,0:T(8,128)(2,1)}, bf16[256,768]{1,0:T(8,128)(2,1)}, u32[]{:S(2)}, u32[]{:S(2)}) collective-permute-start(bf16[256,768]{1,0:T(8,128)(2,1)} %get-tuple-element.35), channel_id=1, source_target_pairs={{0,18},{2,16},{16,2},{18,0},{1,19},{3,17},{17,3},{19,1},{4,22},{6,... | collective-permute-start | bytes 1179656 | tf_op jit(solution)/shard_map/ppermute | solution.py:31
  63.8 3.0 %shard_map.89 = (f32[256,512]{1,0:T(8,128)S(1)}, bf16[256,768]{1,0:T(8,128)(2,1)}, bf16[256,768]{1,0:T(8,128)(2,1)}) custom-call(s32[8]{0:T(128)S(1)} %copy-done.11, bf16[256,1024]{1,0:T(8,128)(2,1)S(1)} %copy-done.2, bf16[256,1024]{1,0:T(8,128)(2,1)S(1)} %copy-done.7, bf16[256,1024]{1,0:T(8,128)(2,1)} %collective-permute-done.1.refs_2_, ...), custom_call_target="tpu_custom_call" | custom-call | flops 10000000000 | bytes 10000000 | tf_op jit(solution)/shard_map/pallas_call | solution.py:185
  68.1 1.2 %collective-permute-start.13 = (bf16[256,768]{1,0:T(8,128)(2,1)}, bf16[256,768]{1,0:T(8,128)(2,1)S(1)}, u32[]{:S(2)}, u32[]{:S(2)}) collective-permute-start(bf16[256,768]{1,0:T(8,128)(2,1)} %get-tuple-element.34), channel_id=1, source_target_pairs={{0,16},{16,0},{1,17},{17,1},{2,18},{18,2},{3,19},{19,3},{4,20},{20... | collective-permute-start | bytes 1179656 | tf_op jit(solution)/shard_map/ppermute | solution.py:30
  69.5 5.2 %collective-permute-done.14.refs_3_ = bf16[256,768]{1,0:T(8,128)(2,1)} collective-permute-done((bf16[256,768]{1,0:T(8,128)(2,1)}, bf16[256,768]{1,0:T(8,128)(2,1)}, u32[]{:S(2)}, u32[]{:S(2)}) %collective-permute-start.14) | collective-permute-done | bytes 393248 | tf_op jit(solution)/shard_map/ppermute | solution.py:31
  74.7 4.1 %collective-permute-done.12.refs_1_ = bf16[256,768]{1,0:T(8,128)(2,1)S(1)} collective-permute-done((bf16[256,768]{1,0:T(8,128)(2,1)}, bf16[256,768]{1,0:T(8,128)(2,1)S(1)}, u32[]{:S(2)}, u32[]{:S(2)}) %collective-permute-start.12) | collective-permute-done | bytes 393248 | tf_op jit(solution)/shard_map/ppermute | solution.py:28
  79.6 1.0 %copy-done.9 = f32[256,512]{1,0:T(8,128)S(1)} copy-done((f32[256,512]{1,0:T(8,128)S(1)}, f32[256,512]{1,0:T(8,128)}, u32[]{:S(2)}) %copy-start.9) | copy-done | bytes 524312
  81.5 2.3 %shard_map.90 = (bf16[256,512]{1,0:T(8,128)(2,1)}, f32[8,3,8,128]{3,2,1,0:T(8,128)S(1)}) custom-call(bf16[2,64,128]{2,1,0:T(8,128)(2,1)S(1)} %copy_bitcast_fusion.q_ref, f32[64,512]{1,0:T(8,128)S(1)} %broadcast_bitcast_fusion.bias_ref, bf16[2,128,512]{2,1,0:T(8,128)(2,1)S(1)} %copy-done.10, f32[256,512]{1,0:T(8,128)S(1)} %copy-done.9, ...), custom_call_target="tpu_custom_call" | custom-call | tf_op jit(solution)/shard_map/pallas_call | solution.py:299
  83.9 10.2 %all_to_all.5.part_ref = f32[8,3,8,128]{3,2,1,0:T(8,128)S(1)} all-to-all(f32[8,3,8,128]{3,2,1,0:T(8,128)S(1)} %get-tuple-element.37), channel_id=1, replica_groups=mesh['y'=2,'z'=4,'x'=2,'c'=2] {'z','x'}, dimensions={0} | all-to-all | bytes 196608 | tf_op jit(solution)/shard_map/all_to_all | solution.py:307
  (67 shorter events, 11.5 us)
Async XLA Ops:
  0.6 1.2 %copy-start = (bf16[1024,512]{1,0:T(8,128)(2,1)S(1)}, bf16[1024,512]{1,0:T(8,128)(2,1)}, u32[]{:S(2)}) copy-start(bf16[1024,512]{1,0:T(8,128)(2,1)} %param.8) | copy-start | bytes 3145732
  2.0 27.6 %collective-permute-start.5 = (bf16[528,512]{1,0:T(8,128)(2,1)S(1)}, bf16[528,512]{1,0:T(8,128)(2,1)S(1)}, u32[]{:S(2)}, u32[]{:S(2)}) collective-permute-start(bf16[528,512]{1,0:T(8,128)(2,1)S(1)} %fusion.1.own.refs_6_), channel_id=1, source_target_pairs={{4,8},{8,4},{5,9},{9,5},{6,10},{10,6},{7,11},{11,7},{20,24},{24,20... | collective-permute-start | bytes 1622024 | tf_op jit(solution)/shard_map/ppermute | solution.py:161
  2.7 28.2 %collective-permute-start.4 = (bf16[528,512]{1,0:T(8,128)(2,1)S(1)}, bf16[528,512]{1,0:T(8,128)(2,1)S(1)}, u32[]{:S(2)}, u32[]{:S(2)}) collective-permute-start(bf16[528,512]{1,0:T(8,128)(2,1)S(1)} %fusion.1.own.refs_6_), channel_id=1, source_target_pairs={{0,4},{4,0},{8,12},{12,8},{1,5},{5,1},{9,13},{13,9},{2,6},{6,2},{1... | collective-permute-start | bytes 1622024 | tf_op jit(solution)/shard_map/ppermute | solution.py:160
  9.1 23.3 %copy-start.13 = (s32[8,8]{1,0:T(8,128)S(1)}, s32[8,8]{1,0:T(8,128)}, u32[]{:S(2)}) copy-start(s32[8,8]{1,0:T(8,128)} %param.12) | copy-start | bytes 772
  9.2 23.4 %copy-start.12 = (s32[4]{0:T(128)S(1)}, s32[4]{0:T(128)}, u32[]{:S(2)}) copy-start(s32[4]{0:T(128)} %param.13) | copy-start | bytes 52
  13.4 13.4 %collective-permute-start = (bf16[256,1024]{1,0:T(8,128)(2,1)}, bf16[256,1024]{1,0:T(8,128)(2,1)S(1)}, u32[]{:S(2)}, u32[]{:S(2)}) collective-permute-start(bf16[256,1024]{1,0:T(8,128)(2,1)} %get-tuple-element.21), channel_id=1, source_target_pairs={{0,2},{2,0},{1,3},{3,1},{4,6},{6,4},{5,7},{7,5},{8,10},{10,8},{9,1... | collective-permute-start | bytes 1572872 | tf_op jit(solution)/shard_map/ppermute | solution.py:28
  14.9 13.1 %collective-permute-start.1 = (bf16[256,1024]{1,0:T(8,128)(2,1)}, bf16[256,1024]{1,0:T(8,128)(2,1)}, u32[]{:S(2)}, u32[]{:S(2)}) collective-permute-start(bf16[256,1024]{1,0:T(8,128)(2,1)} %get-tuple-element.22), channel_id=1, source_target_pairs={{0,16},{16,0},{1,17},{17,1},{2,18},{18,2},{3,19},{19,3},{4,20},{20... | collective-permute-start | bytes 1572872 | tf_op jit(solution)/shard_map/ppermute | solution.py:30
  26.8 2.8 %copy-start.5 = (bf16[256,1024]{1,0:T(8,128)(2,1)}, bf16[256,1024]{1,0:T(8,128)(2,1)S(1)}, u32[]{:S(2)}) copy-start(bf16[256,1024]{1,0:T(8,128)(2,1)S(1)} %collective-permute-done.refs_1_) | copy-start | bytes 1572868
  28.1 13.1 %collective-permute-start.2 = (bf16[256,1024]{1,0:T(8,128)(2,1)}, bf16[256,1024]{1,0:T(8,128)(2,1)}, u32[]{:S(2)}, u32[]{:S(2)}) collective-permute-start(bf16[256,1024]{1,0:T(8,128)(2,1)} %get-tuple-element.24), channel_id=1, source_target_pairs={{0,18},{2,16},{16,2},{18,0},{1,19},{3,17},{17,3},{19,1},{4,22},{6,... | collective-permute-start | bytes 1572872 | tf_op jit(solution)/shard_map/ppermute | solution.py:31
  29.6 13.9 %collective-permute-start.6 = (bf16[528,512]{1,0:T(8,128)(2,1)S(1)}, bf16[528,512]{1,0:T(8,128)(2,1)S(1)}, u32[]{:S(2)}, u32[]{:S(2)}) collective-permute-start(bf16[528,512]{1,0:T(8,128)(2,1)S(1)} %collective-permute-done.5.across.refs_7_), channel_id=1, source_target_pairs={{4,0},{8,12},{5,1},{9,13},{6,2},{10,14},{7,3},{11,15},{20,16},{24,... | collective-permute-start | bytes 1622024 | tf_op jit(solution)/shard_map/ppermute | solution.py:163
  30.9 12.6 %collective-permute-start.7 = (bf16[528,512]{1,0:T(8,128)(2,1)S(1)}, bf16[528,512]{1,0:T(8,128)(2,1)}, u32[]{:S(2)}, u32[]{:S(2)}) collective-permute-start(bf16[528,512]{1,0:T(8,128)(2,1)S(1)} %collective-permute-done.4.near.refs_7_), channel_id=1, source_target_pairs={{4,8},{8,4},{5,9},{9,5},{6,10},{10,6},{7,11},{11,7},{20,24},{24,20... | collective-permute-start | bytes 1622024 | tf_op jit(solution)/shard_map/ppermute | solution.py:162
  32.5 12.3 %copy-start.14 = (s32[8]{0:T(128)S(1)}, s32[8]{0:T(128)}, u32[]{:S(2)}) copy-start(s32[8]{0:T(128)} %param.11) | copy-start | bytes 100
  32.5 12.4 %copy-start.11 = (s32[8]{0:T(128)S(1)}, s32[8]{0:T(128)}, u32[]{:S(2)}) copy-start(s32[8]{0:T(128)} %stack.42.place_ref) | copy-start | bytes 100
  33.4 11.6 %collective-permute-start.10 = (bf16[256,1024]{1,0:T(8,128)(2,1)}, bf16[256,1024]{1,0:T(8,128)(2,1)S(1)}, u32[]{:S(2)}, u32[]{:S(2)}) collective-permute-start(bf16[256,1024]{1,0:T(8,128)(2,1)} %copy-done.5), channel_id=1, source_target_pairs={{0,1},{1,0},{2,3},{3,2},{4,5},{5,4},{6,7},{7,6},{8,9},{9,8},{10,11... | collective-permute-start | bytes 1572872 | tf_op jit(solution)/shard_map/ppermute | solution.py:170
  33.4 11.6 %collective-permute-start.11 = (bf16[256,1024]{1,0:T(8,128)(2,1)}, bf16[256,1024]{1,0:T(8,128)(2,1)S(1)}, u32[]{:S(2)}, u32[]{:S(2)}) collective-permute-start(bf16[256,1024]{1,0:T(8,128)(2,1)} %collective-permute-done.1.refs_2_), channel_id=1, source_target_pairs={{0,1},{1,0},{2,3},{3,2},{4,5},{5,4},{6,7},{7,6},{8,9},{9,8},{10,11... | collective-permute-start | bytes 1572872 | tf_op jit(solution)/shard_map/ppermute | solution.py:170
  41.2 9.0 %collective-permute-start.3 = (bf16[256,1024]{1,0:T(8,128)(2,1)}, bf16[256,1024]{1,0:T(8,128)(2,1)S(1)}, u32[]{:S(2)}, u32[]{:S(2)}) collective-permute-start(bf16[256,1024]{1,0:T(8,128)(2,1)} %collective-permute-done.2.first), channel_id=1, source_target_pairs={{0,1},{1,0},{2,3},{3,2},{4,5},{5,4},{6,7},{7,6},{8,9},{9,8},{10,11... | collective-permute-start | bytes 1572872 | tf_op jit(solution)/shard_map/ppermute | solution.py:170
  43.5 14.5 %collective-permute-start.8 = (bf16[528,512]{1,0:T(8,128)(2,1)}, bf16[528,512]{1,0:T(8,128)(2,1)S(1)}, u32[]{:S(2)}, u32[]{:S(2)}) collective-permute-start(bf16[528,512]{1,0:T(8,128)(2,1)} %collective-permute-done.7.across_next.refs_9_), channel_id=1, source_target_pairs={{4,0},{8,12},{5,1},{9,13},{6,2},{10,14},{7,3},{11,15},{20,16},{24,... | collective-permute-start | bytes 1622024 | tf_op jit(solution)/shard_map/ppermute | solution.py:165
  50.2 13.6 %copy-start.2 = (bf16[256,1024]{1,0:T(8,128)(2,1)S(1)}, bf16[256,1024]{1,0:T(8,128)(2,1)}, u32[]{:S(2)}) copy-start(bf16[256,1024]{1,0:T(8,128)(2,1)} %get-tuple-element.28.refs_0_) | copy-start | bytes 1572868
  50.2 13.6 %copy-start.4 = (bf16[256,1024]{1,0:T(8,128)(2,1)S(1)}, bf16[256,1024]{1,0:T(8,128)(2,1)}, u32[]{:S(2)}) copy-start(bf16[256,1024]{1,0:T(8,128)(2,1)} %get-tuple-element.31.refs_3_) | copy-start | bytes 1572868
  50.2 13.6 %copy-start.7 = (bf16[256,1024]{1,0:T(8,128)(2,1)S(1)}, bf16[256,1024]{1,0:T(8,128)(2,1)}, u32[]{:S(2)}) copy-start(bf16[256,1024]{1,0:T(8,128)(2,1)} %copy-done.5) | copy-start | bytes 1572868
  60.7 8.6 %collective-permute-start.9 = (bf16[4,4,512]{2,1,0:T(4,128)(2,1)S(1)}, bf16[4,4,512]{2,1,0:T(4,128)(2,1)S(1)}, u32[]{:S(2)}, u32[]{:S(2)}) collective-permute-start(bf16[4,4,512]{2,1,0:T(4,128)(2,1)S(1)} %slice.3), channel_id=1, source_target_pairs={{0,2},{2,0},{1,3},{3,1},{4,6},{6,4},{5,7},{7,5},{8,10},{10,8},{9,1... | collective-permute-start | bytes 49160 | tf_op jit(solution)/shard_map/ppermute | solution.py:203
  62.0 12.7 %collective-permute-start.14 = (bf16[256,768]{1,0:T(8,128)(2,1)}, bf16[256,768]{1,0:T(8,128)(2,1)}, u32[]{:S(2)}, u32[]{:S(2)}) collective-permute-start(bf16[256,768]{1,0:T(8,128)(2,1)} %get-tuple-element.35), channel_id=1, source_target_pairs={{0,18},{2,16},{16,2},{18,0},{1,19},{3,17},{17,3},{19,1},{4,22},{6,... | collective-permute-start | bytes 1179656 | tf_op jit(solution)/shard_map/ppermute | solution.py:31
  67.6 11.3 %collective-permute-start.12 = (bf16[256,768]{1,0:T(8,128)(2,1)}, bf16[256,768]{1,0:T(8,128)(2,1)S(1)}, u32[]{:S(2)}, u32[]{:S(2)}) collective-permute-start(bf16[256,768]{1,0:T(8,128)(2,1)} %get-tuple-element.33), channel_id=1, source_target_pairs={{0,2},{2,0},{1,3},{3,1},{4,6},{6,4},{5,7},{7,5},{8,10},{10,8},{9,1... | collective-permute-start | bytes 1179656 | tf_op jit(solution)/shard_map/ppermute | solution.py:28
  68.1 11.4 %collective-permute-start.13 = (bf16[256,768]{1,0:T(8,128)(2,1)}, bf16[256,768]{1,0:T(8,128)(2,1)S(1)}, u32[]{:S(2)}, u32[]{:S(2)}) collective-permute-start(bf16[256,768]{1,0:T(8,128)(2,1)} %get-tuple-element.34), channel_id=1, source_target_pairs={{0,16},{16,0},{1,17},{17,1},{2,18},{18,2},{3,19},{19,3},{4,20},{20... | collective-permute-start | bytes 1179656 | tf_op jit(solution)/shard_map/ppermute | solution.py:30
  (6 other events, 5.9 us)

commit v3 on v2

--- a/solution.py
+++ b/solution.py
@@ -12,25 +12,11 @@
 GROUP = 8
 CLEN = 512
 DOCS = 2
-FLIPS = ((0, 0), (1, 0), (0, 1), (1, 1))
 SWAP = [(0, 1), (1, 0)]
 ALL = pltpu.CompilerParams(vmem_limit_bytes=60 * 2**20)
 ROOM = pltpu.CompilerParams(vmem_limit_bytes=16 * 2**20)
 
 
-def flip_pairs(dx, dy):
-    return [((y * 2 + x), ((y ^ dy) * 2 + (x ^ dx))) for y in range(2) for x in range(2)]
-
-
-def plane_permute(a, flip):
-    dx, dy = flip
-    if dy == 0:
-        return lax.ppermute(a, "x", SWAP)
-    if dx == 0:
-        return lax.ppermute(a, "y", SWAP)
-    return lax.ppermute(a, ("y", "x"), flip_pairs(dx, dy))
-
-
 def dot32(a, b):
     return jnp.dot(a, b, preferred_element_type=jnp.float32)
 
@@ -40,23 +26,14 @@
     return [z, z ^ 1, jnp.where(low, 2, 1), jnp.where(low, 3, 0)]
 
 
-def add_block(core, firsts, seconds, block):
-    width = block.shape[0] // 2
-    top, bottom = block[:width], block[width:]
-    near = jnp.where(core == 0, top, bottom)
-    far = jnp.where(core == 0, bottom, top)
-    return [dot32(f, near) + dot32(s, far) for f, s in zip(firsts, seconds)]
-
-
-def carve_kernel(flips, place_ref, tokens, *refs):
-    *piece_refs, sems = refs
+def carve_kernel(place_ref, tokens, *refs):
+    piece_refs, sems = refs[:3], refs[3]
     width = piece_refs[0].shape[1] // 4
-    order = [place_ref[i] for i in range(4)]
-    core, x, y = place_ref[4], place_ref[6], place_ref[7]
+    core, x = place_ref[4], place_ref[6]
     copies = []
-    for n, (ref, (dx, dy, dc)) in enumerate(zip(piece_refs, flips)):
-        for i, s in enumerate(order):
-            at = (((s * 2 + (x ^ dx)) * 2 + (y ^ dy)) * 2 + (core ^ dc)) * width
+    for n, (ref, (dx, dc)) in enumerate(zip(piece_refs, ((1, 0), (0, 0), (0, 1)))):
+        for i in range(4):
+            at = ((place_ref[i] * 2 + (x ^ dx)) * 2 + (core ^ dc)) * width
             copies.append(
                 pltpu.make_async_copy(
                     tokens.at[:, pl.ds(pl.multiple_of(at, width), width)],
@@ -70,40 +47,63 @@
         copy.wait()
 
 
-def add_up(place_ref, firsts, seconds, blocks, half, start, sums):
-    width = half // 2
-    for index, block in enumerate(blocks, start):
-        cut = slice(index * width, (index + 1) * width)
-        terms = add_block(place_ref[4], [f[:, cut] for f in firsts], [s[:, cut] for s in seconds], block[:half])
-        sums = [term if s is None else s + term for s, term in zip(sums, terms)]
-    return sums
+def half_terms(place_ref, firsts, seconds, index, along_z, along_y):
+    width = firsts[0].shape[1] // 4
+    cut = slice(index * width, (index + 1) * width)
+    same = place_ref[4] == place_ref[7]
+    terms = [None] * len(firsts)
+    for block, mine in ((along_z, same), (along_y, jnp.logical_not(same))):
+        if block is not None:
+            for b, (f, s) in enumerate(zip(firsts, seconds)):
+                term = dot32(jnp.where(mine, f[:, cut], s[:, cut]), block)
+                terms[b] = term if terms[b] is None else terms[b] + term
+    return terms
 
 
 def early_kernel(half, place_ref, *refs):
-    firsts, seconds, (own, near), acc_ref = refs[:3], refs[3:6], refs[6:8], refs[8]
-    for b, s in enumerate(add_up(place_ref, firsts, seconds, [own, near], half, 0, [None] * 3)):
-        acc_ref[b] = s
-
-
-def late_blocks(place_ref, across, out, across_next, out_next):
-    edge = place_ref[5] == 1
-    return [jnp.where(edge, out[...], across[...]), jnp.where(edge, out_next[...], across_next[...])]
-
-
-def late_kernel(half, place_ref, *refs):
-    firsts, seconds, acc_ref, keep_ref, send_refs = refs[:3], refs[3:6], refs[6], refs[11], refs[12:]
-    blocks = late_blocks(place_ref, *refs[7:11])
-    sums = add_up(place_ref, firsts, seconds, blocks, half, 2, [acc_ref[b] for b in range(3)])
-    keep_ref[...] = sums[0]
-    for send, part in zip(send_refs, sums[1:]):
-        pack(part, send)
-
-
-def last_kernel(half, place_ref, first, second, own, near, across, out, across_next, out_next, send_ref, line_ref):
-    blocks = [own[...], near[...], *late_blocks(place_ref, across, out, across_next, out_next)]
-    for i, block in enumerate(blocks):
-        line_ref[place_ref[i]] = block[half:]
-    pack(add_up(place_ref, [first], [second], blocks, half, 0, [None])[0], send_ref)
+    firsts, seconds, (own, weight, near, y_near, acc_ref, weight_ref, sem) = refs[:2], refs[2:4], refs[4:]
+    load = pltpu.make_async_copy(
+        weight.at[pl.ds(pl.multiple_of((1 - place_ref[7]) * half, half), half)], weight_ref, sem
+    )
+    load.start()
+    sums = half_terms(place_ref, firsts, seconds, 1, near[:half], y_near[:half])
+    load.wait()
+    terms = half_terms(place_ref, firsts, seconds, 0, own[:half], weight_ref[...])
+    for b in range(2):
+        acc_ref[b] = sums[b] + terms[b]
+
+
+def middle_kernel(half, q_rows, place_ref, *refs):
+    firsts, seconds = refs[:2], refs[2:4]
+    old_ref, own, near, third, fourth, y_third, acc_ref, line_ref, left_ref = refs[4:]
+    per = own.shape[1] // HD
+    for i, block in enumerate((own, near, third, fourth)):
+        for r in range(q_rows):
+            for h in range(per):
+                at = slice(h * HD, (h + 1) * HD)
+                line_ref[place_ref[i], r * per + h : r * per + h + 1] = block[half + r : half + r + 1, at]
+    sums = half_terms(place_ref, firsts, seconds, 2, third[:half], y_third[:half])
+    terms = half_terms(place_ref, firsts, seconds, 3, fourth[:half], None)
+    width = left_ref.shape[2]
+    cut = slice(3 * width, 4 * width)
+    other = place_ref[4] != place_ref[7]
+    for b in range(2):
+        acc_ref[b] = old_ref[b] + sums[b] + terms[b]
+        left_ref[b] = jnp.where(other, firsts[b][:, cut], seconds[b][:, cut])
+
+
+def late_kernel(half, left_ref, acc_ref, block_ref, keep_out, send_out, keep_ref, send_ref, sems):
+    block = block_ref[:half]
+    pack(acc_ref[1] + dot32(left_ref[1], block), send_ref)
+    copies = [
+        pltpu.make_async_copy(send_ref, send_out, sems.at[0]),
+        pltpu.make_async_copy(keep_ref, keep_out, sems.at[1]),
+    ]
+    copies[0].start()
+    keep_ref[...] = acc_ref[0] + dot32(left_ref[0], block)
+    copies[1].start()
+    for copy in copies:
+        copy.wait()
 
 
 def pack(part, ref):
@@ -137,9 +137,9 @@
     smem = pl.BlockSpec(memory_space=pltpu.SMEM)
     vmem = pl.BlockSpec(memory_space=pltpu.VMEM)
     hbm = pl.BlockSpec(memory_space=pltpu.HBM)
-
-    flips = [(dx, dy, 0) for dx, dy in FLIPS[1:]] + [(0, 0, 0), (0, 0, 1)]
-    piece = jax.ShapeDtypeStruct((rows, 2 * half), tokens.dtype)
+    anywhere = pl.BlockSpec(memory_space=pl.ANY)
+    free = pl.BlockSpec()
+
     own = jnp.concatenate(
         [
             lax.dynamic_slice_in_dim(weight, y * half, half, 0),
@@ -148,62 +148,72 @@
         0,
     )
     own, tokens = fence((own, tokens))
-    piece_x, piece_y, piece_d, kept, kept_other = pl.pallas_call(
-        functools.partial(carve_kernel, flips),
+    piece = jax.ShapeDtypeStruct((rows, 4 * half), tokens.dtype)
+    piece_x, kept, kept_other = pl.pallas_call(
+        carve_kernel,
         in_specs=[smem, hbm],
-        out_specs=[vmem] * 5,
-        out_shape=[piece] * 5,
-        scratch_shapes=[pltpu.SemaphoreType.DMA((20,))],
+        out_specs=[vmem] * 3,
+        out_shape=[piece] * 3,
+        scratch_shapes=[pltpu.SemaphoreType.DMA((12,))],
         compiler_params=ALL,
     )(place, tokens)
     middle, outward = [(1, 2), (2, 1)], [(1, 0), (2, 3)]
     near = lax.ppermute(own, "z", [(0, 1), (1, 0), (2, 3), (3, 2)])
     across = lax.ppermute(own, "z", middle)
+    tok = lax.ppermute(piece_x, "x", SWAP)
+
     across_next = lax.ppermute(near, "z", middle)
     out = lax.ppermute(across, "z", outward)
-    across_then, _ = fence((across_next, out))
-    out_next = lax.ppermute(across_then, "z", outward)
-    tok_x = plane_permute(piece_x, FLIPS[1])
-    tok_y = plane_permute(piece_y, FLIPS[2])
-    tok_x, tok_y, piece_d = fence((tok_x, tok_y, piece_d))
-    tok_d = plane_permute(piece_d, FLIPS[3])
-    other_x, other_y, other_d = (lax.ppermute(t, "c", SWAP) for t in (tok_x, tok_y, tok_d))
-    firsts, seconds = [kept, tok_x, tok_y], [kept_other, other_x, other_y]
-
-    line = jax.ShapeDtypeStruct((nz, q_room, columns), queries.dtype)
-    free = pl.BlockSpec()
+    y_near = lax.ppermute(near, "y", SWAP)
+
+    across_next, out, y_near = fence((across_next, out, y_near))
+    out_next = lax.ppermute(across_next, "z", outward)
+    third = jnp.where(edge, out, across)
+    y_third = lax.ppermute(third, "y", SWAP)
+
+    out_next, y_third = fence((out_next, y_third))
+    fourth = jnp.where(edge, out_next, across_next)
+    y_fourth = lax.ppermute(fourth, "y", SWAP)
+    other = lax.ppermute(tok, "c", SWAP)
+    sides = (kept, tok, kept_other, other)
+
+    acc_shape = jax.ShapeDtypeStruct((2, rows, columns), jnp.float32)
     acc = pl.pallas_call(
         functools.partial(early_kernel, half),
-        in_specs=[smem] + [free] * 8,
+        in_specs=[smem] + [free] * 5 + [anywhere] + [free] * 2,
         out_specs=free,
-        out_shape=jax.ShapeDtypeStruct((3, rows, columns), jnp.float32),
-        compiler_params=ROOM,
-    )(place, *firsts, *seconds, own, near)
-    keep = jax.ShapeDtypeStruct((rows, columns), jnp.float32)
-    send = jax.ShapeDtypeStruct((rows, columns // 2 * 3), jnp.bfloat16)
-    arrived = (across, out, across_next, out_next)
-    keep, send_x, send_y = pl.pallas_call(
+        out_shape=acc_shape,
+        scratch_shapes=[pltpu.VMEM((half, columns), weight.dtype), pltpu.SemaphoreType.DMA],
+        compiler_params=ROOM,
+    )(place, *sides, own, weight, near, y_near)
+    acc, line_q, left = pl.pallas_call(
+        functools.partial(middle_kernel, half, q_rows),
+        in_specs=[smem] + [free] * 10,
+        out_specs=[free] * 3,
+        out_shape=[
+            acc_shape,
+            jax.ShapeDtypeStruct((nz, q_rows * columns // HD, HD), queries.dtype),
+            jax.ShapeDtypeStruct((2, rows, half), tokens.dtype),
+        ],
+        compiler_params=ROOM,
+    )(place, *sides, acc, own, near, third, fourth, y_third)
+    keep = ((rows, columns), jnp.float32)
+    send = ((rows, columns // 2 * 3), jnp.bfloat16)
+    keep_here, send_x = pl.pallas_call(
         functools.partial(late_kernel, half),
-        in_specs=[smem] + [free] * 11,
-        out_specs=[free] * 3,
-        out_shape=[keep, send, send],
-        cost_estimate=pl.CostEstimate(flops=10**10, bytes_accessed=10**7, transcendentals=0),
-        compiler_params=ROOM,
-    )(place, *firsts, *seconds, acc, *arrived)
-    send_d, line_q = pl.pallas_call(
-        functools.partial(last_kernel, half),
-        in_specs=[smem] + [free] * 8,
-        out_specs=[free] * 2,
-        out_shape=[send, line],
-        compiler_params=ROOM,
-    )(place, tok_d, other_d, own, near, *arrived)
-    parts = [keep] + [plane_permute(p, flip) for p, flip in zip((send_x, send_y, send_d), FLIPS[1:])]
-
-    line_q = line_q[:, :q_rows]
+        in_specs=[free] * 3,
+        out_specs=[hbm] * 2,
+        out_shape=[pltpu.HBM(*keep), pltpu.HBM(*send)],
+        scratch_shapes=[pltpu.VMEM(*keep), pltpu.VMEM(*send), pltpu.SemaphoreType.DMA((2,))],
+        compiler_params=ROOM,
+    )(left, acc, y_fourth)
+    parts = [keep_here, lax.ppermute(send_x, "x", SWAP)]
+
     other_q = lax.ppermute(line_q, "x", SWAP)
-    low_q = jnp.where(x == 0, line_q, other_q).reshape(nz, own_q, q_width)
-    high_q = jnp.where(x == 0, other_q, line_q).reshape(nz, own_q, q_width)
-    asked = jnp.stack([low_q, high_q], 1).reshape(nz * 2 * own_q, q_width)
+    asked = jnp.stack([jnp.where(x == 0, line_q, other_q), jnp.where(x == 0, other_q, line_q)], 1)
+    heads = columns // (2 * HD)
+    asked = asked.reshape(nz, 2, own_q, heads, GROUP, HD).transpose(3, 0, 1, 2, 4, 5)
+    asked = asked.reshape(heads, nz * 2 * own_q * GROUP, HD)
     return parts, asked
 
 
@@ -279,9 +289,8 @@
     else:
         parts = [dot32(tokens, lax.all_gather(weight, ("z", "x"), axis=0, tiled=True))]
         asked = lax.all_gather(queries, ("z", "x"), axis=0, tiled=True)
-    n_quest = asked.shape[0]
-    asked = jnp.transpose(asked.reshape(n_quest, heads, GROUP, HD), (1, 0, 2, 3))
-    asked = asked.reshape(heads, n_quest * GROUP, HD)
+        asked = asked.reshape(-1, heads, GROUP, HD).transpose(1, 0, 2, 3).reshape(heads, -1, HD)
+    n_quest = asked.shape[1] // GROUP
 
     pref_rows = prefix.shape[1]
     row_slot = ((z * 2 + x) * rows + jnp.arange(rows, dtype=jnp.int32)) // CLEN

time: 95.4 us -> 89.1 us (0.934)
  starting transfers between devices: 20.5 us -> 16.3 us
  local copies, waits for them, and re-layouts: 8.03 us -> 5.03 us
  other arithmetic: 1.17 us -> 2.98 us
  Pallas kernels: 15 us -> 13.5 us
  blocking collectives: 10.2 us -> 11.7 us
    ppermute x10 -> x7, waiting for transfers between devices: 36.7 us -> 29.1 us  [the longest x1 10.6 us: project(): y_near = lax.ppermute(near, 'y', SWAP)]
    ppermute x1, waiting for transfers between devices: 0.01 us -> 5.07 us  [project(): near = lax.ppermute(own, 'z', [(0, 1), (1, 0), (2, 3), (3, 2)])]
    unnamed x30 -> x22, local copies, waits for them, and re-layouts: 6.35 us -> 2.31 us
    ppermute x1, starting transfers between devices: 5.88 us -> 3.09 us  [project(): near = lax.ppermute(own, 'z', [(0, 1), (1, 0), (2, 3), (3, 2)])]
    select_n x1 -> x2, other arithmetic: 0.02 us -> 1.97 us  [the longest x1 1.11 us: project(): fourth = jnp.where(edge, out_next, across_next)]
    ppermute x1, waiting for transfers between devices: 2.26 us -> 3.99 us  [project(): out = lax.ppermute(across, 'z', outward)]
    ppermute x10 -> x7, starting transfers between devices: 9.85 us -> 8.24 us  [the longest x1 1.68 us: project(): y_near = lax.ppermute(near, 'y', SWAP)]
    all_to_all x1, blocking collectives: 10.2 us -> 11.7 us  [shards(): part = lax.all_to_all(part, ('z', 'x'), 0, 0, tiled=True)]
  transfers between devices with their start and end apart: 15 -> 12, of which waited for: 8 -> 7; matrix products, arithmetic and copies ran while one was open for 2% -> 4% of each run, Pallas kernels for 10% -> 13%
where the time goes in v3:
time: 89.1 us; the launch traced here: 88.6 us
  waiting for transfers between devices  38.2 us (43%)
  starting transfers between devices  16.3 us (18%)
  Pallas kernels  13.5 us (15%)
  blocking collectives  11.7 us (13%)
  local copies, waits for them, and re-layouts  5.03 us (6%)
  other arithmetic  2.98 us (3%)
  between operations  0.95 us (1%)
    all_to_all x1, blocking collectives, shards(): part = lax.all_to_all(part, ('z', 'x'), 0, 0, tiled=True)  11.7 us
    ppermute x1, waiting for transfers between devices, project(): y_near = lax.ppermute(near, 'y', SWAP)  10.6 us
    ppermute x1, waiting for transfers between devices, project(): y_third = lax.ppermute(third, 'y', SWAP)  9.56 us
    ppermute x1, waiting for transfers between devices, project(): parts = [keep_here, lax.ppermute(send_x, 'x', SWAP)]  6.42 us
    ppermute x1, waiting for transfers between devices, project(): near = lax.ppermute(own, 'z', [(0, 1), (1, 0), (2, 3), (3, 2)])  5.07 us
    pallas_call x1, Pallas kernels, project(): pl.pallas_call(carve_kernel, in_specs=[smem, hbm], out_specs=[vmem] * 3,...  4.24 us
    ppermute x1, waiting for transfers between devices, project(): out = lax.ppermute(across, 'z', outward)  3.99 us
    ppermute x1, starting transfers between devices, project(): near = lax.ppermute(own, 'z', [(0, 1), (1, 0), (2, 3), (3, 2)])  3.09 us
  transfers between devices with their start and end apart: 12, of which 7 were waited for; matrix products, arithmetic and copies ran while one was open for 4% of the time, Pallas kernels for 13%

profile of v3, /device:TPU:0, one launch (start us, length us, event | category | flops | bytes accessed | tf_op | source)
XLA Modules:
  0.0 88.6 jit_solution(7270035519464312585)
XLA Ops:
  1.4 1.1 %constant_dynamic-slice_fusion = bf16[512,512]{1,0:T(8,128)(2,1)S(1)} fusion(bf16[1024,512]{1,0:T(8,128)(2,1)} %refs_5_.1, s32[]{:T(128)S(6)} %select_n.52), kind=kLoop, calls=%fused_computation.22 | loop fusion | bytes 1048580 | tf_op jit(solution)/shard_map/dynamic_slice | solution.py:145
  2.5 3.1 %collective-permute-start.2 = (bf16[528,512]{1,0:T(8,128)(2,1)S(1)}, bf16[528,512]{1,0:T(8,128)(2,1)S(1)}, u32[]{:S(2)}, u32[]{:S(2)}) collective-permute-start(bf16[528,512]{1,0:T(8,128)(2,1)S(1)} %fusion.1.refs_4_.refs_5_), channel_id=1, source_target_pairs={{0,4},{4,0},{8,12},{12,8},{1,5},{5,1},{9,13},{13,9},{2,6},{6,2},{1... | collective-permute-start | bytes 1622024 | tf_op jit(solution)/shard_map/ppermute | solution.py:161
  7.0 4.2 %shard_map.86 = (bf16[256,2048]{1,0:T(8,128)(2,1)}, bf16[256,2048]{1,0:T(8,128)(2,1)}, bf16[256,2048]{1,0:T(8,128)(2,1)}) custom-call(s32[8]{0:T(128)} %stack.48.place_ref, bf16[256,8192]{1,0:T(8,128)(2,1)} %tokens), custom_call_target="tpu_custom_call" | custom-call | tf_op jit(solution)/shard_map/pallas_call | solution.py:152
  11.3 1.6 %collective-permute-start = (bf16[256,2048]{1,0:T(8,128)(2,1)}, bf16[256,2048]{1,0:T(8,128)(2,1)}, u32[]{:S(2)}, u32[]{:S(2)}) collective-permute-start(bf16[256,2048]{1,0:T(8,128)(2,1)} %get-tuple-element.21), channel_id=1, source_target_pairs={{0,2},{2,0},{1,3},{3,1},{4,6},{6,4},{5,7},{7,5},{8,10},{10,8},{9,1... | collective-permute-start | bytes 3145736 | tf_op jit(solution)/shard_map/ppermute | solution.py:163
  12.8 5.1 %collective-permute-done.2.refs_6_ = bf16[528,512]{1,0:T(8,128)(2,1)S(1)} collective-permute-done((bf16[528,512]{1,0:T(8,128)(2,1)S(1)}, bf16[528,512]{1,0:T(8,128)(2,1)S(1)}, u32[]{:S(2)}, u32[]{:S(2)}) %collective-permute-start.2) | collective-permute-done | bytes 540704 | tf_op jit(solution)/shard_map/ppermute | solution.py:161
  17.9 1.5 %collective-permute-start.3 = (bf16[528,512]{1,0:T(8,128)(2,1)S(1)}, bf16[528,512]{1,0:T(8,128)(2,1)}, u32[]{:S(2)}, u32[]{:S(2)}) collective-permute-start(bf16[528,512]{1,0:T(8,128)(2,1)S(1)} %collective-permute-done.2.refs_6_), channel_id=1, source_target_pairs={{4,8},{8,4},{5,9},{9,5},{6,10},{10,6},{7,11},{11,7},{20,24},{24,20... | collective-permute-start | bytes 1622024 | tf_op jit(solution)/shard_map/ppermute | solution.py:165
  19.4 1.7 %collective-permute-start.6 = (bf16[528,512]{1,0:T(8,128)(2,1)S(1)}, bf16[528,512]{1,0:T(8,128)(2,1)S(1)}, u32[]{:S(2)}, u32[]{:S(2)}) collective-permute-start(bf16[528,512]{1,0:T(8,128)(2,1)S(1)} %collective-permute-done.2.refs_6_), channel_id=1, source_target_pairs={{0,16},{16,0},{1,17},{17,1},{2,18},{18,2},{3,19},{19,3},{4,20},{20... | collective-permute-start | bytes 1622024 | tf_op jit(solution)/shard_map/ppermute | solution.py:167
  21.0 1.3 %collective-permute-start.5 = (bf16[528,512]{1,0:T(8,128)(2,1)S(1)}, bf16[528,512]{1,0:T(8,128)(2,1)S(1)}, u32[]{:S(2)}, u32[]{:S(2)}) collective-permute-start(bf16[528,512]{1,0:T(8,128)(2,1)S(1)} %collective-permute-done.4), channel_id=1, source_target_pairs={{4,0},{8,12},{5,1},{9,13},{6,2},{10,14},{7,3},{11,15},{20,16},{24,... | collective-permute-start | bytes 1622024 | tf_op jit(solution)/shard_map/ppermute | solution.py:166
  22.3 10.6 %collective-permute-done.6.refs_7_ = bf16[528,512]{1,0:T(8,128)(2,1)S(1)} collective-permute-done((bf16[528,512]{1,0:T(8,128)(2,1)S(1)}, bf16[528,512]{1,0:T(8,128)(2,1)S(1)}, u32[]{:S(2)}, u32[]{:S(2)}) %collective-permute-start.6) | collective-permute-done | bytes 540704 | tf_op jit(solution)/shard_map/ppermute | solution.py:167
  32.9 4.0 %collective-permute-done.5 = bf16[528,512]{1,0:T(8,128)(2,1)S(1)} collective-permute-done((bf16[528,512]{1,0:T(8,128)(2,1)S(1)}, bf16[528,512]{1,0:T(8,128)(2,1)S(1)}, u32[]{:S(2)}, u32[]{:S(2)}) %collective-permute-start.5) | collective-permute-done | bytes 540704 | tf_op jit(solution)/shard_map/ppermute | solution.py:166
  38.3 1.3 %collective-permute-start.7 = (bf16[528,512]{1,0:T(8,128)(2,1)}, bf16[528,512]{1,0:T(8,128)(2,1)}, u32[]{:S(2)}, u32[]{:S(2)}) collective-permute-start(bf16[528,512]{1,0:T(8,128)(2,1)} %collective-permute-done.3), channel_id=1, source_target_pairs={{4,0},{8,12},{5,1},{9,13},{6,2},{10,14},{7,3},{11,15},{20,16},{24,... | collective-permute-start | bytes 1622024 | tf_op jit(solution)/shard_map/ppermute | solution.py:170
  40.7 9.6 %collective-permute-done.8.refs_9_ = bf16[528,512]{1,0:T(8,128)(2,1)} collective-permute-done((bf16[528,512]{1,0:T(8,128)(2,1)}, bf16[528,512]{1,0:T(8,128)(2,1)}, u32[]{:S(2)}, u32[]{:S(2)}) %collective-permute-start.8) | collective-permute-done | bytes 540704 | tf_op jit(solution)/shard_map/ppermute | solution.py:172
  50.2 2.1 %collective-permute-done.7 = bf16[528,512]{1,0:T(8,128)(2,1)} collective-permute-done((bf16[528,512]{1,0:T(8,128)(2,1)}, bf16[528,512]{1,0:T(8,128)(2,1)}, u32[]{:S(2)}, u32[]{:S(2)}) %collective-permute-start.7) | collective-permute-done | bytes 540704 | tf_op jit(solution)/shard_map/ppermute | solution.py:170
  52.4 1.1 %broadcast_select_fusion.refs_8_ = bf16[528,512]{1,0:T(8,128)(2,1)S(1)} fusion(bf16[528,512]{1,0:T(8,128)(2,1)} %collective-permute-done.7, bf16[528,512]{1,0:T(8,128)(2,1)} %collective-permute-done.3, pred[]{:T(512)S(6)} %or.6), kind=kLoop, calls=%fused_computation.4 | loop fusion | flops 270336 | bytes 1622017 | tf_op jit(solution)/shard_map/jit(_where)/select_n | solution.py:175
  53.5 1.6 %collective-permute-start.10 = (bf16[528,512]{1,0:T(8,128)(2,1)S(1)}, bf16[528,512]{1,0:T(8,128)(2,1)S(1)}, u32[]{:S(2)}, u32[]{:S(2)}) collective-permute-start(bf16[528,512]{1,0:T(8,128)(2,1)S(1)} %broadcast_select_fusion.refs_8_), channel_id=1, source_target_pairs={{0,16},{16,0},{1,17},{17,1},{2,18},{18,2},{3,19},{19,3},{4,20},{20... | collective-permute-start | bytes 1622024 | tf_op jit(solution)/shard_map/ppermute | solution.py:176
  55.4 1.2 %copy-done.3 = bf16[1024,512]{1,0:T(8,128)(2,1)S(1)} copy-done((bf16[1024,512]{1,0:T(8,128)(2,1)S(1)}, bf16[1024,512]{1,0:T(8,128)(2,1)}, u32[]{:S(2)}) %copy-start.3) | copy-done | bytes 1048600
  56.6 2.9 %shard_map.87.refs_4_ = f32[2,256,512]{2,1,0:T(8,128)S(1)} custom-call(s32[8]{0:T(128)S(1)} %copy-done.8, bf16[256,2048]{1,0:T(8,128)(2,1)S(1)} %copy-done.1, bf16[256,2048]{1,0:T(8,128)(2,1)} %collective-permute-done.refs_1_, bf16[256,2048]{1,0:T(8,128)(2,1)S(1)} %copy-done.2, bf16[256,2048]{1,0:T(8,128)(2,1)} %collective-permute-done.1.refs_3_, ...), custom_call_target="tpu_custom_call" | custom-call | tf_op jit(solution)/shard_map/pallas_call | solution.py:181
  59.5 3.0 %shard_map.88 = (f32[2,256,512]{2,1,0:T(8,128)S(1)}, bf16[4,16,128]{2,1,0:T(8,128)(2,1)S(1)}, bf16[2,256,512]{2,1,0:T(8,128)(2,1)S(1)}) custom-call(s32[8]{0:T(128)S(1)} %copy-done.8, bf16[256,2048]{1,0:T(8,128)(2,1)S(1)} %copy-done.1, bf16[256,2048]{1,0:T(8,128)(2,1)} %collective-permute-done.refs_1_, bf16[256,2048]{1,0:T(8,128)(2,1)S(1)} %copy-done.2, ...), custom_call_target="tpu_custom_call" | custom-call | tf_op jit(solution)/shard_map/pallas_call | solution.py:189
  62.5 1.5 %collective-permute-start.9 = (bf16[4,16,128]{2,1,0:T(8,128)(2,1)S(1)}, bf16[4,16,128]{2,1,0:T(8,128)(2,1)S(1)}, u32[]{:S(2)}, u32[]{:S(2)}) collective-permute-start(bf16[4,16,128]{2,1,0:T(8,128)(2,1)S(1)} %get-tuple-element.29), channel_id=1, source_target_pairs={{0,2},{2,0},{1,3},{3,1},{4,6},{6,4},{5,7},{7,5},{8,10},{10,8},{9,1... | collective-permute-start | bytes 49160 | tf_op jit(solution)/shard_map/ppermute | solution.py:212
  64.5 1.3 %shard_map.89 = (f32[256,512]{1,0:T(8,128)}, bf16[256,768]{1,0:T(8,128)(2,1)}) custom-call(bf16[2,256,512]{2,1,0:T(8,128)(2,1)S(1)} %get-tuple-element.30.left_ref, f32[2,256,512]{2,1,0:T(8,128)S(1)} %get-tuple-element.31.acc_ref, bf16[528,512]{1,0:T(8,128)(2,1)S(1)} %collective-permute-done.10.block_ref), custom_call_target="tpu_custom_call" | custom-call | tf_op jit(solution)/shard_map/pallas_call | solution.py:202
  65.8 1.6 %collective-permute-start.11 = (bf16[256,768]{1,0:T(8,128)(2,1)}, bf16[256,768]{1,0:T(8,128)(2,1)S(1)}, u32[]{:S(2)}, u32[]{:S(2)}) collective-permute-start(bf16[256,768]{1,0:T(8,128)(2,1)} %get-tuple-element.33), channel_id=1, source_target_pairs={{0,2},{2,0},{1,3},{3,1},{4,6},{6,4},{5,7},{7,5},{8,10},{10,8},{9,1... | collective-permute-start | bytes 1179656 | tf_op jit(solution)/shard_map/ppermute | solution.py:210
  67.4 6.4 %collective-permute-done.11.refs_1_ = bf16[256,768]{1,0:T(8,128)(2,1)S(1)} collective-permute-done((bf16[256,768]{1,0:T(8,128)(2,1)}, bf16[256,768]{1,0:T(8,128)(2,1)S(1)}, u32[]{:S(2)}, u32[]{:S(2)}) %collective-permute-start.11) | collective-permute-done | bytes 393248 | tf_op jit(solution)/shard_map/ppermute | solution.py:210
  74.9 1.3 %shard_map.90 = (bf16[256,512]{1,0:T(8,128)(2,1)}, f32[8,3,8,128]{3,2,1,0:T(8,128)S(1)}) custom-call(bf16[2,64,128]{2,1,0:T(8,128)(2,1)S(1)} %bitcast.17, f32[64,512]{1,0:T(8,128)S(1)} %broadcast_bitcast_fusion.bias_ref, bf16[2,128,512]{2,1,0:T(8,128)(2,1)S(1)} %copy-done.7, f32[256,512]{1,0:T(8,128)S(1)} %copy-done.6, ...), custom_call_target="tpu_custom_call" | custom-call | tf_op jit(solution)/shard_map/pallas_call | solution.py:308
  76.2 11.7 %all_to_all.5.part_ref = f32[8,3,8,128]{3,2,1,0:T(8,128)S(1)} all-to-all(f32[8,3,8,128]{3,2,1,0:T(8,128)S(1)} %get-tuple-element.35), channel_id=1, replica_groups=mesh['y'=2,'z'=4,'x'=2,'c'=2] {'z','x'}, dimensions={0} | all-to-all | bytes 196608 | tf_op jit(solution)/shard_map/all_to_all | solution.py:316
  (51 shorter events, 7.1 us)
Async XLA Ops:
  0.6 39.2 %copy-start = (s32[4]{0:T(128)S(1)}, s32[4]{0:T(128)}, u32[]{:S(2)}) copy-start(s32[4]{0:T(128)} %param.13) | copy-start | bytes 52
  2.5 15.4 %collective-permute-start.2 = (bf16[528,512]{1,0:T(8,128)(2,1)S(1)}, bf16[528,512]{1,0:T(8,128)(2,1)S(1)}, u32[]{:S(2)}, u32[]{:S(2)}) collective-permute-start(bf16[528,512]{1,0:T(8,128)(2,1)S(1)} %fusion.1.refs_4_.refs_5_), channel_id=1, source_target_pairs={{0,4},{4,0},{8,12},{12,8},{1,5},{5,1},{9,13},{13,9},{2,6},{6,2},{1... | collective-permute-start | bytes 1622024 | tf_op jit(solution)/shard_map/ppermute | solution.py:161
  5.6 15.4 %collective-permute-start.4 = (bf16[528,512]{1,0:T(8,128)(2,1)S(1)}, bf16[528,512]{1,0:T(8,128)(2,1)S(1)}, u32[]{:S(2)}, u32[]{:S(2)}) collective-permute-start(bf16[528,512]{1,0:T(8,128)(2,1)S(1)} %fusion.1.refs_4_.refs_5_), channel_id=1, source_target_pairs={{4,8},{8,4},{5,9},{9,5},{6,10},{10,6},{7,11},{11,7},{20,24},{24,20... | collective-permute-start | bytes 1622024 | tf_op jit(solution)/shard_map/ppermute | solution.py:162
  11.3 28.4 %copy-start.9 = (s32[8,8]{1,0:T(8,128)S(1)}, s32[8,8]{1,0:T(8,128)}, u32[]{:S(2)}) copy-start(s32[8,8]{1,0:T(8,128)} %param.12) | copy-start | bytes 772
  11.3 28.3 %collective-permute-start = (bf16[256,2048]{1,0:T(8,128)(2,1)}, bf16[256,2048]{1,0:T(8,128)(2,1)}, u32[]{:S(2)}, u32[]{:S(2)}) collective-permute-start(bf16[256,2048]{1,0:T(8,128)(2,1)} %get-tuple-element.21), channel_id=1, source_target_pairs={{0,2},{2,0},{1,3},{3,1},{4,6},{6,4},{5,7},{7,5},{8,10},{10,8},{9,1... | collective-permute-start | bytes 3145736 | tf_op jit(solution)/shard_map/ppermute | solution.py:163
  17.9 4.4 %collective-permute-start.3 = (bf16[528,512]{1,0:T(8,128)(2,1)S(1)}, bf16[528,512]{1,0:T(8,128)(2,1)}, u32[]{:S(2)}, u32[]{:S(2)}) collective-permute-start(bf16[528,512]{1,0:T(8,128)(2,1)S(1)} %collective-permute-done.2.refs_6_), channel_id=1, source_target_pairs={{4,8},{8,4},{5,9},{9,5},{6,10},{10,6},{7,11},{11,7},{20,24},{24,20... | collective-permute-start | bytes 1622024 | tf_op jit(solution)/shard_map/ppermute | solution.py:165
  19.4 13.6 %collective-permute-start.6 = (bf16[528,512]{1,0:T(8,128)(2,1)S(1)}, bf16[528,512]{1,0:T(8,128)(2,1)S(1)}, u32[]{:S(2)}, u32[]{:S(2)}) collective-permute-start(bf16[528,512]{1,0:T(8,128)(2,1)S(1)} %collective-permute-done.2.refs_6_), channel_id=1, source_target_pairs={{0,16},{16,0},{1,17},{17,1},{2,18},{18,2},{3,19},{19,3},{4,20},{20... | collective-permute-start | bytes 1622024 | tf_op jit(solution)/shard_map/ppermute | solution.py:167
  21.0 15.9 %collective-permute-start.5 = (bf16[528,512]{1,0:T(8,128)(2,1)S(1)}, bf16[528,512]{1,0:T(8,128)(2,1)S(1)}, u32[]{:S(2)}, u32[]{:S(2)}) collective-permute-start(bf16[528,512]{1,0:T(8,128)(2,1)S(1)} %collective-permute-done.4), channel_id=1, source_target_pairs={{4,0},{8,12},{5,1},{9,13},{6,2},{10,14},{7,3},{11,15},{20,16},{24,... | collective-permute-start | bytes 1622024 | tf_op jit(solution)/shard_map/ppermute | solution.py:166
  32.9 6.9 %copy-start.4 = (bf16[528,512]{1,0:T(8,128)(2,1)}, bf16[528,512]{1,0:T(8,128)(2,1)S(1)}, u32[]{:S(2)}) copy-start(bf16[528,512]{1,0:T(8,128)(2,1)S(1)} %collective-permute-done.6.refs_7_) | copy-start | bytes 1622020
  37.8 12.5 %collective-permute-start.8 = (bf16[528,512]{1,0:T(8,128)(2,1)}, bf16[528,512]{1,0:T(8,128)(2,1)}, u32[]{:S(2)}, u32[]{:S(2)}) collective-permute-start(bf16[528,512]{1,0:T(8,128)(2,1)} %broadcast_select_fusion.1.refs_7_), channel_id=1, source_target_pairs={{0,16},{16,0},{1,17},{17,1},{2,18},{18,2},{3,19},{19,3},{4,20},{20... | collective-permute-start | bytes 1622024 | tf_op jit(solution)/shard_map/ppermute | solution.py:172
  38.3 14.1 %collective-permute-start.7 = (bf16[528,512]{1,0:T(8,128)(2,1)}, bf16[528,512]{1,0:T(8,128)(2,1)}, u32[]{:S(2)}, u32[]{:S(2)}) collective-permute-start(bf16[528,512]{1,0:T(8,128)(2,1)} %collective-permute-done.3), channel_id=1, source_target_pairs={{4,0},{8,12},{5,1},{9,13},{6,2},{10,14},{7,3},{11,15},{20,16},{24,... | collective-permute-start | bytes 1622024 | tf_op jit(solution)/shard_map/ppermute | solution.py:170
  39.6 15.7 %collective-permute-start.1 = (bf16[256,2048]{1,0:T(8,128)(2,1)}, bf16[256,2048]{1,0:T(8,128)(2,1)}, u32[]{:S(2)}, u32[]{:S(2)}) collective-permute-start(bf16[256,2048]{1,0:T(8,128)(2,1)} %collective-permute-done.refs_1_), channel_id=1, source_target_pairs={{0,1},{1,0},{2,3},{3,2},{4,5},{5,4},{6,7},{7,6},{8,9},{9,8},{10,11... | collective-permute-start | bytes 3145736 | tf_op jit(solution)/shard_map/ppermute | solution.py:177
  39.8 15.5 %copy-start.2 = (bf16[256,2048]{1,0:T(8,128)(2,1)S(1)}, bf16[256,2048]{1,0:T(8,128)(2,1)}, u32[]{:S(2)}) copy-start(bf16[256,2048]{1,0:T(8,128)(2,1)} %get-tuple-element.22.refs_2_) | copy-start | bytes 3145732
  40.6 14.6 %copy-start.10 = (s32[8]{0:T(128)S(1)}, s32[8]{0:T(128)}, u32[]{:S(2)}) copy-start(s32[8]{0:T(128)} %param.11) | copy-start | bytes 100
  40.6 14.7 %copy-start.1 = (bf16[256,2048]{1,0:T(8,128)(2,1)S(1)}, bf16[256,2048]{1,0:T(8,128)(2,1)}, u32[]{:S(2)}) copy-start(bf16[256,2048]{1,0:T(8,128)(2,1)} %get-tuple-element.20.refs_0_) | copy-start | bytes 3145732
  40.6 14.7 %copy-start.8 = (s32[8]{0:T(128)S(1)}, s32[8]{0:T(128)}, u32[]{:S(2)}) copy-start(s32[8]{0:T(128)} %stack.48.place_ref) | copy-start | bytes 100
  40.7 14.7 %copy-start.5 = (bf16[528,512]{1,0:T(8,128)(2,1)S(1)}, bf16[528,512]{1,0:T(8,128)(2,1)}, u32[]{:S(2)}) copy-start(bf16[528,512]{1,0:T(8,128)(2,1)} %copy-done.4) | copy-start | bytes 1622020
  53.5 11.0 %collective-permute-start.10 = (bf16[528,512]{1,0:T(8,128)(2,1)S(1)}, bf16[528,512]{1,0:T(8,128)(2,1)S(1)}, u32[]{:S(2)}, u32[]{:S(2)}) collective-permute-start(bf16[528,512]{1,0:T(8,128)(2,1)S(1)} %broadcast_select_fusion.refs_8_), channel_id=1, source_target_pairs={{0,16},{16,0},{1,17},{17,1},{2,18},{18,2},{3,19},{19,3},{4,20},{20... | collective-permute-start | bytes 1622024 | tf_op jit(solution)/shard_map/ppermute | solution.py:176
  55.3 1.2 %copy-start.3 = (bf16[1024,512]{1,0:T(8,128)(2,1)S(1)}, bf16[1024,512]{1,0:T(8,128)(2,1)}, u32[]{:S(2)}) copy-start(bf16[1024,512]{1,0:T(8,128)(2,1)} %refs_5_.1) | copy-start | bytes 3145732
  62.5 4.9 %collective-permute-start.9 = (bf16[4,16,128]{2,1,0:T(8,128)(2,1)S(1)}, bf16[4,16,128]{2,1,0:T(8,128)(2,1)S(1)}, u32[]{:S(2)}, u32[]{:S(2)}) collective-permute-start(bf16[4,16,128]{2,1,0:T(8,128)(2,1)S(1)} %get-tuple-element.29), channel_id=1, source_target_pairs={{0,2},{2,0},{1,3},{3,1},{4,6},{6,4},{5,7},{7,5},{8,10},{10,8},{9,1... | collective-permute-start | bytes 49160 | tf_op jit(solution)/shard_map/ppermute | solution.py:212
  64.5 9.3 %copy-start.7 = (bf16[2,128,512]{2,1,0:T(8,128)(2,1)S(1)}, bf16[2,128,512]{2,1,0:T(8,128)(2,1)}, u32[]{:S(2)}) copy-start(bf16[2,128,512]{2,1,0:T(8,128)(2,1)} %pre_ref.1) | copy-start | bytes 786436
  65.8 8.1 %collective-permute-start.11 = (bf16[256,768]{1,0:T(8,128)(2,1)}, bf16[256,768]{1,0:T(8,128)(2,1)S(1)}, u32[]{:S(2)}, u32[]{:S(2)}) collective-permute-start(bf16[256,768]{1,0:T(8,128)(2,1)} %get-tuple-element.33), channel_id=1, source_target_pairs={{0,2},{2,0},{1,3},{3,1},{4,6},{6,4},{5,7},{7,5},{8,10},{10,8},{9,1... | collective-permute-start | bytes 1179656 | tf_op jit(solution)/shard_map/ppermute | solution.py:210
  73.8 1.0 %copy-start.6 = (f32[256,512]{1,0:T(8,128)S(1)}, f32[256,512]{1,0:T(8,128)}, u32[]{:S(2)}) copy-start(f32[256,512]{1,0:T(8,128)} %get-tuple-element.32.refs_0_) | copy-start | bytes 1572868

commit v4 on v3

--- a/solution.py
+++ b/solution.py
@@ -92,18 +92,16 @@
         left_ref[b] = jnp.where(other, firsts[b][:, cut], seconds[b][:, cut])
 
 
-def late_kernel(half, left_ref, acc_ref, block_ref, keep_out, send_out, keep_ref, send_ref, sems):
-    block = block_ref[:half]
-    pack(acc_ref[1] + dot32(left_ref[1], block), send_ref)
-    copies = [
-        pltpu.make_async_copy(send_ref, send_out, sems.at[0]),
-        pltpu.make_async_copy(keep_ref, keep_out, sems.at[1]),
-    ]
-    copies[0].start()
-    keep_ref[...] = acc_ref[0] + dot32(left_ref[0], block)
-    copies[1].start()
-    for copy in copies:
-        copy.wait()
+def mark_kernel(given_ref, mark_ref):
+    mark_ref[...] = jnp.zeros_like(mark_ref)
+
+
+def send_kernel(half, left_ref, acc_ref, block_ref, mark_ref, send_ref):
+    pack(acc_ref[1] + dot32(left_ref[1], block_ref[:half]), send_ref)
+
+
+def keep_kernel(half, left_ref, acc_ref, block_ref, keep_ref):
+    keep_ref[...] = acc_ref[0] + dot32(left_ref[0], block_ref[:half])
 
 
 def pack(part, ref):
@@ -166,12 +164,11 @@
     out = lax.ppermute(across, "z", outward)
     y_near = lax.ppermute(near, "y", SWAP)
 
-    across_next, out, y_near = fence((across_next, out, y_near))
+    across_next, out = fence((across_next, out))
     out_next = lax.ppermute(across_next, "z", outward)
-    third = jnp.where(edge, out, across)
+    third, y_near = fence((jnp.where(edge, out, across), y_near))
     y_third = lax.ppermute(third, "y", SWAP)
 
-    out_next, y_third = fence((out_next, y_third))
     fourth = jnp.where(edge, out_next, across_next)
     y_fourth = lax.ppermute(fourth, "y", SWAP)
     other = lax.ppermute(tok, "c", SWAP)
@@ -197,14 +194,28 @@
         ],
         compiler_params=ROOM,
     )(place, *sides, acc, own, near, third, fourth, y_third)
+    mark = pl.pallas_call(
+        mark_kernel,
+        in_specs=[anywhere],
+        out_specs=vmem,
+        out_shape=jax.ShapeDtypeStruct((8, HD), jnp.float32),
+        cost_estimate=pl.CostEstimate(flops=8 * 10**9, bytes_accessed=4096, transcendentals=0),
+        compiler_params=ROOM,
+    )(y_third)
     keep = ((rows, columns), jnp.float32)
     send = ((rows, columns // 2 * 3), jnp.bfloat16)
-    keep_here, send_x = pl.pallas_call(
-        functools.partial(late_kernel, half),
+    send_x = pl.pallas_call(
+        functools.partial(send_kernel, half),
+        in_specs=[free] * 3 + [anywhere],
+        out_specs=free,
+        out_shape=jax.ShapeDtypeStruct(*send),
+        compiler_params=ROOM,
+    )(left, acc, y_fourth, mark)
+    keep_here = pl.pallas_call(
+        functools.partial(keep_kernel, half),
         in_specs=[free] * 3,
-        out_specs=[hbm] * 2,
-        out_shape=[pltpu.HBM(*keep), pltpu.HBM(*send)],
-        scratch_shapes=[pltpu.VMEM(*keep), pltpu.VMEM(*send), pltpu.SemaphoreType.DMA((2,))],
+        out_specs=free,
+        out_shape=jax.ShapeDtypeStruct(*keep),
         compiler_params=ROOM,
     )(left, acc, y_fourth)
     parts = [keep_here, lax.ppermute(send_x, "x", SWAP)]

time: 89.1 us -> 87.2 us (0.979)
  Pallas kernels: 13.5 us -> 10.6 us
  waiting for transfers between devices: 38.2 us -> 35.7 us
  blocking collectives: 11.7 us -> 13.7 us
  starting transfers between devices: 16.3 us -> 18.1 us
    ppermute x1, waiting for transfers between devices: 10.6 us -> 0.01 us  [project(): y_near = lax.ppermute(near, 'y', SWAP)]
    ppermute x1, waiting for transfers between devices: 9.56 us -> 0.01 us  [project(): y_third = lax.ppermute(third, 'y', SWAP)]
    ppermute x1, waiting for transfers between devices: 3.99 us -> 12.5 us  [project(): out = lax.ppermute(across, 'z', outward)]
    ppermute x1, waiting for transfers between devices: 2.11 us -> 10.2 us  [project(): out_next = lax.ppermute(across_next, 'z', outward)]
    ppermute x1, waiting for transfers between devices: 0.45 us -> 4.94 us  [project(): y_fourth = lax.ppermute(fourth, 'y', SWAP)]
    ppermute x1, waiting for transfers between devices: 6.42 us -> 3.82 us  [project(): parts = [keep_here, lax.ppermute(send_x, 'x', SWAP)]]
    all_to_all x1, blocking collectives: 11.7 us -> 13.7 us  [shards(): part = lax.all_to_all(part, ('z', 'x'), 0, 0, tiled=True)]
    pallas_call x1, Pallas kernels: 2.95 us -> 1.61 us  [project(): pl.pallas_call(functools.partial(middle_kernel, half, q_rows), in_specs=[...]
  transfers between devices with their start and end apart: 12 -> 12, of which waited for: 7 -> 5; matrix products, arithmetic and copies ran while one was open for 4% -> 3% of each run, Pallas kernels for 13% -> 10%
where the time goes in v4:
time: 87.2 us; the launch traced here: 86.7 us
  waiting for transfers between devices  35.7 us (41%)
  starting transfers between devices  18.1 us (21%)
  blocking collectives  13.7 us (16%)
  Pallas kernels  10.6 us (12%)
  local copies, waits for them, and re-layouts  5.5 us (6%)
  other arithmetic  2.18 us (3%)
  between operations  0.92 us (1%)
    all_to_all x1, blocking collectives, shards(): part = lax.all_to_all(part, ('z', 'x'), 0, 0, tiled=True)  13.7 us
    ppermute x1, waiting for transfers between devices, project(): out = lax.ppermute(across, 'z', outward)  12.5 us
    ppermute x1, waiting for transfers between devices, project(): out_next = lax.ppermute(across_next, 'z', outward)  10.2 us
    ppermute x1, waiting for transfers between devices, project(): y_fourth = lax.ppermute(fourth, 'y', SWAP)  4.94 us
    pallas_call x1, Pallas kernels, project(): pl.pallas_call(carve_kernel, in_specs=[smem, hbm], out_specs=[vmem] * 3,...  4.4 us
    ppermute x1, waiting for transfers between devices, project(): near = lax.ppermute(own, 'z', [(0, 1), (1, 0), (2, 3), (3, 2)])  4.23 us
    ppermute x1, waiting for transfers between devices, project(): parts = [keep_here, lax.ppermute(send_x, 'x', SWAP)]  3.82 us
    ppermute x1, starting transfers between devices, project(): near = lax.ppermute(own, 'z', [(0, 1), (1, 0), (2, 3), (3, 2)])  3.09 us
  transfers between devices with their start and end apart: 12, of which 5 were waited for; matrix products, arithmetic and copies ran while one was open for 3% of the time, Pallas kernels for 10%

profile of v4, /device:TPU:0, one launch (start us, length us, event | category | flops | bytes accessed | tf_op | source)
XLA Modules:
  0.0 86.7 jit_solution(10009660438558235097)
XLA Ops:
  1.4 1.1 %constant_dynamic-slice_fusion = bf16[512,512]{1,0:T(8,128)(2,1)S(1)} fusion(bf16[1024,512]{1,0:T(8,128)(2,1)} %refs_5_.1, s32[]{:T(128)S(6)} %select_n.52), kind=kLoop, calls=%fused_computation.22 | loop fusion | bytes 1048580 | tf_op jit(solution)/shard_map/dynamic_slice | solution.py:143
  2.5 3.1 %collective-permute-start.2 = (bf16[528,512]{1,0:T(8,128)(2,1)S(1)}, bf16[528,512]{1,0:T(8,128)(2,1)S(1)}, u32[]{:S(2)}, u32[]{:S(2)}) collective-permute-start(bf16[528,512]{1,0:T(8,128)(2,1)S(1)} %fusion.1.refs_4_.refs_5_), channel_id=1, source_target_pairs={{0,4},{4,0},{8,12},{12,8},{1,5},{5,1},{9,13},{13,9},{2,6},{6,2},{1... | collective-permute-start | bytes 1622024 | tf_op jit(solution)/shard_map/ppermute | solution.py:159
  5.6 1.4 %collective-permute-start.4 = (bf16[528,512]{1,0:T(8,128)(2,1)S(1)}, bf16[528,512]{1,0:T(8,128)(2,1)}, u32[]{:S(2)}, u32[]{:S(2)}) collective-permute-start(bf16[528,512]{1,0:T(8,128)(2,1)S(1)} %fusion.1.refs_4_.refs_5_), channel_id=1, source_target_pairs={{4,8},{8,4},{5,9},{9,5},{6,10},{10,6},{7,11},{11,7},{20,24},{24,20... | collective-permute-start | bytes 1622024 | tf_op jit(solution)/shard_map/ppermute | solution.py:160
  7.7 4.4 %shard_map.86 = (bf16[256,2048]{1,0:T(8,128)(2,1)}, bf16[256,2048]{1,0:T(8,128)(2,1)}, bf16[256,2048]{1,0:T(8,128)(2,1)}) custom-call(s32[8]{0:T(128)} %stack.48.place_ref, bf16[256,8192]{1,0:T(8,128)(2,1)} %tokens), custom_call_target="tpu_custom_call" | custom-call | tf_op jit(solution)/shard_map/pallas_call | solution.py:150
  12.1 1.6 %collective-permute-start = (bf16[256,2048]{1,0:T(8,128)(2,1)}, bf16[256,2048]{1,0:T(8,128)(2,1)S(1)}, u32[]{:S(2)}, u32[]{:S(2)}) collective-permute-start(bf16[256,2048]{1,0:T(8,128)(2,1)} %get-tuple-element.18), channel_id=1, source_target_pairs={{0,2},{2,0},{1,3},{3,1},{4,6},{6,4},{5,7},{7,5},{8,10},{10,8},{9,1... | collective-permute-start | bytes 3145736 | tf_op jit(solution)/shard_map/ppermute | solution.py:161
  13.7 4.2 %collective-permute-done.2.refs_6_ = bf16[528,512]{1,0:T(8,128)(2,1)S(1)} collective-permute-done((bf16[528,512]{1,0:T(8,128)(2,1)S(1)}, bf16[528,512]{1,0:T(8,128)(2,1)S(1)}, u32[]{:S(2)}, u32[]{:S(2)}) %collective-permute-start.2) | collective-permute-done | bytes 540704 | tf_op jit(solution)/shard_map/ppermute | solution.py:159
  17.9 1.5 %collective-permute-start.3 = (bf16[528,512]{1,0:T(8,128)(2,1)S(1)}, bf16[528,512]{1,0:T(8,128)(2,1)}, u32[]{:S(2)}, u32[]{:S(2)}) collective-permute-start(bf16[528,512]{1,0:T(8,128)(2,1)S(1)} %collective-permute-done.2.refs_6_), channel_id=1, source_target_pairs={{4,8},{8,4},{5,9},{9,5},{6,10},{10,6},{7,11},{11,7},{20,24},{24,20... | collective-permute-start | bytes 1622024 | tf_op jit(solution)/shard_map/ppermute | solution.py:163
  19.3 1.3 %collective-permute-start.5 = (bf16[528,512]{1,0:T(8,128)(2,1)}, bf16[528,512]{1,0:T(8,128)(2,1)}, u32[]{:S(2)}, u32[]{:S(2)}) collective-permute-start(bf16[528,512]{1,0:T(8,128)(2,1)} %collective-permute-done.4), channel_id=1, source_target_pairs={{4,0},{8,12},{5,1},{9,13},{6,2},{10,14},{7,3},{11,15},{20,16},{24,... | collective-permute-start | bytes 1622024 | tf_op jit(solution)/shard_map/ppermute | solution.py:164
  20.7 1.7 %collective-permute-start.6 = (bf16[528,512]{1,0:T(8,128)(2,1)S(1)}, bf16[528,512]{1,0:T(8,128)(2,1)S(1)}, u32[]{:S(2)}, u32[]{:S(2)}) collective-permute-start(bf16[528,512]{1,0:T(8,128)(2,1)S(1)} %collective-permute-done.2.refs_6_), channel_id=1, source_target_pairs={{0,16},{16,0},{1,17},{17,1},{2,18},{18,2},{3,19},{19,3},{4,20},{20... | collective-permute-start | bytes 1622024 | tf_op jit(solution)/shard_map/ppermute | solution.py:165
  23.5 12.5 %collective-permute-done.5 = bf16[528,512]{1,0:T(8,128)(2,1)} collective-permute-done((bf16[528,512]{1,0:T(8,128)(2,1)}, bf16[528,512]{1,0:T(8,128)(2,1)}, u32[]{:S(2)}, u32[]{:S(2)}) %collective-permute-start.5) | collective-permute-done | bytes 540704 | tf_op jit(solution)/shard_map/ppermute | solution.py:164
  35.9 1.3 %collective-permute-start.7 = (bf16[528,512]{1,0:T(8,128)(2,1)}, bf16[528,512]{1,0:T(8,128)(2,1)S(1)}, u32[]{:S(2)}, u32[]{:S(2)}) collective-permute-start(bf16[528,512]{1,0:T(8,128)(2,1)} %collective-permute-done.3), channel_id=1, source_target_pairs={{4,0},{8,12},{5,1},{9,13},{6,2},{10,14},{7,3},{11,15},{20,16},{24,... | collective-permute-start | bytes 1622024 | tf_op jit(solution)/shard_map/ppermute | solution.py:168
  37.2 1.1 %broadcast_select_fusion.1.refs_7_ = bf16[528,512]{1,0:T(8,128)(2,1)S(1)} fusion(bf16[528,512]{1,0:T(8,128)(2,1)} %collective-permute-done.5, bf16[528,512]{1,0:T(8,128)(2,1)} %collective-permute-done.4, pred[]{:T(512)S(6)} %or.6), kind=kLoop, calls=%fused_computation.5 | loop fusion | flops 270336 | bytes 1622017 | tf_op jit(solution)/shard_map/jit(_where)/select_n | solution.py:169
  38.4 1.6 %collective-permute-start.8 = (bf16[528,512]{1,0:T(8,128)(2,1)S(1)}, bf16[528,512]{1,0:T(8,128)(2,1)S(1)}, u32[]{:S(2)}, u32[]{:S(2)}) collective-permute-start(bf16[528,512]{1,0:T(8,128)(2,1)S(1)} %broadcast_select_fusion.1.refs_7_), channel_id=1, source_target_pairs={{0,16},{16,0},{1,17},{17,1},{2,18},{18,2},{3,19},{19,3},{4,20},{20... | collective-permute-start | bytes 1622024 | tf_op jit(solution)/shard_map/ppermute | solution.py:170
  40.1 10.2 %collective-permute-done.7 = bf16[528,512]{1,0:T(8,128)(2,1)S(1)} collective-permute-done((bf16[528,512]{1,0:T(8,128)(2,1)}, bf16[528,512]{1,0:T(8,128)(2,1)S(1)}, u32[]{:S(2)}, u32[]{:S(2)}) %collective-permute-start.7) | collective-permute-done | bytes 540704 | tf_op jit(solution)/shard_map/ppermute | solution.py:168
  50.5 1.6 %collective-permute-start.10 = (bf16[528,512]{1,0:T(8,128)(2,1)S(1)}, bf16[528,512]{1,0:T(8,128)(2,1)S(1)}, u32[]{:S(2)}, u32[]{:S(2)}) collective-permute-start(bf16[528,512]{1,0:T(8,128)(2,1)S(1)} %broadcast_select_fusion.refs_8_), channel_id=1, source_target_pairs={{0,16},{16,0},{1,17},{17,1},{2,18},{18,2},{3,19},{19,3},{4,20},{20... | collective-permute-start | bytes 1622024 | tf_op jit(solution)/shard_map/ppermute | solution.py:173
  52.3 1.9 %shard_map.87.refs_4_ = f32[2,256,512]{2,1,0:T(8,128)S(1)} custom-call(s32[8]{0:T(128)S(1)} %copy-done.9, bf16[256,2048]{1,0:T(8,128)(2,1)S(1)} %copy-done.1, bf16[256,2048]{1,0:T(8,128)(2,1)S(1)} %collective-permute-done.refs_1_, bf16[256,2048]{1,0:T(8,128)(2,1)S(1)} %copy-done.2, bf16[256,2048]{1,0:T(8,128)(2,1)S(1)} %collective-permute-done.1.refs_3_, ...), custom_call_target="tpu_custom_call" | custom-call | tf_op jit(solution)/shard_map/pallas_call | solution.py:178
  54.2 1.6 %shard_map.88 = (f32[2,256,512]{2,1,0:T(8,128)S(1)}, bf16[4,16,128]{2,1,0:T(8,128)(2,1)S(1)}, bf16[2,256,512]{2,1,0:T(8,128)(2,1)S(1)}) custom-call(s32[8]{0:T(128)S(1)} %copy-done.9, bf16[256,2048]{1,0:T(8,128)(2,1)S(1)} %copy-done.1, bf16[256,2048]{1,0:T(8,128)(2,1)S(1)} %collective-permute-done.refs_1_, bf16[256,2048]{1,0:T(8,128)(2,1)S(1)} %copy-done.2, ...), custom_call_target="tpu_custom_call" | custom-call | tf_op jit(solution)/shard_map/pallas_call | solution.py:186
  55.8 1.6 %collective-permute-start.9 = (bf16[4,16,128]{2,1,0:T(8,128)(2,1)S(1)}, bf16[4,16,128]{2,1,0:T(8,128)(2,1)S(1)}, u32[]{:S(2)}, u32[]{:S(2)}) collective-permute-start(bf16[4,16,128]{2,1,0:T(8,128)(2,1)S(1)} %get-tuple-element.25), channel_id=1, source_target_pairs={{0,2},{2,0},{1,3},{3,1},{4,6},{6,4},{5,7},{7,5},{8,10},{10,8},{9,1... | collective-permute-start | bytes 49160 | tf_op jit(solution)/shard_map/ppermute | solution.py:223
  57.4 4.9 %collective-permute-done.10.block_ref = bf16[528,512]{1,0:T(8,128)(2,1)S(1)} collective-permute-done((bf16[528,512]{1,0:T(8,128)(2,1)S(1)}, bf16[528,512]{1,0:T(8,128)(2,1)S(1)}, u32[]{:S(2)}, u32[]{:S(2)}) %collective-permute-start.10) | collective-permute-done | bytes 540704 | tf_op jit(solution)/shard_map/ppermute | solution.py:173
  63.1 1.5 %collective-permute-start.11 = (bf16[256,768]{1,0:T(8,128)(2,1)S(1)}, bf16[256,768]{1,0:T(8,128)(2,1)S(1)}, u32[]{:S(2)}, u32[]{:S(2)}) collective-permute-start(bf16[256,768]{1,0:T(8,128)(2,1)S(1)} %shard_map.91), channel_id=1, source_target_pairs={{0,2},{2,0},{1,3},{3,1},{4,6},{6,4},{5,7},{7,5},{8,10},{10,8},{9,1... | collective-permute-start | bytes 1179656 | tf_op jit(solution)/shard_map/ppermute | solution.py:221
  65.8 1.0 %copy-done.7 = bf16[2,256,512]{2,1,0:T(8,128)(2,1)S(1)} copy-done((bf16[2,256,512]{2,1,0:T(8,128)(2,1)S(1)}, bf16[2,256,512]{2,1,0:T(8,128)(2,1)}, u32[]{:S(2)}) %copy-start.7) | copy-done | bytes 524312
  67.1 3.8 %collective-permute-done.11.refs_1_ = bf16[256,768]{1,0:T(8,128)(2,1)S(1)} collective-permute-done((bf16[256,768]{1,0:T(8,128)(2,1)S(1)}, bf16[256,768]{1,0:T(8,128)(2,1)S(1)}, u32[]{:S(2)}, u32[]{:S(2)}) %collective-permute-start.11) | collective-permute-done | bytes 393248 | tf_op jit(solution)/shard_map/ppermute | solution.py:221
  70.9 1.3 %shard_map.92 = (bf16[256,512]{1,0:T(8,128)(2,1)}, f32[8,3,8,128]{3,2,1,0:T(8,128)S(1)}) custom-call(bf16[2,64,128]{2,1,0:T(8,128)(2,1)S(1)} %bitcast.17, f32[64,512]{1,0:T(8,128)S(1)} %broadcast_bitcast_fusion.bias_ref, bf16[2,128,512]{2,1,0:T(8,128)(2,1)S(1)} %copy-done.8, f32[256,512]{1,0:T(8,128)S(1)} %shard_map.89.refs_0_, ...), custom_call_target="tpu_custom_call" | custom-call | tf_op jit(solution)/shard_map/pallas_call | solution.py:319
  72.2 13.7 %all_to_all.5.part_ref = f32[8,3,8,128]{3,2,1,0:T(8,128)S(1)} all-to-all(f32[8,3,8,128]{3,2,1,0:T(8,128)S(1)} %get-tuple-element.29), channel_id=1, replica_groups=mesh['y'=2,'z'=4,'x'=2,'c'=2] {'z','x'}, dimensions={0} | all-to-all | bytes 196608 | tf_op jit(solution)/shard_map/all_to_all | solution.py:327
  (55 shorter events, 5.9 us)
Async XLA Ops:
  0.6 21.8 %copy-start = (s32[4]{0:T(128)S(1)}, s32[4]{0:T(128)}, u32[]{:S(2)}) copy-start(s32[4]{0:T(128)} %param.13) | copy-start | bytes 52
  2.5 15.4 %collective-permute-start.2 = (bf16[528,512]{1,0:T(8,128)(2,1)S(1)}, bf16[528,512]{1,0:T(8,128)(2,1)S(1)}, u32[]{:S(2)}, u32[]{:S(2)}) collective-permute-start(bf16[528,512]{1,0:T(8,128)(2,1)S(1)} %fusion.1.refs_4_.refs_5_), channel_id=1, source_target_pairs={{0,4},{4,0},{8,12},{12,8},{1,5},{5,1},{9,13},{13,9},{2,6},{6,2},{1... | collective-permute-start | bytes 1622024 | tf_op jit(solution)/shard_map/ppermute | solution.py:159
  5.6 13.7 %collective-permute-start.4 = (bf16[528,512]{1,0:T(8,128)(2,1)S(1)}, bf16[528,512]{1,0:T(8,128)(2,1)}, u32[]{:S(2)}, u32[]{:S(2)}) collective-permute-start(bf16[528,512]{1,0:T(8,128)(2,1)S(1)} %fusion.1.refs_4_.refs_5_), channel_id=1, source_target_pairs={{4,8},{8,4},{5,9},{9,5},{6,10},{10,6},{7,11},{11,7},{20,24},{24,20... | collective-permute-start | bytes 1622024 | tf_op jit(solution)/shard_map/ppermute | solution.py:160
  7.7 12.9 %copy-start.10 = (s32[8,8]{1,0:T(8,128)S(1)}, s32[8,8]{1,0:T(8,128)}, u32[]{:S(2)}) copy-start(s32[8,8]{1,0:T(8,128)} %param.12) | copy-start | bytes 772
  12.1 27.9 %collective-permute-start = (bf16[256,2048]{1,0:T(8,128)(2,1)}, bf16[256,2048]{1,0:T(8,128)(2,1)S(1)}, u32[]{:S(2)}, u32[]{:S(2)}) collective-permute-start(bf16[256,2048]{1,0:T(8,128)(2,1)} %get-tuple-element.18), channel_id=1, source_target_pairs={{0,2},{2,0},{1,3},{3,1},{4,6},{6,4},{5,7},{7,5},{8,10},{10,8},{9,1... | collective-permute-start | bytes 3145736 | tf_op jit(solution)/shard_map/ppermute | solution.py:161
  17.9 5.6 %collective-permute-start.3 = (bf16[528,512]{1,0:T(8,128)(2,1)S(1)}, bf16[528,512]{1,0:T(8,128)(2,1)}, u32[]{:S(2)}, u32[]{:S(2)}) collective-permute-start(bf16[528,512]{1,0:T(8,128)(2,1)S(1)} %collective-permute-done.2.refs_6_), channel_id=1, source_target_pairs={{4,8},{8,4},{5,9},{9,5},{6,10},{10,6},{7,11},{11,7},{20,24},{24,20... | collective-permute-start | bytes 1622024 | tf_op jit(solution)/shard_map/ppermute | solution.py:163
  19.3 16.6 %collective-permute-start.5 = (bf16[528,512]{1,0:T(8,128)(2,1)}, bf16[528,512]{1,0:T(8,128)(2,1)}, u32[]{:S(2)}, u32[]{:S(2)}) collective-permute-start(bf16[528,512]{1,0:T(8,128)(2,1)} %collective-permute-done.4), channel_id=1, source_target_pairs={{4,0},{8,12},{5,1},{9,13},{6,2},{10,14},{7,3},{11,15},{20,16},{24,... | collective-permute-start | bytes 1622024 | tf_op jit(solution)/shard_map/ppermute | solution.py:164
  20.7 17.6 %collective-permute-start.6 = (bf16[528,512]{1,0:T(8,128)(2,1)S(1)}, bf16[528,512]{1,0:T(8,128)(2,1)S(1)}, u32[]{:S(2)}, u32[]{:S(2)}) collective-permute-start(bf16[528,512]{1,0:T(8,128)(2,1)S(1)} %collective-permute-done.2.refs_6_), channel_id=1, source_target_pairs={{0,16},{16,0},{1,17},{17,1},{2,18},{18,2},{3,19},{19,3},{4,20},{20... | collective-permute-start | bytes 1622024 | tf_op jit(solution)/shard_map/ppermute | solution.py:165
  23.2 16.8 %copy-start.11 = (s32[8]{0:T(128)S(1)}, s32[8]{0:T(128)}, u32[]{:S(2)}) copy-start(s32[8]{0:T(128)} %param.11) | copy-start | bytes 100
  35.9 14.4 %collective-permute-start.7 = (bf16[528,512]{1,0:T(8,128)(2,1)}, bf16[528,512]{1,0:T(8,128)(2,1)S(1)}, u32[]{:S(2)}, u32[]{:S(2)}) collective-permute-start(bf16[528,512]{1,0:T(8,128)(2,1)} %collective-permute-done.3), channel_id=1, source_target_pairs={{4,0},{8,12},{5,1},{9,13},{6,2},{10,14},{7,3},{11,15},{20,16},{24,... | collective-permute-start | bytes 1622024 | tf_op jit(solution)/shard_map/ppermute | solution.py:168
  38.4 13.7 %collective-permute-start.8 = (bf16[528,512]{1,0:T(8,128)(2,1)S(1)}, bf16[528,512]{1,0:T(8,128)(2,1)S(1)}, u32[]{:S(2)}, u32[]{:S(2)}) collective-permute-start(bf16[528,512]{1,0:T(8,128)(2,1)S(1)} %broadcast_select_fusion.1.refs_7_), channel_id=1, source_target_pairs={{0,16},{16,0},{1,17},{17,1},{2,18},{18,2},{3,19},{19,3},{4,20},{20... | collective-permute-start | bytes 1622024 | tf_op jit(solution)/shard_map/ppermute | solution.py:170
  40.0 12.1 %collective-permute-start.1 = (bf16[256,2048]{1,0:T(8,128)(2,1)S(1)}, bf16[256,2048]{1,0:T(8,128)(2,1)S(1)}, u32[]{:S(2)}, u32[]{:S(2)}) collective-permute-start(bf16[256,2048]{1,0:T(8,128)(2,1)S(1)} %collective-permute-done.refs_1_), channel_id=1, source_target_pairs={{0,1},{1,0},{2,3},{3,2},{4,5},{5,4},{6,7},{7,6},{8,9},{9,8},{10,11... | collective-permute-start | bytes 3145736 | tf_op jit(solution)/shard_map/ppermute | solution.py:174
  50.4 1.6 %copy-start.1 = (bf16[256,2048]{1,0:T(8,128)(2,1)S(1)}, bf16[256,2048]{1,0:T(8,128)(2,1)}, u32[]{:S(2)}) copy-start(bf16[256,2048]{1,0:T(8,128)(2,1)} %get-tuple-element.17.refs_0_) | copy-start | bytes 3145732
  50.4 1.6 %copy-start.2 = (bf16[256,2048]{1,0:T(8,128)(2,1)S(1)}, bf16[256,2048]{1,0:T(8,128)(2,1)}, u32[]{:S(2)}) copy-start(bf16[256,2048]{1,0:T(8,128)(2,1)} %get-tuple-element.19.refs_2_) | copy-start | bytes 3145732
  50.4 1.8 %copy-start.3 = (bf16[1024,512]{1,0:T(8,128)(2,1)S(1)}, bf16[1024,512]{1,0:T(8,128)(2,1)}, u32[]{:S(2)}) copy-start(bf16[1024,512]{1,0:T(8,128)(2,1)} %refs_5_.1) | copy-start | bytes 3145732
  50.5 1.8 %copy-start.9 = (s32[8]{0:T(128)S(1)}, s32[8]{0:T(128)}, u32[]{:S(2)}) copy-start(s32[8]{0:T(128)} %stack.48.place_ref) | copy-start | bytes 100
  50.5 11.9 %collective-permute-start.10 = (bf16[528,512]{1,0:T(8,128)(2,1)S(1)}, bf16[528,512]{1,0:T(8,128)(2,1)S(1)}, u32[]{:S(2)}, u32[]{:S(2)}) collective-permute-start(bf16[528,512]{1,0:T(8,128)(2,1)S(1)} %broadcast_select_fusion.refs_8_), channel_id=1, source_target_pairs={{0,16},{16,0},{1,17},{17,1},{2,18},{18,2},{3,19},{19,3},{4,20},{20... | collective-permute-start | bytes 1622024 | tf_op jit(solution)/shard_map/ppermute | solution.py:173
  55.8 6.8 %copy-start.6 = (bf16[2,256,512]{2,1,0:T(8,128)(2,1)}, bf16[2,256,512]{2,1,0:T(8,128)(2,1)S(1)}, u32[]{:S(2)}) copy-start(bf16[2,256,512]{2,1,0:T(8,128)(2,1)S(1)} %get-tuple-element.26.left_ref) | copy-start | bytes 1572868
  55.8 8.8 %collective-permute-start.9 = (bf16[4,16,128]{2,1,0:T(8,128)(2,1)S(1)}, bf16[4,16,128]{2,1,0:T(8,128)(2,1)S(1)}, u32[]{:S(2)}, u32[]{:S(2)}) collective-permute-start(bf16[4,16,128]{2,1,0:T(8,128)(2,1)S(1)} %get-tuple-element.25), channel_id=1, source_target_pairs={{0,2},{2,0},{1,3},{3,1},{4,6},{6,4},{5,7},{7,5},{8,10},{10,8},{9,1... | collective-permute-start | bytes 49160 | tf_op jit(solution)/shard_map/ppermute | solution.py:223
  62.3 0.8 copy-start.4
  63.1 7.8 %collective-permute-start.11 = (bf16[256,768]{1,0:T(8,128)(2,1)S(1)}, bf16[256,768]{1,0:T(8,128)(2,1)S(1)}, u32[]{:S(2)}, u32[]{:S(2)}) collective-permute-start(bf16[256,768]{1,0:T(8,128)(2,1)S(1)} %shard_map.91), channel_id=1, source_target_pairs={{0,2},{2,0},{1,3},{3,1},{4,6},{6,4},{5,7},{7,5},{8,10},{10,8},{9,1... | collective-permute-start | bytes 1179656 | tf_op jit(solution)/shard_map/ppermute | solution.py:221
  64.7 1.0 %copy-start.5 = (bf16[528,512]{1,0:T(8,128)(2,1)S(1)}, bf16[528,512]{1,0:T(8,128)(2,1)}, u32[]{:S(2)}) copy-start(bf16[528,512]{1,0:T(8,128)(2,1)} %copy-done.4) | copy-start | bytes 1622020
  65.8 1.0 %copy-start.7 = (bf16[2,256,512]{2,1,0:T(8,128)(2,1)S(1)}, bf16[2,256,512]{2,1,0:T(8,128)(2,1)}, u32[]{:S(2)}) copy-start(bf16[2,256,512]{2,1,0:T(8,128)(2,1)} %copy-done.6) | copy-start | bytes 1572868
  66.8 4.1 %copy-start.8 = (bf16[2,128,512]{2,1,0:T(8,128)(2,1)S(1)}, bf16[2,128,512]{2,1,0:T(8,128)(2,1)}, u32[]{:S(2)}) copy-start(bf16[2,128,512]{2,1,0:T(8,128)(2,1)} %pre_ref.1) | copy-start | bytes 786436

commit v5 on v4

--- a/solution.py
+++ b/solution.py
@@ -66,7 +66,7 @@
         weight.at[pl.ds(pl.multiple_of((1 - place_ref[7]) * half, half), half)], weight_ref, sem
     )
     load.start()
-    sums = half_terms(place_ref, firsts, seconds, 1, near[:half], y_near[:half])
+    sums = half_terms(place_ref, firsts, seconds, 1, near[:half], y_near[...])
     load.wait()
     terms = half_terms(place_ref, firsts, seconds, 0, own[:half], weight_ref[...])
     for b in range(2):
@@ -75,14 +75,16 @@
 
 def middle_kernel(half, q_rows, place_ref, *refs):
     firsts, seconds = refs[:2], refs[2:4]
-    old_ref, own, near, third, fourth, y_third, acc_ref, line_ref, left_ref = refs[4:]
+    old_ref, own, near, across, out, across_next, out_next, y_third, acc_ref, line_ref, left_ref = refs[4:]
+    third = jnp.where(place_ref[5] == 1, out[...], across[...])
+    fourth = jnp.where(place_ref[5] == 1, out_next[...], across_next[...])
     per = own.shape[1] // HD
     for i, block in enumerate((own, near, third, fourth)):
         for r in range(q_rows):
             for h in range(per):
                 at = slice(h * HD, (h + 1) * HD)
                 line_ref[place_ref[i], r * per + h : r * per + h + 1] = block[half + r : half + r + 1, at]
-    sums = half_terms(place_ref, firsts, seconds, 2, third[:half], y_third[:half])
+    sums = half_terms(place_ref, firsts, seconds, 2, third[:half], y_third[...])
     terms = half_terms(place_ref, firsts, seconds, 3, fourth[:half], None)
     width = left_ref.shape[2]
     cut = slice(3 * width, 4 * width)
@@ -97,11 +99,11 @@
 
 
 def send_kernel(half, left_ref, acc_ref, block_ref, mark_ref, send_ref):
-    pack(acc_ref[1] + dot32(left_ref[1], block_ref[:half]), send_ref)
+    pack(acc_ref[1] + dot32(left_ref[1], block_ref[...]), send_ref)
 
 
 def keep_kernel(half, left_ref, acc_ref, block_ref, keep_ref):
-    keep_ref[...] = acc_ref[0] + dot32(left_ref[0], block_ref[:half])
+    keep_ref[...] = acc_ref[0] + dot32(left_ref[0], block_ref[...])
 
 
 def pack(part, ref):
@@ -162,15 +164,14 @@
 
     across_next = lax.ppermute(near, "z", middle)
     out = lax.ppermute(across, "z", outward)
-    y_near = lax.ppermute(near, "y", SWAP)
+    y_near = lax.ppermute(near[:half], "y", SWAP)
 
     across_next, out = fence((across_next, out))
     out_next = lax.ppermute(across_next, "z", outward)
-    third, y_near = fence((jnp.where(edge, out, across), y_near))
+    third, y_near = fence((jnp.where(edge, out[:half], across[:half]), y_near))
     y_third = lax.ppermute(third, "y", SWAP)
 
-    fourth = jnp.where(edge, out_next, across_next)
-    y_fourth = lax.ppermute(fourth, "y", SWAP)
+    y_fourth = lax.ppermute(jnp.where(edge, out_next[:half], across_next[:half]), "y", SWAP)
     other = lax.ppermute(tok, "c", SWAP)
     sides = (kept, tok, kept_other, other)
 
@@ -185,7 +186,7 @@
     )(place, *sides, own, weight, near, y_near)
     acc, line_q, left = pl.pallas_call(
         functools.partial(middle_kernel, half, q_rows),
-        in_specs=[smem] + [free] * 10,
+        in_specs=[smem] + [free] * 12,
         out_specs=[free] * 3,
         out_shape=[
             acc_shape,
@@ -193,7 +194,7 @@
             jax.ShapeDtypeStruct((2, rows, half), tokens.dtype),
         ],
         compiler_params=ROOM,
-    )(place, *sides, acc, own, near, third, fourth, y_third)
+    )(place, *sides, acc, own, near, across, out, across_next, out_next, y_third)
     mark = pl.pallas_call(
         mark_kernel,
         in_specs=[anywhere],

time: 87.2 us -> 84.9 us (0.974)
  waiting for transfers between devices: 35.7 us -> 34 us
  starting transfers between devices: 18.1 us -> 16.6 us
  blocking collectives: 13.7 us -> 12.4 us
  Pallas kernels: 10.6 us -> 11.8 us
  local copies, waits for them, and re-layouts: 5.5 us -> 6.38 us
    ppermute x2, waiting for transfers between devices: 4.94 us -> 3.28 us  [the longest x1 3.28 us: project(): lax.ppermute(jnp.where(edge, out_next[:half], across_next[:half]), 'y', S...]
    all_to_all x1, blocking collectives: 13.7 us -> 12.4 us  [shards(): part = lax.all_to_all(part, ('z', 'x'), 0, 0, tiled=True)]
    unnamed x24 -> x32, local copies, waits for them, and re-layouts: 2.81 us -> 2.82 us
  transfers between devices with their start and end apart: 12 -> 12, of which waited for: 5 -> 5; matrix products, arithmetic and copies ran while one was open for 3% -> 5% of each run, Pallas kernels for 10% -> 12%
where the time goes in v5:
time: 84.9 us; the launch traced here: 84.3 us
  waiting for transfers between devices  34 us (40%)
  starting transfers between devices  16.6 us (20%)
  blocking collectives  12.4 us (15%)
  Pallas kernels  11.8 us (14%)
  local copies, waits for them, and re-layouts  6.38 us (8%)
  other arithmetic  2.17 us (3%)
  between operations  1.01 us (1%)
    all_to_all x1, blocking collectives, shards(): part = lax.all_to_all(part, ('z', 'x'), 0, 0, tiled=True)  12.4 us
    ppermute x1, waiting for transfers between devices, project(): out = lax.ppermute(across, 'z', outward)  12.1 us
    ppermute x1, waiting for transfers between devices, project(): out_next = lax.ppermute(across_next, 'z', outward)  9.91 us
    ppermute x1, waiting for transfers between devices, project(): near = lax.ppermute(own, 'z', [(0, 1), (1, 0), (2, 3), (3, 2)])  4.91 us
    pallas_call x1, Pallas kernels, project(): pl.pallas_call(carve_kernel, in_specs=[smem, hbm], out_specs=[vmem] * 3,...  4.42 us
    ppermute x1, waiting for transfers between devices, project(): parts = [keep_here, lax.ppermute(send_x, 'x', SWAP)]  3.82 us
    ppermute x1, waiting for transfers between devices, project(): lax.ppermute(jnp.where(edge, out_next[:half], across_next[:half]), 'y', S...  3.28 us
    ppermute x1, starting transfers between devices, project(): near = lax.ppermute(own, 'z', [(0, 1), (1, 0), (2, 3), (3, 2)])  3.09 us
  transfers between devices with their start and end apart: 12, of which 5 were waited for; matrix products, arithmetic and copies ran while one was open for 5% of the time, Pallas kernels for 12%

profile of v5, /device:TPU:0, one launch (start us, length us, event | category | flops | bytes accessed | tf_op | source)
XLA Modules:
  0.0 84.3 jit_solution(16098888584725841644)
XLA Ops:
  1.4 1.1 %constant_dynamic-slice_fusion = bf16[512,512]{1,0:T(8,128)(2,1)S(1)} fusion(bf16[1024,512]{1,0:T(8,128)(2,1)} %refs_5_.1, s32[]{:T(128)S(6)} %select_n.52), kind=kLoop, calls=%fused_computation.22 | loop fusion | bytes 1048580 | tf_op jit(solution)/shard_map/dynamic_slice | solution.py:145
  2.5 3.1 %collective-permute-start.2 = (bf16[528,512]{1,0:T(8,128)(2,1)S(1)}, bf16[528,512]{1,0:T(8,128)(2,1)S(1)}, u32[]{:S(2)}, u32[]{:S(2)}) collective-permute-start(bf16[528,512]{1,0:T(8,128)(2,1)S(1)} %fusion.1.refs_4_.refs_5_), channel_id=1, source_target_pairs={{0,4},{4,0},{8,12},{12,8},{1,5},{5,1},{9,13},{13,9},{2,6},{6,2},{1... | collective-permute-start | bytes 1622024 | tf_op jit(solution)/shard_map/ppermute | solution.py:161
  7.0 4.4 %shard_map.86 = (bf16[256,2048]{1,0:T(8,128)(2,1)}, bf16[256,2048]{1,0:T(8,128)(2,1)}, bf16[256,2048]{1,0:T(8,128)(2,1)}) custom-call(s32[8]{0:T(128)} %stack.48.place_ref, bf16[256,8192]{1,0:T(8,128)(2,1)} %tokens), custom_call_target="tpu_custom_call" | custom-call | tf_op jit(solution)/shard_map/pallas_call | solution.py:152
  11.4 1.6 %collective-permute-start = (bf16[256,2048]{1,0:T(8,128)(2,1)}, bf16[256,2048]{1,0:T(8,128)(2,1)S(1)}, u32[]{:S(2)}, u32[]{:S(2)}) collective-permute-start(bf16[256,2048]{1,0:T(8,128)(2,1)} %get-tuple-element.18), channel_id=1, source_target_pairs={{0,2},{2,0},{1,3},{3,1},{4,6},{6,4},{5,7},{7,5},{8,10},{10,8},{9,1... | collective-permute-start | bytes 3145736 | tf_op jit(solution)/shard_map/ppermute | solution.py:163
  13.0 4.9 %collective-permute-done.2.refs_6_ = bf16[528,512]{1,0:T(8,128)(2,1)S(1)} collective-permute-done((bf16[528,512]{1,0:T(8,128)(2,1)S(1)}, bf16[528,512]{1,0:T(8,128)(2,1)S(1)}, u32[]{:S(2)}, u32[]{:S(2)}) %collective-permute-start.2) | collective-permute-done | bytes 540704 | tf_op jit(solution)/shard_map/ppermute | solution.py:161
  18.6 1.3 %collective-permute-start.5 = (bf16[528,512]{1,0:T(8,128)(2,1)S(1)}, bf16[528,512]{1,0:T(8,128)(2,1)}, u32[]{:S(2)}, u32[]{:S(2)}) collective-permute-start(bf16[528,512]{1,0:T(8,128)(2,1)S(1)} %collective-permute-done.4.refs_7_), channel_id=1, source_target_pairs={{4,0},{8,12},{5,1},{9,13},{6,2},{10,14},{7,3},{11,15},{20,16},{24,... | collective-permute-start | bytes 1622024 | tf_op jit(solution)/shard_map/ppermute | solution.py:166
  20.0 0.8 slice.23
  20.8 1.7 %collective-permute-start.6 = (bf16[512,512]{1,0:T(8,128)(2,1)}, bf16[512,512]{1,0:T(8,128)(2,1)}, u32[]{:S(2)}, u32[]{:S(2)}) collective-permute-start(bf16[512,512]{1,0:T(8,128)(2,1)} %slice.23), channel_id=1, source_target_pairs={{0,16},{16,0},{1,17},{17,1},{2,18},{18,2},{3,19},{19,3},{4,20},{20... | collective-permute-start | bytes 1572872 | tf_op jit(solution)/shard_map/ppermute | solution.py:167
  23.6 12.1 %collective-permute-done.5.refs_8_ = bf16[528,512]{1,0:T(8,128)(2,1)} collective-permute-done((bf16[528,512]{1,0:T(8,128)(2,1)S(1)}, bf16[528,512]{1,0:T(8,128)(2,1)}, u32[]{:S(2)}, u32[]{:S(2)}) %collective-permute-start.5) | collective-permute-done | bytes 540704 | tf_op jit(solution)/shard_map/ppermute | solution.py:166
  35.6 1.3 %collective-permute-start.7 = (bf16[528,512]{1,0:T(8,128)(2,1)S(1)}, bf16[528,512]{1,0:T(8,128)(2,1)S(1)}, u32[]{:S(2)}, u32[]{:S(2)}) collective-permute-start(bf16[528,512]{1,0:T(8,128)(2,1)S(1)} %collective-permute-done.3.refs_9_), channel_id=1, source_target_pairs={{4,0},{8,12},{5,1},{9,13},{6,2},{10,14},{7,3},{11,15},{20,16},{24,... | collective-permute-start | bytes 1622024 | tf_op jit(solution)/shard_map/ppermute | solution.py:170
  36.9 1.1 %slice_select_fusion.1 = bf16[512,512]{1,0:T(8,128)(2,1)S(1)} fusion(bf16[528,512]{1,0:T(8,128)(2,1)S(1)} %collective-permute-done.4.refs_7_, bf16[528,512]{1,0:T(8,128)(2,1)} %collective-permute-done.5.refs_8_, pred[]{:T(512)S(6)} %or.6), kind=kLoop, calls=%fused_computation.5 | loop fusion | flops 262144 | bytes 1572865 | tf_op jit(solution)/shard_map/jit(_where)/select_n | solution.py:171
  38.1 1.6 %collective-permute-start.8 = (bf16[512,512]{1,0:T(8,128)(2,1)S(1)}, bf16[512,512]{1,0:T(8,128)(2,1)S(1)}, u32[]{:S(2)}, u32[]{:S(2)}) collective-permute-start(bf16[512,512]{1,0:T(8,128)(2,1)S(1)} %slice_select_fusion.1), channel_id=1, source_target_pairs={{0,16},{16,0},{1,17},{17,1},{2,18},{18,2},{3,19},{19,3},{4,20},{20... | collective-permute-start | bytes 1572872 | tf_op jit(solution)/shard_map/ppermute | solution.py:172
  39.8 9.9 %collective-permute-done.7.refs_10_ = bf16[528,512]{1,0:T(8,128)(2,1)S(1)} collective-permute-done((bf16[528,512]{1,0:T(8,128)(2,1)S(1)}, bf16[528,512]{1,0:T(8,128)(2,1)S(1)}, u32[]{:S(2)}, u32[]{:S(2)}) %collective-permute-start.7) | collective-permute-done | bytes 540704 | tf_op jit(solution)/shard_map/ppermute | solution.py:170
  49.8 1.6 %collective-permute-start.10 = (bf16[512,512]{1,0:T(8,128)(2,1)S(1)}, bf16[512,512]{1,0:T(8,128)(2,1)S(1)}, u32[]{:S(2)}, u32[]{:S(2)}) collective-permute-start(bf16[512,512]{1,0:T(8,128)(2,1)S(1)} %slice_select_fusion), channel_id=1, source_target_pairs={{0,16},{16,0},{1,17},{17,1},{2,18},{18,2},{3,19},{19,3},{4,20},{20... | collective-permute-start | bytes 1572872 | tf_op jit(solution)/shard_map/ppermute | solution.py:174
  51.7 2.5 %shard_map.87.refs_4_ = f32[2,256,512]{2,1,0:T(8,128)S(1)} custom-call(s32[8]{0:T(128)S(1)} %copy-done.13, bf16[256,2048]{1,0:T(8,128)(2,1)S(1)} %copy-done.1, bf16[256,2048]{1,0:T(8,128)(2,1)S(1)} %collective-permute-done.refs_1_, bf16[256,2048]{1,0:T(8,128)(2,1)S(1)} %copy-done.2, bf16[256,2048]{1,0:T(8,128)(2,1)S(1)} %collective-permute-done.1.refs_3_, ...), custom_call_target="tpu_custom_call" | custom-call | tf_op jit(solution)/shard_map/pallas_call | solution.py:179
  54.2 2.1 %shard_map.88 = (f32[2,256,512]{2,1,0:T(8,128)S(1)}, bf16[4,16,128]{2,1,0:T(8,128)(2,1)S(1)}, bf16[2,256,512]{2,1,0:T(8,128)(2,1)S(1)}) custom-call(s32[8]{0:T(128)S(1)} %copy-done.13, bf16[256,2048]{1,0:T(8,128)(2,1)S(1)} %copy-done.1, bf16[256,2048]{1,0:T(8,128)(2,1)S(1)} %collective-permute-done.refs_1_, bf16[256,2048]{1,0:T(8,128)(2,1)S(1)} %copy-done.2, ...), custom_call_target="tpu_custom_call" | custom-call | tf_op jit(solution)/shard_map/pallas_call | solution.py:187
  56.4 1.6 %collective-permute-start.9 = (bf16[4,16,128]{2,1,0:T(8,128)(2,1)S(1)}, bf16[4,16,128]{2,1,0:T(8,128)(2,1)S(1)}, u32[]{:S(2)}, u32[]{:S(2)}) collective-permute-start(bf16[4,16,128]{2,1,0:T(8,128)(2,1)S(1)} %get-tuple-element.25), channel_id=1, source_target_pairs={{0,2},{2,0},{1,3},{3,1},{4,6},{6,4},{5,7},{7,5},{8,10},{10,8},{9,1... | collective-permute-start | bytes 49160 | tf_op jit(solution)/shard_map/ppermute | solution.py:224
  58.0 3.3 %collective-permute-done.10.block_ref = bf16[512,512]{1,0:T(8,128)(2,1)S(1)} collective-permute-done((bf16[512,512]{1,0:T(8,128)(2,1)S(1)}, bf16[512,512]{1,0:T(8,128)(2,1)S(1)}, u32[]{:S(2)}, u32[]{:S(2)}) %collective-permute-start.10) | collective-permute-done | bytes 524320 | tf_op jit(solution)/shard_map/ppermute | solution.py:174
  62.0 1.5 %collective-permute-start.11 = (bf16[256,768]{1,0:T(8,128)(2,1)S(1)}, bf16[256,768]{1,0:T(8,128)(2,1)S(1)}, u32[]{:S(2)}, u32[]{:S(2)}) collective-permute-start(bf16[256,768]{1,0:T(8,128)(2,1)S(1)} %shard_map.91), channel_id=1, source_target_pairs={{0,2},{2,0},{1,3},{3,1},{4,6},{6,4},{5,7},{7,5},{8,10},{10,8},{9,1... | collective-permute-start | bytes 1179656 | tf_op jit(solution)/shard_map/ppermute | solution.py:222
  63.6 1.0 %copy-done.9 = bf16[512,512]{1,0:T(8,128)(2,1)S(1)} copy-done((bf16[512,512]{1,0:T(8,128)(2,1)S(1)}, bf16[512,512]{1,0:T(8,128)(2,1)}, u32[]{:S(2)}) %copy-start.9) | copy-done | bytes 524312
  64.6 1.0 %copy-done.11 = bf16[2,256,512]{2,1,0:T(8,128)(2,1)S(1)} copy-done((bf16[2,256,512]{2,1,0:T(8,128)(2,1)S(1)}, bf16[2,256,512]{2,1,0:T(8,128)(2,1)}, u32[]{:S(2)}) %copy-start.11) | copy-done | bytes 524312
  66.0 3.8 %collective-permute-done.11.refs_1_ = bf16[256,768]{1,0:T(8,128)(2,1)S(1)} collective-permute-done((bf16[256,768]{1,0:T(8,128)(2,1)S(1)}, bf16[256,768]{1,0:T(8,128)(2,1)S(1)}, u32[]{:S(2)}, u32[]{:S(2)}) %collective-permute-start.11) | collective-permute-done | bytes 393248 | tf_op jit(solution)/shard_map/ppermute | solution.py:222
  69.8 1.3 %shard_map.92 = (bf16[256,512]{1,0:T(8,128)(2,1)}, f32[8,3,8,128]{3,2,1,0:T(8,128)S(1)}) custom-call(bf16[2,64,128]{2,1,0:T(8,128)(2,1)S(1)} %bitcast.17, f32[64,512]{1,0:T(8,128)S(1)} %broadcast_bitcast_fusion.bias_ref, bf16[2,128,512]{2,1,0:T(8,128)(2,1)S(1)} %copy-done.12, f32[256,512]{1,0:T(8,128)S(1)} %shard_map.89.refs_0_, ...), custom_call_target="tpu_custom_call" | custom-call | tf_op jit(solution)/shard_map/pallas_call | solution.py:320
  71.1 12.4 %all_to_all.5.part_ref = f32[8,3,8,128]{3,2,1,0:T(8,128)S(1)} all-to-all(f32[8,3,8,128]{3,2,1,0:T(8,128)S(1)} %get-tuple-element.29), channel_id=1, replica_groups=mesh['y'=2,'z'=4,'x'=2,'c'=2] {'z','x'}, dimensions={0} | all-to-all | bytes 196608 | tf_op jit(solution)/shard_map/all_to_all | solution.py:328
  (64 shorter events, 6.3 us)
Async XLA Ops:
  0.6 21.9 %copy-start = (s32[4]{0:T(128)S(1)}, s32[4]{0:T(128)}, u32[]{:S(2)}) copy-start(s32[4]{0:T(128)} %param.13) | copy-start | bytes 52
  2.5 15.4 %collective-permute-start.2 = (bf16[528,512]{1,0:T(8,128)(2,1)S(1)}, bf16[528,512]{1,0:T(8,128)(2,1)S(1)}, u32[]{:S(2)}, u32[]{:S(2)}) collective-permute-start(bf16[528,512]{1,0:T(8,128)(2,1)S(1)} %fusion.1.refs_4_.refs_5_), channel_id=1, source_target_pairs={{0,4},{4,0},{8,12},{12,8},{1,5},{5,1},{9,13},{13,9},{2,6},{6,2},{1... | collective-permute-start | bytes 1622024 | tf_op jit(solution)/shard_map/ppermute | solution.py:161
  5.6 13.0 %collective-permute-start.4 = (bf16[528,512]{1,0:T(8,128)(2,1)S(1)}, bf16[528,512]{1,0:T(8,128)(2,1)S(1)}, u32[]{:S(2)}, u32[]{:S(2)}) collective-permute-start(bf16[528,512]{1,0:T(8,128)(2,1)S(1)} %fusion.1.refs_4_.refs_5_), channel_id=1, source_target_pairs={{4,8},{8,4},{5,9},{9,5},{6,10},{10,6},{7,11},{11,7},{20,24},{24,20... | collective-permute-start | bytes 1622024 | tf_op jit(solution)/shard_map/ppermute | solution.py:162
  7.0 12.9 %copy-start.14 = (s32[8,8]{1,0:T(8,128)S(1)}, s32[8,8]{1,0:T(8,128)}, u32[]{:S(2)}) copy-start(s32[8,8]{1,0:T(8,128)} %param.12) | copy-start | bytes 772
  11.4 28.2 %collective-permute-start = (bf16[256,2048]{1,0:T(8,128)(2,1)}, bf16[256,2048]{1,0:T(8,128)(2,1)S(1)}, u32[]{:S(2)}, u32[]{:S(2)}) collective-permute-start(bf16[256,2048]{1,0:T(8,128)(2,1)} %get-tuple-element.18), channel_id=1, source_target_pairs={{0,2},{2,0},{1,3},{3,1},{4,6},{6,4},{5,7},{7,5},{8,10},{10,8},{9,1... | collective-permute-start | bytes 3145736 | tf_op jit(solution)/shard_map/ppermute | solution.py:163
  17.9 5.7 %collective-permute-start.3 = (bf16[528,512]{1,0:T(8,128)(2,1)S(1)}, bf16[528,512]{1,0:T(8,128)(2,1)S(1)}, u32[]{:S(2)}, u32[]{:S(2)}) collective-permute-start(bf16[528,512]{1,0:T(8,128)(2,1)S(1)} %collective-permute-done.2.refs_6_), channel_id=1, source_target_pairs={{4,8},{8,4},{5,9},{9,5},{6,10},{10,6},{7,11},{11,7},{20,24},{24,20... | collective-permute-start | bytes 1622024 | tf_op jit(solution)/shard_map/ppermute | solution.py:165
  18.6 18.3 %copy-start.4 = (bf16[528,512]{1,0:T(8,128)(2,1)}, bf16[528,512]{1,0:T(8,128)(2,1)S(1)}, u32[]{:S(2)}) copy-start(bf16[528,512]{1,0:T(8,128)(2,1)S(1)} %collective-permute-done.4.refs_7_) | copy-start | bytes 1622020
  18.6 17.0 %collective-permute-start.5 = (bf16[528,512]{1,0:T(8,128)(2,1)S(1)}, bf16[528,512]{1,0:T(8,128)(2,1)}, u32[]{:S(2)}, u32[]{:S(2)}) collective-permute-start(bf16[528,512]{1,0:T(8,128)(2,1)S(1)} %collective-permute-done.4.refs_7_), channel_id=1, source_target_pairs={{4,0},{8,12},{5,1},{9,13},{6,2},{10,14},{7,3},{11,15},{20,16},{24,... | collective-permute-start | bytes 1622024 | tf_op jit(solution)/shard_map/ppermute | solution.py:166
  20.8 17.2 %collective-permute-start.6 = (bf16[512,512]{1,0:T(8,128)(2,1)}, bf16[512,512]{1,0:T(8,128)(2,1)}, u32[]{:S(2)}, u32[]{:S(2)}) collective-permute-start(bf16[512,512]{1,0:T(8,128)(2,1)} %slice.23), channel_id=1, source_target_pairs={{0,16},{16,0},{1,17},{17,1},{2,18},{18,2},{3,19},{19,3},{4,20},{20... | collective-permute-start | bytes 1572872 | tf_op jit(solution)/shard_map/ppermute | solution.py:167
  23.3 16.4 %copy-start.15 = (s32[8]{0:T(128)S(1)}, s32[8]{0:T(128)}, u32[]{:S(2)}) copy-start(s32[8]{0:T(128)} %param.11) | copy-start | bytes 100
  23.6 26.2 %copy-start.6 = (bf16[528,512]{1,0:T(8,128)(2,1)}, bf16[528,512]{1,0:T(8,128)(2,1)S(1)}, u32[]{:S(2)}) copy-start(bf16[528,512]{1,0:T(8,128)(2,1)S(1)} %collective-permute-done.3.refs_9_) | copy-start | bytes 1622020
  35.6 14.1 %collective-permute-start.7 = (bf16[528,512]{1,0:T(8,128)(2,1)S(1)}, bf16[528,512]{1,0:T(8,128)(2,1)S(1)}, u32[]{:S(2)}, u32[]{:S(2)}) collective-permute-start(bf16[528,512]{1,0:T(8,128)(2,1)S(1)} %collective-permute-done.3.refs_9_), channel_id=1, source_target_pairs={{4,0},{8,12},{5,1},{9,13},{6,2},{10,14},{7,3},{11,15},{20,16},{24,... | collective-permute-start | bytes 1622024 | tf_op jit(solution)/shard_map/ppermute | solution.py:170
  38.1 13.4 %collective-permute-start.8 = (bf16[512,512]{1,0:T(8,128)(2,1)S(1)}, bf16[512,512]{1,0:T(8,128)(2,1)S(1)}, u32[]{:S(2)}, u32[]{:S(2)}) collective-permute-start(bf16[512,512]{1,0:T(8,128)(2,1)S(1)} %slice_select_fusion.1), channel_id=1, source_target_pairs={{0,16},{16,0},{1,17},{17,1},{2,18},{18,2},{3,19},{19,3},{4,20},{20... | collective-permute-start | bytes 1572872 | tf_op jit(solution)/shard_map/ppermute | solution.py:172
  39.7 11.8 %collective-permute-start.1 = (bf16[256,2048]{1,0:T(8,128)(2,1)S(1)}, bf16[256,2048]{1,0:T(8,128)(2,1)S(1)}, u32[]{:S(2)}, u32[]{:S(2)}) collective-permute-start(bf16[256,2048]{1,0:T(8,128)(2,1)S(1)} %collective-permute-done.refs_1_), channel_id=1, source_target_pairs={{0,1},{1,0},{2,3},{3,2},{4,5},{5,4},{6,7},{7,6},{8,9},{9,8},{10,11... | collective-permute-start | bytes 3145736 | tf_op jit(solution)/shard_map/ppermute | solution.py:175
  49.8 1.6 %copy-start.1 = (bf16[256,2048]{1,0:T(8,128)(2,1)S(1)}, bf16[256,2048]{1,0:T(8,128)(2,1)}, u32[]{:S(2)}) copy-start(bf16[256,2048]{1,0:T(8,128)(2,1)} %get-tuple-element.17.refs_0_) | copy-start | bytes 3145732
  49.8 1.8 %copy-start.3 = (bf16[1024,512]{1,0:T(8,128)(2,1)S(1)}, bf16[1024,512]{1,0:T(8,128)(2,1)}, u32[]{:S(2)}) copy-start(bf16[1024,512]{1,0:T(8,128)(2,1)} %refs_5_.1) | copy-start | bytes 3145732
  49.8 1.8 %copy-start.13 = (s32[8]{0:T(128)S(1)}, s32[8]{0:T(128)}, u32[]{:S(2)}) copy-start(s32[8]{0:T(128)} %stack.48.place_ref) | copy-start | bytes 100
  49.8 11.4 %collective-permute-start.10 = (bf16[512,512]{1,0:T(8,128)(2,1)S(1)}, bf16[512,512]{1,0:T(8,128)(2,1)S(1)}, u32[]{:S(2)}, u32[]{:S(2)}) collective-permute-start(bf16[512,512]{1,0:T(8,128)(2,1)S(1)} %slice_select_fusion), channel_id=1, source_target_pairs={{0,16},{16,0},{1,17},{17,1},{2,18},{18,2},{3,19},{19,3},{4,20},{20... | collective-permute-start | bytes 1572872 | tf_op jit(solution)/shard_map/ppermute | solution.py:174
  51.7 2.5 %copy-start.5 = (bf16[528,512]{1,0:T(8,128)(2,1)S(1)}, bf16[528,512]{1,0:T(8,128)(2,1)}, u32[]{:S(2)}) copy-start(bf16[528,512]{1,0:T(8,128)(2,1)} %copy-done.4) | copy-start | bytes 1622020
  51.7 2.5 %copy-start.7 = (bf16[528,512]{1,0:T(8,128)(2,1)S(1)}, bf16[528,512]{1,0:T(8,128)(2,1)}, u32[]{:S(2)}) copy-start(bf16[528,512]{1,0:T(8,128)(2,1)} %copy-done.6) | copy-start | bytes 1622020
  56.4 5.2 %copy-start.10 = (bf16[2,256,512]{2,1,0:T(8,128)(2,1)}, bf16[2,256,512]{2,1,0:T(8,128)(2,1)S(1)}, u32[]{:S(2)}) copy-start(bf16[2,256,512]{2,1,0:T(8,128)(2,1)S(1)} %get-tuple-element.26.left_ref) | copy-start | bytes 1572868
  56.4 7.2 %collective-permute-start.9 = (bf16[4,16,128]{2,1,0:T(8,128)(2,1)S(1)}, bf16[4,16,128]{2,1,0:T(8,128)(2,1)S(1)}, u32[]{:S(2)}, u32[]{:S(2)}) collective-permute-start(bf16[4,16,128]{2,1,0:T(8,128)(2,1)S(1)} %get-tuple-element.25), channel_id=1, source_target_pairs={{0,2},{2,0},{1,3},{3,1},{4,6},{6,4},{5,7},{7,5},{8,10},{10,8},{9,1... | collective-permute-start | bytes 49160 | tf_op jit(solution)/shard_map/ppermute | solution.py:224
  62.0 7.8 %collective-permute-start.11 = (bf16[256,768]{1,0:T(8,128)(2,1)S(1)}, bf16[256,768]{1,0:T(8,128)(2,1)S(1)}, u32[]{:S(2)}, u32[]{:S(2)}) collective-permute-start(bf16[256,768]{1,0:T(8,128)(2,1)S(1)} %shard_map.91), channel_id=1, source_target_pairs={{0,2},{2,0},{1,3},{3,1},{4,6},{6,4},{5,7},{7,5},{8,10},{10,8},{9,1... | collective-permute-start | bytes 1179656 | tf_op jit(solution)/shard_map/ppermute | solution.py:222
  65.7 4.1 %copy-start.12 = (bf16[2,128,512]{2,1,0:T(8,128)(2,1)S(1)}, bf16[2,128,512]{2,1,0:T(8,128)(2,1)}, u32[]{:S(2)}) copy-start(bf16[2,128,512]{2,1,0:T(8,128)(2,1)} %pre_ref.1) | copy-start | bytes 786436
  (4 other events, 4.5 us)

commit v6 on v5

--- a/solution.py
+++ b/solution.py
@@ -200,7 +200,7 @@
         in_specs=[anywhere],
         out_specs=vmem,
         out_shape=jax.ShapeDtypeStruct((8, HD), jnp.float32),
-        cost_estimate=pl.CostEstimate(flops=8 * 10**9, bytes_accessed=4096, transcendentals=0),
+        cost_estimate=pl.CostEstimate(flops=11 * 10**9, bytes_accessed=4096, transcendentals=0),
         compiler_params=ROOM,
     )(y_third)
     keep = ((rows, columns), jnp.float32)
@@ -229,42 +229,61 @@
     return parts, asked
 
 
-def attend_kernel(q_ref, bias_ref, pre_ref, *refs):
+CONTRACT = (((1,), (1,)), ((), ()))
+
+
+def scored(q, key, bias):
+    return lax.dot_general(q, key, CONTRACT, preferred_element_type=jnp.float32) * (1.0 / HD**0.5) + bias
+
+
+def row_sum(e):
+    return jnp.sum(e, axis=1, keepdims=True)
+
+
+def prefix_kernel(q_ref, bias_ref, pre_ref, mixed_ref, stat_ref):
+    heads, rows = q_ref.shape[0], q_ref.shape[1]
+    docs, pref_rows = pre_ref.shape[0], pre_ref.shape[1]
+    lane = lax.broadcasted_iota(jnp.int32, (rows, HD), 1)
+    stat = jnp.zeros((rows, HD), jnp.float32)
+    for g in range(heads):
+        key = slice(2 * g * HD, (2 * g + 1) * HD)
+        val = slice((2 * g + 1) * HD, (2 * g + 2) * HD)
+        scores = [
+            scored(q_ref[g], pre_ref[d, :, key], bias_ref[:, d * pref_rows : (d + 1) * pref_rows])
+            for d in range(docs)
+        ]
+        peak = functools.reduce(jnp.maximum, [jnp.max(s, axis=1, keepdims=True) for s in scores])
+        terms = [jnp.exp(s - peak) for s in scores]
+        total = functools.reduce(jnp.add, [row_sum(e) for e in terms])
+        mixed_ref[g] = functools.reduce(
+            jnp.add, [dot32(e.astype(jnp.bfloat16), pre_ref[d, :, val]) for d, e in enumerate(terms)]
+        )
+        stat = jnp.where(lane == 2 * g, peak, jnp.where(lane == 2 * g + 1, total, stat))
+    stat_ref[...] = stat
+
+
+def attend_kernel(q_ref, bias_ref, mixed_ref, stat_ref, *refs):
     keep_ref, *got_refs, new_ref, out_ref = refs
-    for g in range(q_ref.shape[0]):
+    heads, rows = q_ref.shape[0], q_ref.shape[1]
+    n_quest = rows // GROUP
+    start = bias_ref.shape[1] - new_ref.shape[0]
+    lane = lax.broadcasted_iota(jnp.int32, (rows, HD), 1)
+    stat = jnp.zeros((rows, HD), jnp.float32)
+    for g in range(heads):
         cut = [slice((2 * g + i) * HD, (2 * g + i + 1) * HD) for i in range(2)]
         sums = [keep_ref[:, at] for at in cut]
         for got in got_refs:
             sums = [s + more for s, more in zip(sums, unpack(got, g))]
-        for at, s in zip(cut, sums):
-            new_ref[:, at] = s.astype(jnp.bfloat16)
-    heads = q_ref.shape[0]
-    rows = q_ref.shape[1]
-    docs, pref_rows = pre_ref.shape[0], pre_ref.shape[1]
-    lane = lax.broadcasted_iota(jnp.int32, (rows, HD), 1)
-    contract = (((1,), (1,)), ((), ()))
-    stat = jnp.zeros((rows, HD), jnp.float32)
-    for g in range(heads):
-        key = slice(2 * g * HD, (2 * g + 1) * HD)
-        val = slice((2 * g + 1) * HD, (2 * g + 2) * HD)
-        q = q_ref[g]
-        parts = [(pre_ref[d, :, key], pre_ref[d, :, val]) for d in range(docs)]
-        parts.append((new_ref[:, key], new_ref[:, val]))
-        scores = []
-        at = 0
-        for k, _ in parts:
-            s = lax.dot_general(q, k, contract, preferred_element_type=jnp.float32)
-            s = s * (1.0 / HD**0.5) + bias_ref[:, at : at + k.shape[0]]
-            scores.append(s)
-            at += k.shape[0]
-        peak = functools.reduce(jnp.maximum, [jnp.max(s, axis=1, keepdims=True) for s in scores])
-        total = jnp.zeros((rows, 1), jnp.float32)
-        mixed = jnp.zeros((rows, HD), jnp.float32)
-        for s, (_, v) in zip(scores, parts):
-            e = jnp.exp(s - peak)
-            total = total + jnp.sum(e, axis=1, keepdims=True)
-            mixed = mixed + jnp.dot(e.astype(jnp.bfloat16), v, preferred_element_type=jnp.float32)
-        n_quest = rows // GROUP
+        key, value = (s.astype(jnp.bfloat16) for s in sums)
+        new_ref[:, cut[0]] = key
+        new_ref[:, cut[1]] = value
+        score = scored(q_ref[g], key, bias_ref[:, start:])
+        before = stat_ref[:, 2 * g : 2 * g + 1]
+        peak = jnp.maximum(before, jnp.max(score, axis=1, keepdims=True))
+        scale = jnp.exp(before - peak)
+        e = jnp.exp(score - peak)
+        total = scale * stat_ref[:, 2 * g + 1 : 2 * g + 2] + row_sum(e)
+        mixed = scale * mixed_ref[g] + dot32(e.astype(jnp.bfloat16), value)
         out_ref[:, g] = mixed.reshape(n_quest, GROUP, HD)
         stat = jnp.where(lane == 2 * g, peak, jnp.where(lane == 2 * g + 1, total, stat))
     out_ref[:, heads] = stat.reshape(n_quest, GROUP, HD)
@@ -317,6 +336,14 @@
     bias = jnp.where(visible, 0.0, -jnp.inf).astype(jnp.float32)
     bias = jnp.repeat(bias, GROUP, axis=0)
 
+    prefix_part = pl.pallas_call(
+        prefix_kernel,
+        out_shape=(
+            jax.ShapeDtypeStruct((heads, n_quest * GROUP, HD), jnp.float32),
+            jax.ShapeDtypeStruct((n_quest * GROUP, HD), jnp.float32),
+        ),
+        compiler_params=ROOM,
+    )(asked, bias, prefix)
     new_cache, part = pl.pallas_call(
         attend_kernel,
         out_shape=(
@@ -324,7 +351,7 @@
             jax.ShapeDtypeStruct((n_quest, heads + 1, GROUP, HD), jnp.float32),
         ),
         compiler_params=ROOM,
-    )(asked, bias, prefix, *parts)
+    )(asked, bias, *prefix_part, *parts)
     part = lax.all_to_all(part, ("z", "x"), 0, 0, tiled=True)
     attended = pl.pallas_call(
         functools.partial(finish_kernel, 2 * nz),

time: 84.9 us -> 84.9 us (level)
  no operation moved by 1% of the time
where the time goes in v6:
time: 84.9 us; the launch traced here: 84.3 us
  waiting for transfers between devices  34.2 us (40%)
  starting transfers between devices  16.5 us (19%)
  Pallas kernels  12.4 us (15%)
  blocking collectives  12.4 us (15%)
  local copies, waits for them, and re-layouts  5.61 us (7%)
  other arithmetic  2.17 us (3%)
  between operations  1 us (1%)
    all_to_all x1, blocking collectives, shards(): part = lax.all_to_all(part, ('z', 'x'), 0, 0, tiled=True)  12.4 us
    ppermute x1, waiting for transfers between devices, project(): out = lax.ppermute(across, 'z', outward)  12.1 us
    ppermute x1, waiting for transfers between devices, project(): out_next = lax.ppermute(across_next, 'z', outward)  9.97 us
    ppermute x1, waiting for transfers between devices, project(): near = lax.ppermute(own, 'z', [(0, 1), (1, 0), (2, 3), (3, 2)])  4.97 us
    pallas_call x1, Pallas kernels, project(): pl.pallas_call(carve_kernel, in_specs=[smem, hbm], out_specs=[vmem] * 3,...  4.41 us
    ppermute x1, waiting for transfers between devices, project(): parts = [keep_here, lax.ppermute(send_x, 'x', SWAP)]  3.9 us
    ppermute x1, waiting for transfers between devices, project(): lax.ppermute(jnp.where(edge, out_next[:half], across_next[:half]), 'y', S...  3.28 us
    ppermute x1, starting transfers between devices, project(): near = lax.ppermute(own, 'z', [(0, 1), (1, 0), (2, 3), (3, 2)])  3.09 us
  transfers between devices with their start and end apart: 12, of which 5 were waited for; matrix products, arithmetic and copies ran while one was open for 5% of the time, Pallas kernels for 12%

profile of v6, /device:TPU:0, one launch (start us, length us, event | category | flops | bytes accessed | tf_op | source)
XLA Modules:
  0.0 84.3 jit_solution(3912602394244676121)
XLA Ops:
  1.4 1.1 %constant_dynamic-slice_fusion = bf16[512,512]{1,0:T(8,128)(2,1)S(1)} fusion(bf16[1024,512]{1,0:T(8,128)(2,1)} %refs_5_.1, s32[]{:T(128)S(6)} %select_n.52), kind=kLoop, calls=%fused_computation.22 | loop fusion | bytes 1048580 | tf_op jit(solution)/shard_map/dynamic_slice | solution.py:145
  2.5 3.1 %collective-permute-start.2 = (bf16[528,512]{1,0:T(8,128)(2,1)S(1)}, bf16[528,512]{1,0:T(8,128)(2,1)S(1)}, u32[]{:S(2)}, u32[]{:S(2)}) collective-permute-start(bf16[528,512]{1,0:T(8,128)(2,1)S(1)} %fusion.1.refs_4_.refs_5_), channel_id=1, source_target_pairs={{0,4},{4,0},{8,12},{12,8},{1,5},{5,1},{9,13},{13,9},{2,6},{6,2},{1... | collective-permute-start | bytes 1622024 | tf_op jit(solution)/shard_map/ppermute | solution.py:161
  6.9 4.4 %shard_map.86 = (bf16[256,2048]{1,0:T(8,128)(2,1)}, bf16[256,2048]{1,0:T(8,128)(2,1)}, bf16[256,2048]{1,0:T(8,128)(2,1)}) custom-call(s32[8]{0:T(128)} %stack.48.place_ref, bf16[256,8192]{1,0:T(8,128)(2,1)} %tokens), custom_call_target="tpu_custom_call" | custom-call | tf_op jit(solution)/shard_map/pallas_call | solution.py:152
  11.4 1.6 %collective-permute-start = (bf16[256,2048]{1,0:T(8,128)(2,1)}, bf16[256,2048]{1,0:T(8,128)(2,1)S(1)}, u32[]{:S(2)}, u32[]{:S(2)}) collective-permute-start(bf16[256,2048]{1,0:T(8,128)(2,1)} %get-tuple-element.20), channel_id=1, source_target_pairs={{0,2},{2,0},{1,3},{3,1},{4,6},{6,4},{5,7},{7,5},{8,10},{10,8},{9,1... | collective-permute-start | bytes 3145736 | tf_op jit(solution)/shard_map/ppermute | solution.py:163
  12.9 5.0 %collective-permute-done.2.refs_6_ = bf16[528,512]{1,0:T(8,128)(2,1)S(1)} collective-permute-done((bf16[528,512]{1,0:T(8,128)(2,1)S(1)}, bf16[528,512]{1,0:T(8,128)(2,1)S(1)}, u32[]{:S(2)}, u32[]{:S(2)}) %collective-permute-start.2) | collective-permute-done | bytes 540704 | tf_op jit(solution)/shard_map/ppermute | solution.py:161
  18.6 1.3 %collective-permute-start.5 = (bf16[528,512]{1,0:T(8,128)(2,1)S(1)}, bf16[528,512]{1,0:T(8,128)(2,1)}, u32[]{:S(2)}, u32[]{:S(2)}) collective-permute-start(bf16[528,512]{1,0:T(8,128)(2,1)S(1)} %collective-permute-done.4.refs_7_), channel_id=1, source_target_pairs={{4,0},{8,12},{5,1},{9,13},{6,2},{10,14},{7,3},{11,15},{20,16},{24,... | collective-permute-start | bytes 1622024 | tf_op jit(solution)/shard_map/ppermute | solution.py:166
  20.0 0.8 slice.23
  20.8 1.7 %collective-permute-start.6 = (bf16[512,512]{1,0:T(8,128)(2,1)}, bf16[512,512]{1,0:T(8,128)(2,1)}, u32[]{:S(2)}, u32[]{:S(2)}) collective-permute-start(bf16[512,512]{1,0:T(8,128)(2,1)} %slice.23), channel_id=1, source_target_pairs={{0,16},{16,0},{1,17},{17,1},{2,18},{18,2},{3,19},{19,3},{4,20},{20... | collective-permute-start | bytes 1572872 | tf_op jit(solution)/shard_map/ppermute | solution.py:167
  22.5 0.8 gather_fusion
  23.6 12.1 %collective-permute-done.5.refs_8_ = bf16[528,512]{1,0:T(8,128)(2,1)} collective-permute-done((bf16[528,512]{1,0:T(8,128)(2,1)S(1)}, bf16[528,512]{1,0:T(8,128)(2,1)}, u32[]{:S(2)}, u32[]{:S(2)}) %collective-permute-start.5) | collective-permute-done | bytes 540704 | tf_op jit(solution)/shard_map/ppermute | solution.py:166
  35.6 1.3 %collective-permute-start.7 = (bf16[528,512]{1,0:T(8,128)(2,1)S(1)}, bf16[528,512]{1,0:T(8,128)(2,1)S(1)}, u32[]{:S(2)}, u32[]{:S(2)}) collective-permute-start(bf16[528,512]{1,0:T(8,128)(2,1)S(1)} %collective-permute-done.3.refs_9_), channel_id=1, source_target_pairs={{4,0},{8,12},{5,1},{9,13},{6,2},{10,14},{7,3},{11,15},{20,16},{24,... | collective-permute-start | bytes 1622024 | tf_op jit(solution)/shard_map/ppermute | solution.py:170
  36.9 1.1 %slice_select_fusion.1 = bf16[512,512]{1,0:T(8,128)(2,1)S(1)} fusion(bf16[528,512]{1,0:T(8,128)(2,1)S(1)} %collective-permute-done.4.refs_7_, bf16[528,512]{1,0:T(8,128)(2,1)} %collective-permute-done.5.refs_8_, pred[]{:T(512)S(6)} %or.6), kind=kLoop, calls=%fused_computation.5 | loop fusion | flops 262144 | bytes 1572865 | tf_op jit(solution)/shard_map/jit(_where)/select_n | solution.py:171
  38.1 1.6 %collective-permute-start.8 = (bf16[512,512]{1,0:T(8,128)(2,1)S(1)}, bf16[512,512]{1,0:T(8,128)(2,1)S(1)}, u32[]{:S(2)}, u32[]{:S(2)}) collective-permute-start(bf16[512,512]{1,0:T(8,128)(2,1)S(1)} %slice_select_fusion.1), channel_id=1, source_target_pairs={{0,16},{16,0},{1,17},{17,1},{2,18},{18,2},{3,19},{19,3},{4,20},{20... | collective-permute-start | bytes 1572872 | tf_op jit(solution)/shard_map/ppermute | solution.py:172
  39.8 10.0 %collective-permute-done.7.refs_10_ = bf16[528,512]{1,0:T(8,128)(2,1)S(1)} collective-permute-done((bf16[528,512]{1,0:T(8,128)(2,1)S(1)}, bf16[528,512]{1,0:T(8,128)(2,1)S(1)}, u32[]{:S(2)}, u32[]{:S(2)}) %collective-permute-start.7) | collective-permute-done | bytes 540704 | tf_op jit(solution)/shard_map/ppermute | solution.py:170
  49.8 1.6 %collective-permute-start.10 = (bf16[512,512]{1,0:T(8,128)(2,1)S(1)}, bf16[512,512]{1,0:T(8,128)(2,1)S(1)}, u32[]{:S(2)}, u32[]{:S(2)}) collective-permute-start(bf16[512,512]{1,0:T(8,128)(2,1)S(1)} %slice_select_fusion), channel_id=1, source_target_pairs={{0,16},{16,0},{1,17},{17,1},{2,18},{18,2},{3,19},{19,3},{4,20},{20... | collective-permute-start | bytes 1572872 | tf_op jit(solution)/shard_map/ppermute | solution.py:174
  51.7 2.5 %shard_map.87.refs_4_ = f32[2,256,512]{2,1,0:T(8,128)S(1)} custom-call(s32[8]{0:T(128)S(1)} %copy-done.13, bf16[256,2048]{1,0:T(8,128)(2,1)S(1)} %copy-done.1, bf16[256,2048]{1,0:T(8,128)(2,1)S(1)} %collective-permute-done.refs_1_, bf16[256,2048]{1,0:T(8,128)(2,1)S(1)} %copy-done.2, bf16[256,2048]{1,0:T(8,128)(2,1)S(1)} %collective-permute-done.1.refs_3_, ...), custom_call_target="tpu_custom_call" | custom-call | tf_op jit(solution)/shard_map/pallas_call | solution.py:179
  54.2 2.1 %shard_map.88 = (f32[2,256,512]{2,1,0:T(8,128)S(1)}, bf16[4,16,128]{2,1,0:T(8,128)(2,1)S(1)}, bf16[2,256,512]{2,1,0:T(8,128)(2,1)S(1)}) custom-call(s32[8]{0:T(128)S(1)} %copy-done.13, bf16[256,2048]{1,0:T(8,128)(2,1)S(1)} %copy-done.1, bf16[256,2048]{1,0:T(8,128)(2,1)S(1)} %collective-permute-done.refs_1_, bf16[256,2048]{1,0:T(8,128)(2,1)S(1)} %copy-done.2, ...), custom_call_target="tpu_custom_call" | custom-call | tf_op jit(solution)/shard_map/pallas_call | solution.py:187
  56.4 1.6 %collective-permute-start.9 = (bf16[4,16,128]{2,1,0:T(8,128)(2,1)S(1)}, bf16[4,16,128]{2,1,0:T(8,128)(2,1)S(1)}, u32[]{:S(2)}, u32[]{:S(2)}) collective-permute-start(bf16[4,16,128]{2,1,0:T(8,128)(2,1)S(1)} %get-tuple-element.27), channel_id=1, source_target_pairs={{0,2},{2,0},{1,3},{3,1},{4,6},{6,4},{5,7},{7,5},{8,10},{10,8},{9,1... | collective-permute-start | bytes 49160 | tf_op jit(solution)/shard_map/ppermute | solution.py:224
  58.0 3.3 %collective-permute-done.10.block_ref = bf16[512,512]{1,0:T(8,128)(2,1)S(1)} collective-permute-done((bf16[512,512]{1,0:T(8,128)(2,1)S(1)}, bf16[512,512]{1,0:T(8,128)(2,1)S(1)}, u32[]{:S(2)}, u32[]{:S(2)}) %collective-permute-start.10) | collective-permute-done | bytes 524320 | tf_op jit(solution)/shard_map/ppermute | solution.py:174
  62.0 1.5 %collective-permute-start.11 = (bf16[256,768]{1,0:T(8,128)(2,1)S(1)}, bf16[256,768]{1,0:T(8,128)(2,1)S(1)}, u32[]{:S(2)}, u32[]{:S(2)}) collective-permute-start(bf16[256,768]{1,0:T(8,128)(2,1)S(1)} %shard_map.92), channel_id=1, source_target_pairs={{0,2},{2,0},{1,3},{3,1},{4,6},{6,4},{5,7},{7,5},{8,10},{10,8},{9,1... | collective-permute-start | bytes 1179656 | tf_op jit(solution)/shard_map/ppermute | solution.py:222
  64.6 1.0 %copy-done.11 = bf16[2,256,512]{2,1,0:T(8,128)(2,1)S(1)} copy-done((bf16[2,256,512]{2,1,0:T(8,128)(2,1)S(1)}, bf16[2,256,512]{2,1,0:T(8,128)(2,1)}, u32[]{:S(2)}) %copy-start.11) | copy-done | bytes 524312
  65.9 3.9 %collective-permute-done.11.refs_1_ = bf16[256,768]{1,0:T(8,128)(2,1)S(1)} collective-permute-done((bf16[256,768]{1,0:T(8,128)(2,1)S(1)}, bf16[256,768]{1,0:T(8,128)(2,1)S(1)}, u32[]{:S(2)}, u32[]{:S(2)}) %collective-permute-start.11) | collective-permute-done | bytes 393248 | tf_op jit(solution)/shard_map/ppermute | solution.py:222
  69.8 1.3 %shard_map.93 = (bf16[256,512]{1,0:T(8,128)(2,1)}, f32[8,3,8,128]{3,2,1,0:T(8,128)S(1)}) custom-call(bf16[2,64,128]{2,1,0:T(8,128)(2,1)S(1)} %bitcast.18, f32[64,512]{1,0:T(8,128)S(1)} %broadcast_bitcast_fusion.bias_ref, f32[2,64,128]{2,1,0:T(8,128)S(1)} %get-tuple-element.28.mixed_ref, f32[64,128]{1,0:T(8,128)S(1)} %get-tuple-element.29.stat_ref, ...), custom_call_target="tpu_custom_call" | custom-call | tf_op jit(solution)/shard_map/pallas_call | solution.py:347
  71.1 12.4 %all_to_all.5.part_ref = f32[8,3,8,128]{3,2,1,0:T(8,128)S(1)} all-to-all(f32[8,3,8,128]{3,2,1,0:T(8,128)S(1)} %get-tuple-element.33), channel_id=1, replica_groups=mesh['y'=2,'z'=4,'x'=2,'c'=2] {'z','x'}, dimensions={0} | all-to-all | bytes 196608 | tf_op jit(solution)/shard_map/all_to_all | solution.py:355
  (65 shorter events, 6.3 us)
Async XLA Ops:
  0.6 21.9 %copy-start = (s32[4]{0:T(128)S(1)}, s32[4]{0:T(128)}, u32[]{:S(2)}) copy-start(s32[4]{0:T(128)} %param.13) | copy-start | bytes 52
  2.5 15.4 %collective-permute-start.2 = (bf16[528,512]{1,0:T(8,128)(2,1)S(1)}, bf16[528,512]{1,0:T(8,128)(2,1)S(1)}, u32[]{:S(2)}, u32[]{:S(2)}) collective-permute-start(bf16[528,512]{1,0:T(8,128)(2,1)S(1)} %fusion.1.refs_4_.refs_5_), channel_id=1, source_target_pairs={{0,4},{4,0},{8,12},{12,8},{1,5},{5,1},{9,13},{13,9},{2,6},{6,2},{1... | collective-permute-start | bytes 1622024 | tf_op jit(solution)/shard_map/ppermute | solution.py:161
  5.6 13.0 %collective-permute-start.4 = (bf16[528,512]{1,0:T(8,128)(2,1)S(1)}, bf16[528,512]{1,0:T(8,128)(2,1)S(1)}, u32[]{:S(2)}, u32[]{:S(2)}) collective-permute-start(bf16[528,512]{1,0:T(8,128)(2,1)S(1)} %fusion.1.refs_4_.refs_5_), channel_id=1, source_target_pairs={{4,8},{8,4},{5,9},{9,5},{6,10},{10,6},{7,11},{11,7},{20,24},{24,20... | collective-permute-start | bytes 1622024 | tf_op jit(solution)/shard_map/ppermute | solution.py:162
  6.9 13.0 %copy-start.14 = (s32[8,8]{1,0:T(8,128)S(1)}, s32[8,8]{1,0:T(8,128)}, u32[]{:S(2)}) copy-start(s32[8,8]{1,0:T(8,128)} %param.12) | copy-start | bytes 772
  11.4 28.4 %collective-permute-start = (bf16[256,2048]{1,0:T(8,128)(2,1)}, bf16[256,2048]{1,0:T(8,128)(2,1)S(1)}, u32[]{:S(2)}, u32[]{:S(2)}) collective-permute-start(bf16[256,2048]{1,0:T(8,128)(2,1)} %get-tuple-element.20), channel_id=1, source_target_pairs={{0,2},{2,0},{1,3},{3,1},{4,6},{6,4},{5,7},{7,5},{8,10},{10,8},{9,1... | collective-permute-start | bytes 3145736 | tf_op jit(solution)/shard_map/ppermute | solution.py:163
  17.9 5.7 %collective-permute-start.3 = (bf16[528,512]{1,0:T(8,128)(2,1)S(1)}, bf16[528,512]{1,0:T(8,128)(2,1)S(1)}, u32[]{:S(2)}, u32[]{:S(2)}) collective-permute-start(bf16[528,512]{1,0:T(8,128)(2,1)S(1)} %collective-permute-done.2.refs_6_), channel_id=1, source_target_pairs={{4,8},{8,4},{5,9},{9,5},{6,10},{10,6},{7,11},{11,7},{20,24},{24,20... | collective-permute-start | bytes 1622024 | tf_op jit(solution)/shard_map/ppermute | solution.py:165
  18.6 18.3 %copy-start.4 = (bf16[528,512]{1,0:T(8,128)(2,1)}, bf16[528,512]{1,0:T(8,128)(2,1)S(1)}, u32[]{:S(2)}) copy-start(bf16[528,512]{1,0:T(8,128)(2,1)S(1)} %collective-permute-done.4.refs_7_) | copy-start | bytes 1622020
  18.6 17.0 %collective-permute-start.5 = (bf16[528,512]{1,0:T(8,128)(2,1)S(1)}, bf16[528,512]{1,0:T(8,128)(2,1)}, u32[]{:S(2)}, u32[]{:S(2)}) collective-permute-start(bf16[528,512]{1,0:T(8,128)(2,1)S(1)} %collective-permute-done.4.refs_7_), channel_id=1, source_target_pairs={{4,0},{8,12},{5,1},{9,13},{6,2},{10,14},{7,3},{11,15},{20,16},{24,... | collective-permute-start | bytes 1622024 | tf_op jit(solution)/shard_map/ppermute | solution.py:166
  20.8 17.2 %collective-permute-start.6 = (bf16[512,512]{1,0:T(8,128)(2,1)}, bf16[512,512]{1,0:T(8,128)(2,1)}, u32[]{:S(2)}, u32[]{:S(2)}) collective-permute-start(bf16[512,512]{1,0:T(8,128)(2,1)} %slice.23), channel_id=1, source_target_pairs={{0,16},{16,0},{1,17},{17,1},{2,18},{18,2},{3,19},{19,3},{4,20},{20... | collective-permute-start | bytes 1572872 | tf_op jit(solution)/shard_map/ppermute | solution.py:167
  23.3 16.4 %copy-start.15 = (s32[8]{0:T(128)S(1)}, s32[8]{0:T(128)}, u32[]{:S(2)}) copy-start(s32[8]{0:T(128)} %param.11) | copy-start | bytes 100
  23.6 26.2 %copy-start.6 = (bf16[528,512]{1,0:T(8,128)(2,1)}, bf16[528,512]{1,0:T(8,128)(2,1)S(1)}, u32[]{:S(2)}) copy-start(bf16[528,512]{1,0:T(8,128)(2,1)S(1)} %collective-permute-done.3.refs_9_) | copy-start | bytes 1622020
  35.6 14.1 %collective-permute-start.7 = (bf16[528,512]{1,0:T(8,128)(2,1)S(1)}, bf16[528,512]{1,0:T(8,128)(2,1)S(1)}, u32[]{:S(2)}, u32[]{:S(2)}) collective-permute-start(bf16[528,512]{1,0:T(8,128)(2,1)S(1)} %collective-permute-done.3.refs_9_), channel_id=1, source_target_pairs={{4,0},{8,12},{5,1},{9,13},{6,2},{10,14},{7,3},{11,15},{20,16},{24,... | collective-permute-start | bytes 1622024 | tf_op jit(solution)/shard_map/ppermute | solution.py:170
  38.1 13.4 %collective-permute-start.8 = (bf16[512,512]{1,0:T(8,128)(2,1)S(1)}, bf16[512,512]{1,0:T(8,128)(2,1)S(1)}, u32[]{:S(2)}, u32[]{:S(2)}) collective-permute-start(bf16[512,512]{1,0:T(8,128)(2,1)S(1)} %slice_select_fusion.1), channel_id=1, source_target_pairs={{0,16},{16,0},{1,17},{17,1},{2,18},{18,2},{3,19},{19,3},{4,20},{20... | collective-permute-start | bytes 1572872 | tf_op jit(solution)/shard_map/ppermute | solution.py:172
  39.7 11.7 %collective-permute-start.1 = (bf16[256,2048]{1,0:T(8,128)(2,1)S(1)}, bf16[256,2048]{1,0:T(8,128)(2,1)S(1)}, u32[]{:S(2)}, u32[]{:S(2)}) collective-permute-start(bf16[256,2048]{1,0:T(8,128)(2,1)S(1)} %collective-permute-done.refs_1_), channel_id=1, source_target_pairs={{0,1},{1,0},{2,3},{3,2},{4,5},{5,4},{6,7},{7,6},{8,9},{9,8},{10,11... | collective-permute-start | bytes 3145736 | tf_op jit(solution)/shard_map/ppermute | solution.py:175
  49.8 1.6 %copy-start.1 = (bf16[256,2048]{1,0:T(8,128)(2,1)S(1)}, bf16[256,2048]{1,0:T(8,128)(2,1)}, u32[]{:S(2)}) copy-start(bf16[256,2048]{1,0:T(8,128)(2,1)} %get-tuple-element.19.refs_0_) | copy-start | bytes 3145732
  49.8 1.8 %copy-start.3 = (bf16[1024,512]{1,0:T(8,128)(2,1)S(1)}, bf16[1024,512]{1,0:T(8,128)(2,1)}, u32[]{:S(2)}) copy-start(bf16[1024,512]{1,0:T(8,128)(2,1)} %refs_5_.1) | copy-start | bytes 3145732
  49.8 1.8 %copy-start.13 = (s32[8]{0:T(128)S(1)}, s32[8]{0:T(128)}, u32[]{:S(2)}) copy-start(s32[8]{0:T(128)} %stack.48.place_ref) | copy-start | bytes 100
  49.8 11.4 %collective-permute-start.10 = (bf16[512,512]{1,0:T(8,128)(2,1)S(1)}, bf16[512,512]{1,0:T(8,128)(2,1)S(1)}, u32[]{:S(2)}, u32[]{:S(2)}) collective-permute-start(bf16[512,512]{1,0:T(8,128)(2,1)S(1)} %slice_select_fusion), channel_id=1, source_target_pairs={{0,16},{16,0},{1,17},{17,1},{2,18},{18,2},{3,19},{19,3},{4,20},{20... | collective-permute-start | bytes 1572872 | tf_op jit(solution)/shard_map/ppermute | solution.py:174
  51.7 2.5 %copy-start.5 = (bf16[528,512]{1,0:T(8,128)(2,1)S(1)}, bf16[528,512]{1,0:T(8,128)(2,1)}, u32[]{:S(2)}) copy-start(bf16[528,512]{1,0:T(8,128)(2,1)} %copy-done.4) | copy-start | bytes 1622020
  51.7 2.5 %copy-start.7 = (bf16[528,512]{1,0:T(8,128)(2,1)S(1)}, bf16[528,512]{1,0:T(8,128)(2,1)}, u32[]{:S(2)}) copy-start(bf16[528,512]{1,0:T(8,128)(2,1)} %copy-done.6) | copy-start | bytes 1622020
  56.4 5.2 %copy-start.10 = (bf16[2,256,512]{2,1,0:T(8,128)(2,1)}, bf16[2,256,512]{2,1,0:T(8,128)(2,1)S(1)}, u32[]{:S(2)}) copy-start(bf16[2,256,512]{2,1,0:T(8,128)(2,1)S(1)} %get-tuple-element.30.left_ref) | copy-start | bytes 1572868
  56.4 7.2 %collective-permute-start.9 = (bf16[4,16,128]{2,1,0:T(8,128)(2,1)S(1)}, bf16[4,16,128]{2,1,0:T(8,128)(2,1)S(1)}, u32[]{:S(2)}, u32[]{:S(2)}) collective-permute-start(bf16[4,16,128]{2,1,0:T(8,128)(2,1)S(1)} %get-tuple-element.27), channel_id=1, source_target_pairs={{0,2},{2,0},{1,3},{3,1},{4,6},{6,4},{5,7},{7,5},{8,10},{10,8},{9,1... | collective-permute-start | bytes 49160 | tf_op jit(solution)/shard_map/ppermute | solution.py:224
  61.2 2.4 %copy-start.12 = (bf16[2,128,512]{2,1,0:T(8,128)(2,1)S(1)}, bf16[2,128,512]{2,1,0:T(8,128)(2,1)}, u32[]{:S(2)}) copy-start(bf16[2,128,512]{2,1,0:T(8,128)(2,1)} %pre_ref.1) | copy-start | bytes 786436
  62.0 7.8 %collective-permute-start.11 = (bf16[256,768]{1,0:T(8,128)(2,1)S(1)}, bf16[256,768]{1,0:T(8,128)(2,1)S(1)}, u32[]{:S(2)}, u32[]{:S(2)}) collective-permute-start(bf16[256,768]{1,0:T(8,128)(2,1)S(1)} %shard_map.92), channel_id=1, source_target_pairs={{0,2},{2,0},{1,3},{3,1},{4,6},{6,4},{5,7},{7,5},{8,10},{10,8},{9,1... | collective-permute-start | bytes 1179656 | tf_op jit(solution)/shard_map/ppermute | solution.py:222
  (4 other events, 4.5 us)
